TPU v7x, 256 devices: a whole 4x4x8 slice. The times are simulated.
256 devices in a mesh: row: 4 (over y), col: 8 (over z), feat: 8 (over x, core).
Axes of the slice: x: 4, y: 4, z: 8, core: 2. Of those that a mesh axis runs over, the one named last changes fastest.
Arguments:
- features: bfloat16 [16384, 128], P(('col', 'row'), 'feat'), may hold values from -6 to 6
- weight_in: bfloat16 [128, 256], P(None, 'feat'), may hold values from -0.5 to 0.5
- bias: float32 [256], P('feat'), may hold values from -3 to 3
- weight_out: bfloat16 [256, 172], P('feat'), may hold values from -50 to 50
- adj_tiles: bfloat16 [4, 8, 384, 128, 128], P('row', 'col'), may hold values from 0 to 0.039794922
- tile_rows: int32 [4, 8, 384], P('row', 'col'), may hold values from 0 to 31, as said below
- tile_cols: int32 [4, 8, 384], P('row', 'col'), may hold values from 0 to 15, as said below
- tile_live: int32 [4, 8], P('row', 'col'), may hold values from 48 to 384, as said below
- labels: int32 [16384], P(('row', 'col')), may hold values from 0 to 171
- label_mask: int32 [16384], P(('row', 'col')), may hold values from 0 to 1, as said below
Outputs:
- loss: float32 [], replicated
- grad_w1: float32 [128, 256], P(None, 'feat')
- grad_b1: float32 [256], P('feat')
- grad_w2: float32 [256, 172], P('feat')
Inputs may be any that keep to these rules, and one draw needn't show every extreme that they name: `tile_rows`: the slots of one row-column block name distinct tiles. `tile_cols`: the slots of one row-column block name distinct tiles. `tile_live`: some row-column block uses all 384 slots. `label_mask`: at least one node is labelled.
All inputs are finite; a program needn't handle non-finite values.
Results may differ from a plain program's by a relative error of at most 0.0075.
Values may be sent and summed in bfloat16 or wider, within the bound.
No kernel may reach another device: no remote copies, remote signals or barrier semaphores. Data moves between devices by JAX's collectives and lax.ppermute only.
A program may use at most 64 MiB of HBM per device.

v0:
```python
import jax
import jax.numpy as jnp
from jax import lax
from jax.sharding import PartitionSpec as P

CLASSES = 172
TILE = 128


def gelu_tanh(values):
    return jax.nn.gelu(values, approximate=True)


def local_sums(
    source_blocks, slot_tiles, pick_index, place_index, slot_weight, place_count, transpose
):
    picked = source_blocks[pick_index]
    if transpose:
        terms = jnp.einsum("tij,tih->tjh", slot_tiles, picked, preferred_element_type=jnp.float32)
    else:
        terms = jnp.einsum("tij,tjh->tih", slot_tiles, picked, preferred_element_type=jnp.float32)
    placing = (place_index[None, :] == jnp.arange(place_count, dtype=jnp.int32)[:, None]).astype(
        jnp.float32
    )
    placing = (placing * slot_weight[None, :]).astype(jnp.bfloat16)
    upper = terms.astype(jnp.bfloat16)
    lower = (terms - upper.astype(jnp.float32)).astype(jnp.bfloat16)
    summed = jnp.einsum("bt,tih->bih", placing, upper, preferred_element_type=jnp.float32)
    summed = summed + jnp.einsum("bt,tih->bih", placing, lower, preferred_element_type=jnp.float32)
    return summed.reshape(place_count * TILE, terms.shape[2])


def on_device(
    features,
    weight_in,
    bias,
    weight_out,
    adj_tiles,
    tile_rows,
    tile_cols,
    tile_live,
    labels,
    label_mask,
):
    node_rows = features.shape[0]
    row_blocks = node_rows * lax.axis_size("col") // TILE
    col_blocks = node_rows * lax.axis_size("row") // TILE
    slot_tiles = adj_tiles.reshape(adj_tiles.shape[2:])
    slot_rows = tile_rows.reshape(-1)
    slot_cols = tile_cols.reshape(-1)
    slot_weight = (jnp.arange(slot_rows.shape[0], dtype=jnp.int32) < tile_live.reshape(())).astype(
        jnp.float32
    )
    all_inputs = lax.all_gather(features, "feat", axis=1, tiled=True)
    projected = jnp.dot(all_inputs, weight_in, preferred_element_type=jnp.float32).astype(
        jnp.bfloat16
    )
    width = projected.shape[1]
    column_block = lax.all_gather(projected, "row", axis=0, tiled=True)
    partial_value = local_sums(
        column_block.reshape(col_blocks, TILE, width),
        slot_tiles,
        slot_cols,
        slot_rows,
        slot_weight,
        row_blocks,
        False,
    )
    gathered = lax.psum_scatter(partial_value, "col", scatter_dimension=0, tiled=True)
    row_labels, row_mask = (labels, label_mask)
    preact = gathered + bias
    hidden = gelu_tanh(preact).astype(jnp.bfloat16)
    logits = lax.psum(jnp.dot(hidden, weight_out, preferred_element_type=jnp.float32), "feat")
    count = lax.psum(jnp.sum(label_mask).astype(jnp.float32), ("row", "col"))
    weights = row_mask.astype(jnp.float32) / count
    shifted = logits - jnp.max(logits, axis=1, keepdims=True)
    expsum = jnp.sum(jnp.exp(shifted), axis=1, keepdims=True)
    onehot = (row_labels[:, None] == jnp.arange(CLASSES, dtype=jnp.int32)[None, :]).astype(
        jnp.float32
    )
    row_loss = (jnp.log(expsum[:, 0]) - jnp.sum(shifted * onehot, axis=1)) * weights
    grad_logits = ((jnp.exp(shifted) / expsum - onehot) * weights[:, None]).astype(jnp.bfloat16)
    grad_hidden = jnp.einsum(
        "nc,hc->nh", grad_logits, weight_out, preferred_element_type=jnp.float32
    )
    grad_preact = jax.vjp(gelu_tanh, preact)[1](grad_hidden)[0].astype(jnp.bfloat16)
    loss_part = jnp.sum(row_loss)
    bias_part = jnp.sum(grad_preact.astype(jnp.float32), axis=0)
    output_part = jnp.einsum("nh,nc->hc", hidden, grad_logits, preferred_element_type=jnp.float32)
    row_gradients = lax.all_gather(grad_preact, "col", axis=0, tiled=True)
    backward = local_sums(
        row_gradients.reshape(row_blocks, TILE, width),
        slot_tiles,
        slot_rows,
        slot_cols,
        slot_weight,
        col_blocks,
        True,
    )
    grad_proj = lax.psum_scatter(backward, "row", scatter_dimension=0, tiled=True).astype(
        jnp.bfloat16
    )
    input_part = jnp.einsum("nf,nh->fh", all_inputs, grad_proj, preferred_element_type=jnp.float32)
    loss, grad_b1, grad_w2, grad_w1 = lax.psum(
        (loss_part, bias_part, output_part, input_part), ("row", "col")
    )
    return (loss, grad_w1, grad_b1, grad_w2)


def solution(mesh):
    in_specs = (
        P(("col", "row"), "feat"),
        P(None, "feat"),
        P("feat"),
        P("feat", None),
        P("row", "col", None, None, None),
        P("row", "col", None),
        P("row", "col", None),
        P("row", "col"),
        P(("row", "col")),
        P(("row", "col")),
    )
    out_specs = (P(), P(None, "feat"), P("feat"), P("feat", None))
    return jax.shard_map(
        on_device, mesh=mesh, in_specs=in_specs, out_specs=out_specs, check_vma=False
    )
```

profile of v0, /device:TPU:32, one launch (start us, length us, event | category | flops | bytes accessed | tf_op | source)
XLA Modules:
  0.0 403.5 jit_solution(17958686558323592323)
XLA Ops:
  7.9 13.3 %all_gather.9 = bf16[512,128]{0,1:T(8,128)(2,1)S(1)} all-gather(bf16[512,16]{0,1:T(8,128)(2,1)} %param.10), channel_id=1, replica_groups=mesh['row'=4,'col'=8,'feat'=8] {'feat'}, dimensions={1}, use_global_device_ids=true | all-gather | bytes 147456 | tf_op jit(solution)/shard_map/all_gather | solution.py:54
  21.2 0.8 convolution_convert_fusion
  22.0 12.5 %all_gather.10 = bf16[2048,32]{0,1:T(8,128)(2,1)S(1)} all-gather(bf16[512,32]{0,1:T(8,128)(2,1)S(1)} %convolution_convert_fusion), channel_id=1, replica_groups=mesh['row'=4,'col'=8,'feat'=8] {'row'}, dimensions={0}, use_global_device_ids=true | all-gather | bytes 163840 | tf_op jit(solution)/shard_map/all_gather | solution.py:59
  35.3 2.4 gather_fusion
  37.7 11.3 %fusion.5 = (bf16[384,128,32]{1,2,0:T(8,128)(2,1)}, bf16[384,128,32]{1,2,0:T(8,128)(2,1)}) fusion(bf16[384,128,32]{1,2,0:T(8,128)(2,1)S(1)} %gather_fusion, bf16[1,1,384,128,128]{4,3,2,1,0:T(8,128)(2,1)} %param.14), kind=kOutput, calls=%fused_computation.11 | convolution fusion | flops 408944640 | bytes 22020096 | tf_op jit(solution)/shard_map/tij,tjh->tih/dot_general | solution.py:21
  49.0 3.1 fusion.10
  52.2 1.1 fusion.14
  53.3 1.1 copy.44
  55.8 73.8 %psum.43 = f32[]{:T(128)} all-reduce(f32[]{:T(128)S(6)} %convert_element_type.68), channel_id=1, replica_groups=mesh['row'=4,'col'=8,'feat'=8] {'row','col'}, use_global_device_ids=true, to_apply=%region_6.0 | all-reduce | flops 1 | bytes 8 | tf_op jit(solution)/shard_map/psum | solution.py:74
  130.2 1.8 fusion.54
  132.8 62.0 %all-reduce.3.cloned.1.call-done = f32[512,172]{0,1:T(8,128)} async-done(((f32[512,172]{0,1:T(8,128)}), f32[512,172]{0,1:T(8,128)}) %all-reduce.3.cloned.1.call-update) | async-done | bytes 352272 | tf_op jit(solution)/shard_map/psum | solution.py:73
  194.8 1.0 reduce_max.9
  195.8 1.1 exponential_reduce_fusion
  196.9 1.3 multiply_reduce_fusion
  198.1 1.1 multiply_convert_fusion
  199.3 1.7 convert_reduce_fusion
  200.9 25.3 %all_gather.11 = bf16[4096,32]{0,1:T(8,128)(2,1)S(1)} all-gather(bf16[512,32]{0,1:T(8,128)(2,1)S(1)} %get-tuple-element.11), channel_id=1, replica_groups=mesh['row'=4,'col'=8,'feat'=8] {'col'}, dimensions={0}, use_global_device_ids=true | all-gather | bytes 294912 | tf_op jit(solution)/shard_map/all_gather | solution.py:90
  226.3 2.6 gather_fusion.1
  228.9 6.4 %fusion.4 = (bf16[384,128,32]{1,2,0:T(8,128)(2,1)S(1)}, bf16[384,128,32]{1,2,0:T(8,128)(2,1)S(1)}) fusion(bf16[384,128,32]{1,2,0:T(8,128)(2,1)S(1)} %gather_fusion.1, bf16[1,1,384,128,128]{4,3,2,1,0:T(8,128)(2,1)} %param.14), kind=kOutput, calls=%fused_computation.8 | convolution fusion | flops 408944640 | bytes 22020096 | tf_op jit(solution)/shard_map/tij,tih->tjh/dot_general | solution.py:19
  235.4 0.9 fusion.6
  236.3 0.9 fusion.17
  238.3 21.5 %reduce-scatter.5.cloned.1.call-done = f32[512,32]{0,1:T(8,128)} async-done(((f32[2048,32]{0,1:T(8,128)}), f32[512,32]{0,1:T(8,128)}) %reduce-scatter.5.cloned.1.call-update) | async-done | bytes 65552 | tf_op jit(solution)/shard_map/reduce_scatter | solution.py:100
  259.8 1.0 convolution_bitcast_fusion
  260.8 136.2 %all-reduce = (f32[]{:T(128)}, f32[128,32]{0,1:T(8,128)}, f32[32]{0:T(128)}, f32[32,172]{1,0:T(8,128)}) all-reduce(f32[]{:T(128)} %get-tuple-element.14, f32[128,32]{0,1:T(8,128)S(1)} %convolution_bitcast_fusion, f32[32]{0:T(128)S(1)} %copy-done.12, f32[32,172]{1,0:T(8,128)S(1)} %fusion.53), channel_id=1, replica_groups=mesh['row'=4,'col'=8,'feat'=8] {'row','col'}, use_global_device_ids=true, to_apply=%region_8.0 | all-reduce | flops 9633 | bytes 77064 | tf_op jit(solution)/shard_map/psum | solution.py:104
  (49 shorter events, 3.9 us)
Async XLA Ops:
  7.2 123.1 %copy-start = (bf16[32,172]{1,0:T(8,128)(2,1)S(1)}, bf16[32,172]{1,0:T(8,128)(2,1)}, u32[]{:S(2)}) copy-start(bf16[32,172]{1,0:T(8,128)(2,1)} %param.13) | copy-start | bytes 33028
  7.2 123.0 %reduce-scatter.3.cloned.1.call-start = ((), (), s32[]{:S(2)}) async-start(), calls=%async_computation.2 | async-start | bytes 589824 | tf_op jit(solution)/shard_map/reduce_scatter | solution.py:69
  7.9 44.3 %copy-start.6 = (bf16[384]{0:T(512)(128)(2,1)}, bf16[384]{0:T(512)(128)(2,1)S(1)}, u32[]{:S(2)}) copy-start(bf16[384]{0:T(512)(128)(2,1)S(1)} %fusion.46) | copy-start | bytes 2308
  37.7 11.3 %copy-start.11 = (s32[1,1,384]{2,1,0:T(1,128)S(1)}, s32[1,1,384]{2,1,0:T(1,128)}, u32[]{:S(2)}) copy-start(s32[1,1,384]{2,1,0:T(1,128)} %param.15) | copy-start | bytes 4612
  49.0 3.2 copy-start.1
  52.1 2.4 copy-start.9
  52.2 77.5 %copy-start.10 = (s32[1,1,384]{2,1,0:T(1,128)S(1)}, s32[1,1,384]{2,1,0:T(1,128)}, u32[]{:S(2)}) copy-start(s32[1,1,384]{2,1,0:T(1,128)} %param.16) | copy-start | bytes 4612
  52.2 78.1 %copy-start.13 = (f32[32]{0:T(128)S(1)}, f32[32]{0:T(128)}, u32[]{:S(2)}) copy-start(f32[32]{0:T(128)} %param.12) | copy-start | bytes 388
  52.2 143.6 %copy-start.8 = (s32[512]{0:T(512)S(1)}, s32[512]{0:T(512)}, u32[]{:S(2)}) copy-start(s32[512]{0:T(512)} %param.18) | copy-start | bytes 6148
  54.5 140.3 %all-reduce.3.cloned.1.call-start = ((), (), s32[]{:S(2)}) async-start(), calls=%async_computation.3 | async-start | bytes 720896 | tf_op jit(solution)/shard_map/psum | solution.py:73
  132.1 127.7 %reduce-scatter.5.cloned.1.call-start = ((), (), s32[]{:S(2)}) async-start(), calls=%async_computation.4 | async-start | bytes 327680 | tf_op jit(solution)/shard_map/reduce_scatter | solution.py:100
  199.2 1.7 copy-start.2
  228.9 6.4 %copy-start.5 = (s32[384]{0:T(512)S(1)}, s32[384]{0:T(512)}, u32[]{:S(2)}) copy-start(s32[384]{0:T(512)} %reduce.2) | copy-start | bytes 4612
  228.9 6.4 %copy-start.7 = (bf16[384]{0:T(512)(128)(2,1)S(1)}, bf16[384]{0:T(512)(128)(2,1)}, u32[]{:S(2)}) copy-start(bf16[384]{0:T(512)(128)(2,1)} %copy-done.6) | copy-start | bytes 2308
  235.3 2.7 copy-start.3
  235.4 2.7 copy-start.4
  235.4 2.7 copy-start.14
  236.3 24.5 %copy-start.12 = (f32[32]{0:T(128)S(1)}, f32[32]{0:T(128)}, u32[]{:S(2)}) copy-start(f32[32]{0:T(128)} %get-tuple-element.10) | copy-start | bytes 388
Sparse Core Ops, SparseCore 0:
  54.6 38.0 reduce-scatter.2
  132.2 62.5 all-reduce.2
  238.2 21.5 reduce-scatter.4
where the time goes:
time: 410 us; the launch traced here: 404 us
  blocking collectives  261 us (64%)
  waiting for transfers between devices  83.6 us (20%)
  matrix products  29.3 us (7%)
  between operations  15.3 us (4%)
  local copies, waits for them, and re-layouts  7.05 us (2%)
  other arithmetic  7.04 us (2%)
    psum x1, blocking collectives, on_device(): lax.psum((loss_part, bias_part, output_part, input_part), ('row', 'col'))  136 us
    psum x1, blocking collectives, on_device(): count = lax.psum(jnp.sum(label_mask).astype(jnp.float32), ('row', 'col'))  73.8 us
    psum x1, waiting for transfers between devices, on_device(): lax.psum(jnp.dot(hidden, weight_out, preferred_element_type=jnp.float32),...  62 us
    all_gather x1, blocking collectives, on_device(): row_gradients = lax.all_gather(grad_preact, 'col', axis=0, tiled=True)  25.3 us
    reduce_scatter x1, waiting for transfers between devices, on_device(): lax.psum_scatter(backward, 'row', scatter_dimension=0, tiled=True)  21.5 us
    all_gather x1, blocking collectives, on_device(): all_inputs = lax.all_gather(features, 'feat', axis=1, tiled=True)  13.3 us
    all_gather x1, blocking collectives, on_device(): column_block = lax.all_gather(projected, 'row', axis=0, tiled=True)  12.5 us
    dot_general x1, matrix products, local_sums(): jnp.einsum('tij,tjh->tih', slot_tiles, picked, preferred_element_type=jnp...  11.3 us
  transfers between devices with their start and end apart: 3, of which 2 were waited for; matrix products, arithmetic and copies ran while one was open for 1% of the time, Pallas kernels for 0%

commit v1 on v0

v1 whole, which is shorter than its diff:
```python
import functools

import jax
import jax.numpy as jnp
from jax import lax
from jax.experimental import pallas as pl
from jax.experimental.pallas import tpu as pltpu
from jax.sharding import PartitionSpec as P

CLASSES = 172
TILE = 128
REST = CLASSES - TILE
SLOTS = 24
GELU_SCALE = 0.7978845608028654
GELU_CUBE = 0.044715
F32 = jnp.float32
BF16 = jnp.bfloat16


def dot(a, b, contract=((1,), (0,))):
    return lax.dot_general(a, b, (contract, ((), ())), preferred_element_type=F32)


def gelu_parts(v):
    squared = v * v
    t = jnp.tanh(GELU_SCALE * v * (1.0 + GELU_CUBE * squared))
    return squared, t


def aggregate_kernel(rows_ref, cols_ref, live_ref, x_ref, tiles_ref, out_ref, acc_ref):
    step = pl.program_id(0)
    live = live_ref[0]

    @pl.when(step == 0)
    def _():
        acc_ref[...] = jnp.zeros_like(acc_ref)

    @pl.when(step * SLOTS < live)
    def _():
        for k in range(SLOTS):
            slot = step * SLOTS + k
            col = cols_ref[slot]
            row = rows_ref[slot]
            start = pl.multiple_of((col % 4) * TILE, TILE)
            block = x_ref[col // 4, :, pl.ds(start, TILE)]
            block = jnp.where(slot < live, block, jnp.zeros_like(block))
            acc_ref[row] += dot(block, tiles_ref[k], ((1,), (1,)))

    @pl.when(step == pl.num_programs(0) - 1)
    def _():
        out_ref[...] = acc_ref[...].astype(BF16)


def aggregate(x_all, tiles, rows, cols, live, row_blocks):
    slots = tiles.shape[0]
    feats = x_all.shape[1]

    def tile_map(step, rows, cols, live):
        return (jnp.minimum(step, (live[0] - 1) // SLOTS), 0, 0)

    return pl.pallas_call(
        aggregate_kernel,
        out_shape=jax.ShapeDtypeStruct((row_blocks, feats, TILE), BF16),
        grid_spec=pltpu.PrefetchScalarGridSpec(
            num_scalar_prefetch=3,
            grid=(slots // SLOTS,),
            in_specs=[
                pl.BlockSpec(x_all.shape, lambda *_: (0, 0, 0)),
                pl.BlockSpec((SLOTS, TILE, TILE), tile_map),
            ],
            out_specs=pl.BlockSpec((row_blocks, feats, TILE), lambda *_: (0, 0, 0)),
            scratch_shapes=[pltpu.VMEM((row_blocks, feats, TILE), F32)],
        ),
    )(rows, cols, live, x_all, tiles)


def pack_kernel(parts_ref, weights_ref, out_ref):
    total = jnp.sum(parts_ref[...].astype(F32), axis=0).astype(BF16)
    nodes = total.shape[0]
    for k in range(out_ref.shape[0]):
        out_ref[k, :nodes, :] = total
        out_ref[k, nodes:, :] = weights_ref[...]


def node_kernel(all_ref, own_ref, labels_ref, mask_ref, out_ref, y_ref):
    groups = all_ref.shape[0]
    blocks = 4
    for f in range(groups):
        for b in range(blocks):
            y_ref[16 * f : 16 * f + 16, TILE * b : TILE * b + TILE] = all_ref[f, 16 * b : 16 * b + 16, :]
    y = y_ref[...]
    base = 16 * blocks
    w1 = all_ref[:, base : base + 32, :].reshape(32 * groups, TILE)
    w2a = all_ref[:, base + 32 : base + 64, :].reshape(32 * groups, TILE)
    w2b = all_ref[:, base + 64 : base + 96, :].reshape(32 * groups, TILE)

    def bias_of(block):
        wide = block.astype(F32)
        return wide[:, REST : REST + 1] + wide[:, REST + 1 : REST + 2] + wide[:, REST + 2 : REST + 3]

    preact = dot(w1, y) + bias_of(w2b)
    _, t = gelu_parts(preact)
    hidden = (0.5 * preact * (1.0 + t)).astype(BF16)
    logits_a = dot(w2a, hidden, ((0,), (0,)))
    logits_b = dot(w2b, hidden, ((0,), (0,)))[:48]
    labels = labels_ref[...]
    mask = mask_ref[...].astype(F32)
    class_a = lax.broadcasted_iota(jnp.int32, logits_a.shape, 0)
    class_b = lax.broadcasted_iota(jnp.int32, logits_b.shape, 0) + TILE
    logits_b = jnp.where(class_b < CLASSES, logits_b, -jnp.inf)
    top = jnp.maximum(
        jnp.max(logits_a, axis=0, keepdims=True), jnp.max(logits_b, axis=0, keepdims=True)
    )
    shifted_a = logits_a - top
    shifted_b = logits_b - top
    exp_a = jnp.exp(shifted_a)
    exp_b = jnp.exp(shifted_b)
    expsum = jnp.sum(exp_a, axis=0, keepdims=True) + jnp.sum(exp_b, axis=0, keepdims=True)
    hit_a = class_a == labels
    hit_b = class_b == labels
    picked = jnp.sum(jnp.where(hit_a, shifted_a, 0.0), axis=0, keepdims=True) + jnp.sum(
        jnp.where(hit_b, shifted_b, 0.0), axis=0, keepdims=True
    )
    loss = jnp.sum((jnp.log(expsum) - picked) * mask)
    count = jnp.sum(mask)
    inverse = 1.0 / expsum
    grad_a = ((exp_a * inverse - hit_a.astype(F32)) * mask).astype(BF16)
    grad_b = ((exp_b * inverse - hit_b.astype(F32)) * mask).astype(BF16)

    own_w1 = own_ref[:32, :]
    own_w2a = own_ref[32:64, :]
    own_w2b = own_ref[64:96, :]
    own_pre = dot(own_w1, y) + bias_of(own_w2b)
    squared, own_t = gelu_parts(own_pre)
    own_hidden = (0.5 * own_pre * (1.0 + own_t)).astype(BF16)
    slope = 0.5 * (1.0 + own_t) + 0.5 * own_pre * (1.0 - own_t * own_t) * (
        GELU_SCALE * (1.0 + 3.0 * GELU_CUBE * squared)
    )
    grad_hidden = dot(own_w2a, grad_a) + dot(own_w2b[:, :48], grad_b)
    grad_pre = (grad_hidden * slope).astype(BF16)
    grad_b1 = jnp.sum(grad_pre.astype(F32), axis=1, keepdims=True)
    grad_w1 = dot(grad_pre, y, ((1,), (1,)))
    grad_w2a = dot(own_hidden, grad_a, ((1,), (1,)))
    grad_w2b = dot(own_hidden, grad_b, ((1,), (1,)))
    lane = lax.broadcasted_iota(jnp.int32, (32, TILE), 1)
    sub = lax.broadcasted_iota(jnp.int32, (32, TILE), 0)
    wide = jnp.concatenate([grad_w2b, jnp.zeros((32, TILE - 48), F32)], axis=1)
    extra = jnp.where(sub == 0, loss, jnp.where(sub == 1, count, 0.0))
    last = jnp.where(
        lane < REST, wide, jnp.where(lane == REST, grad_b1, jnp.where(lane == REST + 1, extra, 0.0))
    )
    for k in range(out_ref.shape[0]):
        out_ref[k, :32, :] = grad_w1
        out_ref[k, 32:64, :] = grad_w2a
        out_ref[k, 64:, :] = last


def middle_kernel(parts_ref, out_ref):
    total = jnp.sum(parts_ref[...], axis=0)
    upper = total.astype(BF16).astype(F32)
    rest = total - upper
    shape = (32, TILE)
    lane = lax.broadcasted_iota(jnp.int32, shape, 1)
    moved = pltpu.roll(rest[64:], 2, 1)
    tail = jnp.where((lane >= REST + 2) & (lane < REST + 4), moved, upper[64:])
    for k in range(out_ref.shape[0]):
        out_ref[k, :64, :] = upper[:64].astype(BF16)
        out_ref[k, 64:, :] = tail.astype(BF16)


def final_kernel(parts_ref, w1_ref, w2_ref, b1_ref, loss_ref):
    total = jnp.sum(parts_ref[...].astype(F32), axis=0)
    tail = total[64:]
    tail = tail + pltpu.roll(tail, TILE - 2, 1)
    count = tail[1:2, REST + 1 : REST + 2]
    inverse = 1.0 / count
    w1_ref[...] = total[:32] * inverse
    w2_ref[:, :TILE] = total[32:64] * inverse
    w2_ref[:, TILE:] = total[64:, :REST] * inverse
    b1_ref[...] = tail[:, REST : REST + 1] * inverse
    loss_ref[...] = tail[0:1, REST + 1 : REST + 2] * inverse


def call(kernel, out_shape, *args, scratch=()):
    return pl.pallas_call(kernel, out_shape=out_shape, scratch_shapes=scratch)(*args)


def on_device(
    features,
    weight_in,
    bias,
    weight_out,
    adj_tiles,
    tile_rows,
    tile_cols,
    tile_live,
    labels,
    label_mask,
):
    n_row, n_col, n_feat = lax.axis_size("row"), lax.axis_size("col"), lax.axis_size("feat")
    row_blocks = features.shape[0] * n_col // TILE

    x_mine = features.T
    x_all = lax.all_to_all(jnp.broadcast_to(x_mine, (n_row, *x_mine.shape)), "row", 0, 0)
    partial = aggregate(
        x_all,
        adj_tiles.reshape(adj_tiles.shape[2:]),
        tile_rows.reshape(-1),
        tile_cols.reshape(-1),
        tile_live.reshape(-1),
        row_blocks,
    )
    feats = x_mine.shape[0]
    parts = lax.all_to_all(partial.reshape(n_col, -1, TILE), "col", 0, 0)

    def rounded(v):
        return lax.reduce_precision(v, 8, 7)

    high = rounded(bias)
    middle = rounded(bias - high)
    low = rounded(bias - high - middle)
    bias_lanes = jnp.stack([high, middle, low], axis=1).astype(BF16)
    tail = jnp.concatenate(
        [weight_out[:, TILE:], bias_lanes, jnp.zeros((32, TILE - REST - 3), BF16)], axis=1
    )
    own = jnp.concatenate([weight_in.T, weight_out[:, :TILE], tail], axis=0)
    message_rows = parts.shape[1] + own.shape[0]
    message = call(pack_kernel, jax.ShapeDtypeStruct((n_feat, message_rows, TILE), BF16), parts, own)
    gathered = lax.all_to_all(message, "feat", 0, 0)
    grads = call(
        node_kernel,
        jax.ShapeDtypeStruct((n_row, 96, TILE), F32),
        gathered,
        own,
        labels.reshape(1, -1),
        label_mask.reshape(1, -1),
        scratch=[pltpu.VMEM((feats * n_feat, features.shape[0]), BF16)],
    )
    grads = lax.all_to_all(grads, "row", 0, 0)
    grads = call(middle_kernel, jax.ShapeDtypeStruct((n_col, 96, TILE), BF16), grads)
    grads = lax.all_to_all(grads, "col", 0, 0)
    w1, w2, b1, loss = call(
        final_kernel,
        (
            jax.ShapeDtypeStruct((32, TILE), F32),
            jax.ShapeDtypeStruct((32, CLASSES), F32),
            jax.ShapeDtypeStruct((32, 1), F32),
            jax.ShapeDtypeStruct((1, 1), F32),
        ),
        grads,
    )
    return (loss.reshape(()), w1.T, b1.reshape(-1), w2)


def solution(mesh):
    in_specs = (
        P(("col", "row"), "feat"),
        P(None, "feat"),
        P("feat"),
        P("feat", None),
        P("row", "col", None, None, None),
        P("row", "col", None),
        P("row", "col", None),
        P("row", "col"),
        P(("row", "col")),
        P(("row", "col")),
    )
    out_specs = (P(), P(None, "feat"), P("feat"), P("feat", None))
    return jax.shard_map(
        on_device, mesh=mesh, in_specs=in_specs, out_specs=out_specs, check_vma=False
    )
```

time: 410 us -> 90.6 us (0.22); the launches traced: 404 us -> 89 us
  blocking collectives: 261 us -> 42.3 us
  waiting for transfers between devices: 83.6 us -> 8.99 us
  matrix products: 29.3 us -> 0 us
  starting transfers between devices: 0.12 us -> 15.8 us
  between operations: 15.3 us -> 1.35 us
  Pallas kernels: 0 us -> 13.1 us
    psum x2 -> x0, blocking collectives: 210 us -> none  [the longest x1 136 us: on_device(): lax.psum((loss_part, bias_part, output_part, input_part), ('row', 'col'))]
    psum x1 -> x0, waiting for transfers between devices: 62 us -> none  [on_device(): lax.psum(jnp.dot(hidden, weight_out, preferred_element_type=jnp.float32),...]
    all_gather x3 -> x0, blocking collectives: 51.2 us -> none  [the longest x1 25.3 us: on_device(): row_gradients = lax.all_gather(grad_preact, 'col', axis=0, tiled=True)]
    all_to_all x0 -> x3, blocking collectives: none -> 42.3 us  [the longest x1 15.9 us: on_device(): grads = lax.all_to_all(grads, 'row', 0, 0)]
    dot_general x11 -> x0, matrix products: 29.3 us -> none  [the longest x1 11.3 us: local_sums(): jnp.einsum('tij,tjh->tih', slot_tiles, picked, preferred_element_type=jnp...]
    reduce_scatter x2 -> x0, waiting for transfers between devices: 21.5 us -> none  [the longest x1 21.5 us: on_device(): lax.psum_scatter(backward, 'row', scatter_dimension=0, tiled=True)]
    all_to_all x0 -> x2, starting transfers between devices: none -> 15.8 us  [the longest x1 11.3 us: on_device(): parts = lax.all_to_all(partial.reshape(n_col, -1, TILE), 'col', 0, 0)]
    pallas_call x0 -> x5, Pallas kernels: none -> 13.1 us  [the longest x4 7.79 us: call(): pl.pallas_call(kernel, out_shape=out_shape, scratch_shapes=scratch)(*args)]
  transfers between devices with their start and end apart: 3 -> 2, of which waited for: 2 -> 2; matrix products, arithmetic and copies ran while one was open for 1% -> 4% of each run, Pallas kernels for 0% -> 0%
where the time goes in v1:
time: 90.6 us; the launch traced here: 89 us
  blocking collectives  42.3 us (47%)
  starting transfers between devices  15.8 us (17%)
  Pallas kernels  13.1 us (14%)
  waiting for transfers between devices  8.99 us (10%)
  other arithmetic  4.51 us (5%)
  local copies, waits for them, and re-layouts  3.03 us (3%)
  between operations  1.35 us (1%)
    all_to_all x1, blocking collectives, on_device(): grads = lax.all_to_all(grads, 'row', 0, 0)  15.9 us
    all_to_all x1, blocking collectives, on_device(): grads = lax.all_to_all(grads, 'col', 0, 0)  13.8 us
    all_to_all x1, blocking collectives, on_device(): gathered = lax.all_to_all(message, 'feat', 0, 0)  12.6 us
    all_to_all x1, starting transfers between devices, on_device(): parts = lax.all_to_all(partial.reshape(n_col, -1, TILE), 'col', 0, 0)  11.3 us
    pallas_call x4, Pallas kernels, call(): pl.pallas_call(kernel, out_shape=out_shape, scratch_shapes=scratch)(*args)  7.79 us
    all_to_all x1, waiting for transfers between devices, on_device(): parts = lax.all_to_all(partial.reshape(n_col, -1, TILE), 'col', 0, 0)  6.57 us
    pallas_call x1, Pallas kernels, aggregate(): pl.pallas_call(aggregate_kernel, out_shape=jax.ShapeDtypeStruct((row_bloc...  5.3 us
    all_to_all x1, starting transfers between devices, on_device(): lax.all_to_all(jnp.broadcast_to(x_mine, (n_row, *x_mine.shape)), 'row', 0...  4.46 us
  transfers between devices with their start and end apart: 2, of which 2 were waited for; matrix products, arithmetic and copies ran while one was open for 4% of the time, Pallas kernels for 0%

profile of v1, /device:TPU:32, one launch (start us, length us, event | category | flops | bytes accessed | tf_op | source)
XLA Modules:
  0.0 89.0 jit_solution(3977020906887943110)
XLA Ops:
  0.6 0.0 slice-start.1
  0.7 1.3 %broadcast_in_dim.6 = bf16[4,16,512]{2,1,0:T(8,128)(2,1)} broadcast(bf16[16,512]{1,0:T(8,128)(2,1)} %bitcast.18), dimensions={1,2} | broadcast | bytes 81920 | tf_op jit(solution)/shard_map/broadcast_in_dim | solution.py:204
  2.0 4.5 %all-to-all-start = ((bf16[4,16,512]{2,1,0:T(8,128)(2,1)}), bf16[4,16,512]{2,1,0:T(8,128)(2,1)S(1)}, u32[]{:S(2)}, u32[]{:S(2)}) async-start(bf16[4,16,512]{2,1,0:T(8,128)(2,1)} %broadcast_in_dim.6), calls=%async_computation | async-start | bytes 131072 | tf_op jit(solution)/shard_map/all_to_all | solution.py:204
  7.1 1.3 %reduce.rows_ref = s32[384]{0:T(512)} reduce(s32[1,1,384]{2,1,0:T(1,128)} %param.15, s32[]{:T(128)} %constant.6), dimensions={0,1}, to_apply=%param.15.reduce_sub_computation | reduce | bytes 3076 | tf_op args[5]
  8.4 1.3 %reduce.1.cols_ref = s32[384]{0:T(512)} reduce(s32[1,1,384]{2,1,0:T(1,128)} %param.16, s32[]{:T(128)} %constant.6), dimensions={0,1}, to_apply=%param.16.reduce_sub_computation | reduce | bytes 3076 | tf_op args[6]
  9.7 2.4 %all-to-all-done.x_ref = bf16[4,16,512]{2,1,0:T(8,128)(2,1)S(1)} async-done(((bf16[4,16,512]{2,1,0:T(8,128)(2,1)}), bf16[4,16,512]{2,1,0:T(8,128)(2,1)S(1)}, u32[]{:S(2)}, u32[]{:S(2)}) %all-to-all-start) | async-done | bytes 65568 | tf_op jit(solution)/shard_map/all_to_all | solution.py:204
  12.1 0.6 copy-done.1
  12.7 5.3 %shard_map.129 = bf16[32,16,128]{2,1,0:T(8,128)(2,1)} custom-call(s32[384]{0:T(512)} %reduce.rows_ref, s32[384]{0:T(512)} %reduce.1.cols_ref, s32[1]{0:T(128)} %bitcast.15.live_ref, bf16[4,16,512]{2,1,0:T(8,128)(2,1)} %copy-done.1, bf16[384,128,128]{2,1,0:T(8,128)(2,1)} %bitcast.16), custom_call_target="tpu_custom_call" | custom-call | tf_op jit(solution)/shard_map/pallas_call | solution.py:61
  18.0 11.3 %all-to-all-start.1 = ((bf16[8,64,128]{2,1,0:T(8,128)(2,1)}), bf16[8,64,128]{2,1,0:T(8,128)(2,1)S(1)}, u32[]{:S(2)}, u32[]{:S(2)}) async-start(bf16[8,64,128]{2,1,0:T(8,128)(2,1)} %bitcast.17), calls=%async_computation.1 | async-start | bytes 262144 | tf_op jit(solution)/shard_map/all_to_all | solution.py:214
  29.3 0.1 copy.19
  29.4 0.1 copy.18
  29.5 0.1 copy.17
  29.7 0.1 concatenate.7
  29.8 0.6 pad_maximum_fusion.weights_ref.own_ref
  30.4 6.6 %all-to-all-done.1.parts_ref = bf16[8,64,128]{2,1,0:T(8,128)(2,1)S(1)} async-done(((bf16[8,64,128]{2,1,0:T(8,128)(2,1)}), bf16[8,64,128]{2,1,0:T(8,128)(2,1)S(1)}, u32[]{:S(2)}, u32[]{:S(2)}) %all-to-all-start.1) | async-done | bytes 131104 | tf_op jit(solution)/shard_map/all_to_all | solution.py:214
  37.0 0.6 copy-done
  37.6 1.7 %shard_map.130 = bf16[8,160,128]{2,1,0:T(8,128)(2,1)} custom-call(bf16[8,64,128]{2,1,0:T(8,128)(2,1)} %copy-done, bf16[96,128]{1,0:T(8,128)(2,1)} %pad_maximum_fusion.weights_ref.own_ref), custom_call_target="tpu_custom_call" | custom-call | tf_op jit(solution)/shard_map/pallas_call | solution.py:185
  39.3 12.6 %all_to_all.25.all_ref = bf16[8,160,128]{2,1,0:T(8,128)(2,1)} all-to-all(bf16[8,160,128]{2,1,0:T(8,128)(2,1)} %shard_map.130), channel_id=1, replica_groups=mesh['row'=4,'col'=8,'feat'=8] {'feat'}, dimensions={0} | all-to-all | bytes 655360 | tf_op jit(solution)/shard_map/all_to_all | solution.py:229
  51.9 2.7 %shard_map.131 = f32[4,96,128]{2,1,0:T(8,128)} custom-call(bf16[8,160,128]{2,1,0:T(8,128)(2,1)} %all_to_all.25.all_ref, bf16[96,128]{1,0:T(8,128)(2,1)} %pad_maximum_fusion.weights_ref.own_ref, s32[1,512]{1,0:T(1,128)} %bitcast.20, s32[1,512]{1,0:T(1,128)} %bitcast.21), custom_call_target="tpu_custom_call" | custom-call | tf_op jit(solution)/shard_map/pallas_call | solution.py:185
  54.6 15.9 %all_to_all.26.parts_ref = f32[4,96,128]{2,1,0:T(8,128)} all-to-all(f32[4,96,128]{2,1,0:T(8,128)} %shard_map.131), channel_id=1, replica_groups=mesh['row'=4,'col'=8,'feat'=8] {'row'}, dimensions={0} | all-to-all | bytes 393216 | tf_op jit(solution)/shard_map/all_to_all | solution.py:239
  70.5 1.7 %shard_map.132 = bf16[8,96,128]{2,1,0:T(8,128)(2,1)} custom-call(f32[4,96,128]{2,1,0:T(8,128)} %all_to_all.26.parts_ref), custom_call_target="tpu_custom_call" | custom-call | tf_op jit(solution)/shard_map/pallas_call | solution.py:185
  72.1 13.8 %all_to_all.27.parts_ref = bf16[8,96,128]{2,1,0:T(8,128)(2,1)} all-to-all(bf16[8,96,128]{2,1,0:T(8,128)(2,1)} %shard_map.132), channel_id=1, replica_groups=mesh['row'=4,'col'=8,'feat'=8] {'col'}, dimensions={0} | all-to-all | bytes 393216 | tf_op jit(solution)/shard_map/all_to_all | solution.py:241
  85.9 1.7 %shard_map.133 = (f32[32,128]{1,0:T(8,128)}, f32[32,172]{1,0:T(8,128)}, f32[32,1]{1,0:T(8,128)}, f32[1,1]{1,0:T(1,128)}) custom-call(bf16[8,96,128]{2,1,0:T(8,128)(2,1)} %all_to_all.27.parts_ref), custom_call_target="tpu_custom_call" | custom-call | tf_op jit(solution)/shard_map/pallas_call | solution.py:185
  87.7 1.3 %reduce.2 = f32[32]{0:T(128)} reduce(f32[32,1]{1,0:T(8,128)} %get-tuple-element.10, f32[]{:T(128)} %constant.8), dimensions={1}, to_apply=%get-tuple-element.10.reduce_sub_computation | reduce | bytes 260 | tf_op jit(solution)/shard_map/pallas_call | solution.py:185
  (11 shorter events, 0.0 us)
Async XLA Ops:
  0.6 29.0 %slice-start = ((bf16[32,172]{1,0:T(8,128)(2,1)}), bf16[32,44]{1,0:T(8,128)(2,1)S(1)}, s32[]{:S(2)}) async-start(bf16[32,172]{1,0:T(8,128)(2,1)} %param.13), calls=%async_computation.5 | async-start | bytes 16384 | tf_op jit(solution)/shard_map/slice | solution.py:224
  0.6 29.1 %slice-start.1 = ((bf16[32,172]{1,0:T(8,128)(2,1)}), bf16[32,128]{1,0:T(8,128)(2,1)S(1)}, s32[]{:S(2)}) async-start(bf16[32,172]{1,0:T(8,128)(2,1)} %param.13), calls=%async_computation.6 | async-start | bytes 16384 | tf_op jit(solution)/shard_map/slice | solution.py:226
  0.7 28.7 %copy-start.3 = (f32[32]{0:T(128)S(1)}, f32[32]{0:T(128)}, u32[]{:S(2)}) copy-start(f32[32]{0:T(128)} %param.12) | copy-start | bytes 388
  0.7 29.1 %copy-start.2 = (bf16[128,32]{0,1:T(8,128)(2,1)S(1)}, bf16[128,32]{0,1:T(8,128)(2,1)}, u32[]{:S(2)}) copy-start(bf16[128,32]{0,1:T(8,128)(2,1)} %param.11) | copy-start | bytes 24580
  2.0 10.1 %all-to-all-start = ((bf16[4,16,512]{2,1,0:T(8,128)(2,1)}), bf16[4,16,512]{2,1,0:T(8,128)(2,1)S(1)}, u32[]{:S(2)}, u32[]{:S(2)}) async-start(bf16[4,16,512]{2,1,0:T(8,128)(2,1)} %broadcast_in_dim.6), calls=%async_computation | async-start | bytes 131072 | tf_op jit(solution)/shard_map/all_to_all | solution.py:204
  12.1 0.6 copy-start.1
  18.0 18.9 %all-to-all-start.1 = ((bf16[8,64,128]{2,1,0:T(8,128)(2,1)}), bf16[8,64,128]{2,1,0:T(8,128)(2,1)S(1)}, u32[]{:S(2)}, u32[]{:S(2)}) async-start(bf16[8,64,128]{2,1,0:T(8,128)(2,1)} %bitcast.17), calls=%async_computation.1 | async-start | bytes 262144 | tf_op jit(solution)/shard_map/all_to_all | solution.py:214
  37.0 0.6 copy-start

commit v2 on v1

v2 whole, which is shorter than its diff:
```python
import functools

import jax
import jax.numpy as jnp
from jax import lax
from jax.experimental import pallas as pl
from jax.experimental.pallas import tpu as pltpu
from jax.sharding import PartitionSpec as P

CLASSES = 172
TILE = 128
REST = CLASSES - TILE
HALF = TILE // 2
GELU_SCALE = 0.7978845608028654
GELU_CUBE = 0.044715
COST = 60000000
F32 = jnp.float32
BF16 = jnp.bfloat16
IN_VMEM = pl.BlockSpec(memory_space=pltpu.VMEM)
IN_SMEM = pl.BlockSpec(memory_space=pltpu.SMEM)

def dot(a, b, contract=((1,), (0,))):
    return lax.dot_general(a, b, (contract, ((), ())), preferred_element_type=F32)

def gelu_parts(v):
    squared = v * v
    t = jnp.tanh(GELU_SCALE * v * (1.0 + GELU_CUBE * squared))
    return squared, t

def call(kernel, out_shape, *args, scalars=0, scratch=(), limit=16 * 2**20, cost=None):
    placed = args[:scalars] + tuple(
        pltpu.with_memory_space_constraint(arg, pltpu.VMEM) for arg in args[scalars:]
    )
    many = isinstance(out_shape, tuple)
    return pl.pallas_call(
        kernel,
        out_shape=out_shape,
        in_specs=[IN_SMEM] * scalars + [IN_VMEM] * (len(args) - scalars),
        out_specs=(IN_VMEM,) * len(out_shape) if many else IN_VMEM,
        scratch_shapes=scratch,
        compiler_params=pltpu.CompilerParams(vmem_limit_bytes=limit),
        cost_estimate=cost,
    )(*placed)

def pair_kernel(x_ref, other_ref, out_ref):
    first = lax.axis_index("core") == 0
    mine, other = x_ref[...], other_ref[...]
    feats = mine.shape[0]
    out_ref[:feats, :] = jnp.where(first, mine, other)
    out_ref[feats:, :] = jnp.where(first, other, mine)


def load_kernel(tiles_ref, out_ref, sems):
    chunk = tiles_ref.shape[0] // sems.shape[0]
    copies = []
    for k in range(sems.shape[0]):
        part = pl.ds(k * chunk, chunk)
        copies.append(pltpu.make_async_copy(tiles_ref.at[part], out_ref.at[part], sems.at[k]))
    for copy in copies:
        copy.start()
    for copy in copies:
        copy.wait()


def setup_kernel(live_ref, rows_ref, cols_ref, w1_ref, w2_ref, bias_ref, slots_ref, weights_ref):
    inverse(live_ref, rows_ref, cols_ref, slots_ref)
    pack_weights(w1_ref, w2_ref, bias_ref, weights_ref)


def inverse(live_ref, rows_ref, cols_ref, out_ref):
    places = out_ref.shape[1]
    slots = rows_ref.shape[2]
    slot = lax.broadcasted_iota(jnp.int32, (1, slots), 1)
    rows = rows_ref[0]
    place = ((rows >> 2) * 2 + (rows & 1)) * (places // 16) + cols_ref[0]
    mine = (slot < live_ref[0, 0]) & (((rows >> 1) & 1) == lax.axis_index("core"))
    place = jnp.where(mine, place, -1)
    here = lax.broadcasted_iota(jnp.int32, (places, slots), 0) == place
    onehot = jnp.where(here, 1.0, 0.0).astype(BF16)
    number = lax.broadcasted_iota(jnp.int32, (8, slots), 1) + 1
    digit = lax.broadcasted_iota(jnp.int32, (8, slots), 0)
    digits = jnp.where(digit == 0, number & 127, jnp.where(digit == 1, number >> 7, 0))
    found = dot(digits.astype(F32).astype(BF16), onehot, ((1,), (1,)))
    out_ref[...] = (found[0:1] + 128.0 * found[1:2]).astype(jnp.int32) - 1


def aggregate_kernel(slot_ref, x0_ref, x1_ref, x2_ref, x3_ref, tiles_ref, out_ref, all_ref):
    feats, nodes = x0_ref.shape
    row, n_row = lax.axis_index("row"), lax.axis_size("row")
    for k, part in enumerate((x0_ref, x1_ref, x2_ref, x3_ref)):
        source = lax.rem(row + n_row - k, n_row)
        all_ref[:, pl.ds(pl.multiple_of(source * nodes, TILE), nodes)] = part[...]
    x_all = all_ref[...]
    groups = out_ref.shape[0]
    col_blocks = slot_ref.shape[1] // (2 * groups)
    for group in range(groups):
        strips = []
        for block in (2 * group, 2 * group + 1):
            tiles = []
            for j in range(col_blocks):
                slot = slot_ref[0, block * col_blocks + j]
                tile = tiles_ref[jnp.maximum(slot, 0)]
                tiles.append(jnp.where(slot >= 0, tile, jnp.zeros_like(tile)))
            strips.append(jnp.concatenate(tiles, 1))
        wide = dot(x_all, jnp.concatenate(strips, 0), ((1,), (1,))).astype(BF16)
        out_ref[group, :feats, :] = wide[:, :TILE]
        out_ref[group, feats:, :] = wide[:, TILE:]


def pack_weights(w1_ref, w2_ref, bias_ref, out_ref):
    shape = (32, TILE)
    lane = lax.broadcasted_iota(jnp.int32, shape, 1)
    sub = lax.broadcasted_iota(jnp.int32, shape, 0)
    row = jnp.concatenate([bias_ref[...], jnp.zeros((1, TILE - 32), F32)], axis=1)
    bias = jnp.sum(jnp.where(lane == sub, row, 0.0), axis=1, keepdims=True)
    high = bias.astype(BF16).astype(F32)
    middle = (bias - high).astype(BF16).astype(F32)
    low = bias - high - middle
    rest = jnp.concatenate(
        [w2_ref[:, TILE:].astype(F32), jnp.zeros((32, TILE - REST), F32)], axis=1
    )
    for place, part in ((REST, high), (REST + 1, middle), (REST + 2, low)):
        rest = jnp.where(lane == place, part, rest)
    out_ref[:32, :] = w1_ref[...]
    out_ref[32:64, :] = w2_ref[:, :TILE]
    out_ref[64:, :] = rest.astype(BF16)

def total_kernel(parts_ref, weights_ref, out_ref):
    total = jnp.sum(parts_ref[...].astype(F32), axis=0).astype(BF16)
    rows = total.shape[0]
    for k in range(out_ref.shape[0]):
        out_ref[k, :rows, :] = total
        out_ref[k, rows:, :] = weights_ref[...]

def lanes16():
    return lax.broadcasted_iota(jnp.int32, (16, TILE), 1)

def is_fine(lane):
    return (lane == REST) | (lane == REST + 1) | (lane == HALF + REST)

def split_tail(tail):
    upper = tail.astype(BF16).astype(F32)
    moved = pltpu.roll(tail - upper, 2, 1)
    return jnp.where(is_fine(lanes16() - 2), moved, upper).astype(BF16)

def join_tail(tail):
    return jnp.where(is_fine(lanes16()), tail + pltpu.roll(tail, TILE - 2, 1), tail)

def node_kernel(all_ref, own_ref, labels_ref, mask_ref, out_ref, y_ref):
    groups = all_ref.shape[0]
    for f in range(groups):
        for b in range(2):
            feat, node = 32 * (f // 2), TILE * (2 * (f % 2) + b)
            y_ref[feat : feat + 32, node : node + TILE] = all_ref[f, 32 * b : 32 * b + 32, :]
    y = y_ref[...]
    w1 = all_ref[:, 64:96, :].reshape(32 * groups, TILE)
    w2a = all_ref[:, 96:128, :].reshape(32 * groups, TILE)
    w2b = all_ref[:, 128:, :].reshape(32 * groups, TILE)

    def bias_of(block):
        wide = block.astype(F32)
        return wide[:, REST : REST + 1] + wide[:, REST + 1 : REST + 2] + wide[:, REST + 2 : REST + 3]

    preact = dot(w1, y) + bias_of(w2b)
    _, t = gelu_parts(preact)
    hidden = (0.5 * preact * (1.0 + t)).astype(BF16)
    logits_a = dot(w2a, hidden, ((0,), (0,)))
    logits_b = dot(w2b, hidden, ((0,), (0,)))[:48]
    labels = labels_ref[...]
    mask = mask_ref[...].astype(F32)
    class_a = lax.broadcasted_iota(jnp.int32, logits_a.shape, 0)
    class_b = lax.broadcasted_iota(jnp.int32, logits_b.shape, 0) + TILE
    logits_b = jnp.where(class_b < CLASSES, logits_b, -jnp.inf)
    top = jnp.maximum(
        jnp.max(logits_a, axis=0, keepdims=True), jnp.max(logits_b, axis=0, keepdims=True)
    )
    shifted_a = logits_a - top
    shifted_b = logits_b - top
    exp_a = jnp.exp(shifted_a)
    exp_b = jnp.exp(shifted_b)
    expsum = jnp.sum(exp_a, axis=0, keepdims=True) + jnp.sum(exp_b, axis=0, keepdims=True)
    hit_a = class_a == labels
    hit_b = class_b == labels
    picked = jnp.sum(jnp.where(hit_a, shifted_a, 0.0), axis=0, keepdims=True) + jnp.sum(
        jnp.where(hit_b, shifted_b, 0.0), axis=0, keepdims=True
    )
    loss = jnp.sum((jnp.log(expsum) - picked) * mask)
    count = jnp.sum(mask)
    inverse = 1.0 / expsum
    grad_a = ((exp_a * inverse - hit_a.astype(F32)) * mask).astype(BF16)
    grad_b = ((exp_b * inverse - hit_b.astype(F32)) * mask).astype(BF16)

    own_w1 = own_ref[:32, :]
    own_w2a = own_ref[32:64, :]
    own_w2b = own_ref[64:, :]
    own_pre = dot(own_w1, y) + bias_of(own_w2b)
    squared, own_t = gelu_parts(own_pre)
    own_hidden = (0.5 * own_pre * (1.0 + own_t)).astype(BF16)
    slope = 0.5 * (1.0 + own_t) + 0.5 * own_pre * (1.0 - own_t * own_t) * (
        GELU_SCALE * (1.0 + 3.0 * GELU_CUBE * squared)
    )
    grad_hidden = dot(own_w2a, grad_a) + dot(own_w2b[:, :48], grad_b)
    grad_pre = (grad_hidden * slope).astype(BF16)
    grad_b1 = jnp.sum(grad_pre.astype(F32), axis=1, keepdims=True)
    grad_w1 = dot(grad_pre, y, ((1,), (1,))).astype(BF16)
    grad_w2a = dot(own_hidden, grad_a, ((1,), (1,))).astype(BF16)
    grad_w2b = dot(own_hidden, grad_b, ((1,), (1,)))
    lane = lanes16()
    sub = lax.broadcasted_iota(jnp.int32, lane.shape, 0)
    wide = jnp.concatenate([grad_w2b, jnp.zeros((32, TILE - 48), F32)], axis=1)
    extra = jnp.where(sub == 0, loss, jnp.where(sub == 1, count, 0.0))
    tail = jnp.where(lane < HALF, wide[:16], pltpu.roll(wide[16:], HALF, 1))
    tail = jnp.where(lane == REST, grad_b1[:16], tail)
    tail = jnp.where(lane == REST + 1, extra, tail)
    tail = jnp.where(lane == HALF + REST, grad_b1[16:], tail)
    tail = split_tail(tail)
    for k in range(out_ref.shape[0]):
        out_ref[k, :32, :] = grad_w1
        out_ref[k, 32:64, :] = grad_w2a
        out_ref[k, 64:, :] = tail

def middle_kernel(parts_ref, out_ref):
    total = jnp.sum(parts_ref[...].astype(F32), axis=0)
    tail = split_tail(join_tail(total[64:]))
    for k in range(out_ref.shape[0]):
        out_ref[k, :64, :] = total[:64].astype(BF16)
        out_ref[k, 64:, :] = tail

def final_kernel(parts_ref, w1_ref, w2_ref, b1_ref, loss_ref):
    total = jnp.sum(parts_ref[...].astype(F32), axis=0)
    tail = join_tail(total[64:])
    inverse = 1.0 / tail[1:2, REST + 1 : REST + 2]
    w1_ref[...] = total[:32] * inverse
    w2_ref[:, :TILE] = total[32:64] * inverse
    w2_ref[:16, TILE:] = tail[:, :REST] * inverse
    w2_ref[16:, TILE:] = pltpu.roll(tail, HALF, 1)[:, :REST] * inverse
    column = jnp.concatenate(
        [tail[:, REST : REST + 1], tail[:, HALF + REST : HALF + REST + 1]], axis=0
    )
    square = (32, 32)
    eye = lax.broadcasted_iota(jnp.int32, square, 0) == lax.broadcasted_iota(jnp.int32, square, 1)
    b1_ref[...] = jnp.sum(jnp.where(eye, column, 0.0), axis=0, keepdims=True) * inverse
    loss_ref[...] = tail[0:1, REST + 1 : REST + 2] * inverse

def on_device(
    features,
    weight_in,
    bias,
    weight_out,
    adj_tiles,
    tile_rows,
    tile_cols,
    tile_live,
    labels,
    label_mask,
):
    n_row, n_col = lax.axis_size("row"), lax.axis_size("col")
    n_core = lax.axis_size("core")
    n_feat = lax.axis_size("x") * n_core
    nodes, feats = features.shape
    row_blocks = nodes * n_col // TILE
    col_blocks = nodes * n_row // TILE
    grad_rows = 80

    x_mine = features.T
    x_other = lax.ppermute(x_mine, "core", [(0, 1), (1, 0)])
    x_pair = call(pair_kernel, pltpu.VMEM((2 * feats, nodes), BF16), x_mine, x_other)
    x_rows = [
        lax.ppermute(x_pair, "row", [(r, (r + k) % n_row) for r in range(n_row)])
        for k in range(1, n_row)
    ]
    tiles = adj_tiles.reshape(adj_tiles.shape[2:])
    loaded = pl.pallas_call(
        load_kernel,
        out_shape=pltpu.VMEM(tiles.shape, BF16),
        in_specs=[pl.BlockSpec(memory_space=pltpu.HBM)],
        out_specs=IN_VMEM,
        scratch_shapes=[pltpu.SemaphoreType.DMA((8,))],
        compiler_params=pltpu.CompilerParams(vmem_limit_bytes=2**20),
        cost_estimate=pl.CostEstimate(
            flops=0, bytes_accessed=4 * tiles.size, transcendentals=0
        ),
    )(pltpu.with_memory_space_constraint(tiles, pltpu.HBM))
    slots, weights = pl.pallas_call(
        setup_kernel,
        out_shape=(
            pltpu.VMEM((1, row_blocks // 2 * col_blocks), jnp.int32),
            pltpu.VMEM((96, TILE), BF16),
        ),
        in_specs=[IN_SMEM] + [IN_VMEM] * 5,
        out_specs=(IN_VMEM, IN_VMEM),
        compiler_params=pltpu.CompilerParams(vmem_limit_bytes=8 * 2**20),
    )(tile_live, tile_rows, tile_cols, weight_in.T, weight_out, bias.reshape(1, -1))
    partial = call(
        aggregate_kernel,
        pltpu.VMEM((n_col, 4 * feats, TILE), BF16),
        slots,
        x_pair,
        *x_rows,
        loaded,
        scalars=1,
        scratch=[pltpu.VMEM((2 * feats, n_row * nodes), BF16)],
    )
    parts = lax.all_to_all(partial, "col", 0, 0)
    rows = parts.shape[1] + weights.shape[0]
    message = call(total_kernel, pltpu.VMEM((n_feat, rows, TILE), BF16), parts, weights)
    gathered = lax.all_to_all(message, ("x", "core"), 0, 0)
    grads = call(
        node_kernel,
        pltpu.VMEM((n_row, grad_rows, TILE), BF16),
        gathered,
        weights,
        labels.reshape(1, -1),
        label_mask.reshape(1, -1),
        scratch=[pltpu.VMEM((feats * n_feat, nodes), BF16)],
    )
    grads = lax.all_to_all(grads, "row", 0, 0)
    grads = call(middle_kernel, pltpu.VMEM((n_col, grad_rows, TILE), BF16), grads)
    grads = lax.all_to_all(grads, "col", 0, 0)
    w1, w2, b1, loss = call(
        final_kernel,
        (
            jax.ShapeDtypeStruct((32, TILE), F32),
            jax.ShapeDtypeStruct((32, CLASSES), F32),
            jax.ShapeDtypeStruct((1, 32), F32),
            jax.ShapeDtypeStruct((1, 1), F32),
        ),
        grads,
    )
    return (loss.reshape(()), w1.T, b1.reshape(-1), w2)

def solution(mesh):
    shape = mesh.devices.shape
    split = jax.sharding.Mesh(
        mesh.devices.reshape(*shape[:2], shape[2] // 2, 2), ("row", "col", "x", "core")
    )
    feat = ("x", "core")
    in_specs = (
        P(("col", "row"), feat),
        P(None, feat),
        P(feat),
        P(feat, None),
        P("row", "col", None, None, None),
        P("row", "col", None),
        P("row", "col", None),
        P("row", "col"),
        P(("row", "col")),
        P(("row", "col")),
    )
    out_specs = (P(), P(None, feat), P(feat), P(feat, None))
    return jax.shard_map(
        on_device, mesh=split, in_specs=in_specs, out_specs=out_specs, check_vma=False
    )
```

time: 90.6 us -> 68.5 us (0.76)
  starting transfers between devices: 15.8 us -> 4.71 us
  waiting for transfers between devices: 8.99 us -> 1.39 us
  blocking collectives: 42.3 us -> 49.2 us
  other arithmetic: 4.51 us -> 0 us
  Pallas kernels: 13.1 us -> 10.2 us
  local copies, waits for them, and re-layouts: 3.03 us -> 0.76 us
    all_to_all x2 -> x0, starting transfers between devices: 15.8 us -> none  [the longest x1 11.3 us: on_device(): parts = lax.all_to_all(partial.reshape(n_col, -1, TILE), 'col', 0, 0)]
    all_to_all x1 -> x2, blocking collectives: 12.6 us -> 28.3 us  [the longest x1 16 us: on_device(): parts = lax.all_to_all(partial, 'col', 0, 0)]
    all_to_all x2 -> x0, waiting for transfers between devices: 8.99 us -> none  [the longest x1 6.57 us: on_device(): parts = lax.all_to_all(partial.reshape(n_col, -1, TILE), 'col', 0, 0)]
    all_to_all x1, blocking collectives: 15.9 us -> 9.05 us  [on_device(): grads = lax.all_to_all(grads, 'row', 0, 0)]
    ppermute x0 -> x4, starting transfers between devices: none -> 4.71 us  [the longest x3 4.61 us: on_device(): lax.ppermute(x_pair, 'row', [(r, (r + k) % n_row) for r in range(n_row)])]
    pallas_call x5 -> x8, Pallas kernels: 13.1 us -> 10.2 us  [the longest x6 5.33 us: call(): pl.pallas_call(kernel, out_shape=out_shape, in_specs=[IN_SMEM] * scalars...]
    unnamed x2 -> x0, other arithmetic: 2.55 us -> none
    all_to_all x1, blocking collectives: 13.8 us -> 11.8 us  [on_device(): grads = lax.all_to_all(grads, 'col', 0, 0)]
  transfers between devices with their start and end apart: 2 -> 4, of which waited for: 2 -> 1; matrix products, arithmetic and copies ran while one was open for 4% -> 0% of each run, Pallas kernels for 0% -> 7%
where the time goes in v2:
time: 68.5 us; the launch traced here: 67.7 us
  blocking collectives  49.2 us (72%)
  Pallas kernels  10.2 us (15%)
  starting transfers between devices  4.71 us (7%)
  between operations  1.44 us (2%)
  waiting for transfers between devices  1.39 us (2%)
  local copies, waits for them, and re-layouts  0.76 us (1%)
    all_to_all x1, blocking collectives, on_device(): parts = lax.all_to_all(partial, 'col', 0, 0)  16 us
    all_to_all x1, blocking collectives, on_device(): gathered = lax.all_to_all(message, ('x', 'core'), 0, 0)  12.3 us
    all_to_all x1, blocking collectives, on_device(): grads = lax.all_to_all(grads, 'col', 0, 0)  11.8 us
    all_to_all x1, blocking collectives, on_device(): grads = lax.all_to_all(grads, 'row', 0, 0)  9.05 us
    pallas_call x6, Pallas kernels, call(): pl.pallas_call(kernel, out_shape=out_shape, in_specs=[IN_SMEM] * scalars...  5.33 us
    pallas_call x1, Pallas kernels, on_device(): pl.pallas_call(load_kernel, out_shape=pltpu.VMEM(tiles.shape, BF16), in_s...  4.72 us
    ppermute x3, starting transfers between devices, on_device(): lax.ppermute(x_pair, 'row', [(r, (r + k) % n_row) for r in range(n_row)])  4.61 us
    ppermute x1, waiting for transfers between devices, on_device(): x_other = lax.ppermute(x_mine, 'core', [(0, 1), (1, 0)])  1.38 us
  transfers between devices with their start and end apart: 4, of which 1 were waited for; matrix products, arithmetic and copies ran while one was open for 0% of the time, Pallas kernels for 7%

profile of v2, /device:TPU:32, one launch (start us, length us, event | category | flops | bytes accessed | tf_op | source)
XLA Modules:
  0.0 67.7 jit_solution(14066800946055196847)
XLA Ops:
  0.6 0.1 collective-permute-start
  0.7 1.4 %collective-permute-done.other_ref = bf16[16,512]{1,0:T(8,128)(2,1)S(1)} collective-permute-done((bf16[16,512]{1,0:T(8,128)(2,1)}, bf16[16,512]{1,0:T(8,128)(2,1)S(1)}, u32[]{:S(2)}, u32[]{:S(2)}) %collective-permute-start) | collective-permute-done | bytes 16416 | tf_op jit(solution)/shard_map/ppermute | solution.py:266
  2.1 0.7 %copy-done.1 = bf16[512,16]{0,1:T(8,128)(2,1)S(1)} copy-done((bf16[512,16]{0,1:T(8,128)(2,1)S(1)}, bf16[512,16]{0,1:T(8,128)(2,1)}, u32[]{:S(2)}) %copy-start.1) | copy-done | bytes 16408
  2.8 3.0 %collective-permute-start.3 = (bf16[32,512]{1,0:T(8,128)(2,1)S(1)}, bf16[32,512]{1,0:T(8,128)(2,1)S(1)}, u32[]{:S(2)}, u32[]{:S(2)}) collective-permute-start(bf16[32,512]{1,0:T(8,128)(2,1)S(1)} %shard_map.130.x0_ref), channel_id=1, source_target_pairs={{0,192},{64,0},{128,64},{192,128},{1,193},{65,1},{129,65},{193,129... | collective-permute-start | bytes 98312 | tf_op jit(solution)/shard_map/ppermute | solution.py:269
  5.9 0.6 collective-permute-start.2
  6.5 1.0 %collective-permute-start.1 = (bf16[32,512]{1,0:T(8,128)(2,1)S(1)}, bf16[32,512]{1,0:T(8,128)(2,1)S(1)}, u32[]{:S(2)}, u32[]{:S(2)}) collective-permute-start(bf16[32,512]{1,0:T(8,128)(2,1)S(1)} %shard_map.130.x0_ref), channel_id=1, source_target_pairs={{0,64},{64,128},{128,192},{192,0},{1,65},{65,129},{129,193},{193,1... | collective-permute-start | bytes 98312 | tf_op jit(solution)/shard_map/ppermute | solution.py:269
  8.1 0.0 copy-start
  8.1 0.0 copy-start.2
  8.1 0.0 copy-start.5
  8.1 0.0 copy-start.6
  8.2 0.0 copy-start.7
  8.2 4.7 %shard_map.131.tiles_ref = bf16[384,128,128]{2,1,0:T(8,128)(2,1)S(1)} custom-call(bf16[384,128,128]{2,1,0:T(8,128)(2,1)} %bitcast.15), custom_call_target="tpu_custom_call" | custom-call | bytes 25165824 | tf_op jit(solution)/shard_map/pallas_call | solution.py:273
  12.9 0.0 copy-start.3
  12.9 0.0 copy-start.4
  13.0 0.2 shard_map.129
  13.2 0.0 collective-permute-done.3.x3_ref
  13.2 3.1 %shard_map.132 = bf16[8,64,128]{2,1,0:T(8,128)(2,1)S(1)} custom-call(s32[1,256]{1,0:T(1,128)S(1)} %get-tuple-element.10.slot_ref, bf16[32,512]{1,0:T(8,128)(2,1)S(1)} %shard_map.130.x0_ref, bf16[32,512]{1,0:T(8,128)(2,1)S(1)} %collective-permute-done.1.x1_ref, bf16[32,512]{1,0:T(8,128)(2,1)S(1)} %collective-permute-done.2.x2_ref, ...), custom_call_target="tpu_custom_call" | custom-call | tf_op jit(solution)/shard_map/pallas_call | solution.py:35
  16.3 16.0 %all_to_all.20.parts_ref = bf16[8,64,128]{2,1,0:T(8,128)(2,1)S(1)} all-to-all(bf16[8,64,128]{2,1,0:T(8,128)(2,1)S(1)} %shard_map.132), channel_id=1, replica_groups=mesh['row'=4,'col'=8,'x'=4,'core'=2] {'col'}, dimensions={0} | all-to-all | bytes 262144 | tf_op jit(solution)/shard_map/all_to_all | solution.py:304
  32.4 12.3 %all_to_all.21.all_ref = bf16[8,160,128]{2,1,0:T(8,128)(2,1)S(1)} all-to-all(bf16[8,160,128]{2,1,0:T(8,128)(2,1)S(1)} %shard_map.133), channel_id=1, replica_groups=mesh['row'=4,'col'=8,'x'=4,'core'=2] {'x','core'}, dimensions={0} | all-to-all | bytes 655360 | tf_op jit(solution)/shard_map/all_to_all | solution.py:307
  44.7 1.2 %shard_map.134 = bf16[4,80,128]{2,1,0:T(8,128)(2,1)S(1)} custom-call(bf16[8,160,128]{2,1,0:T(8,128)(2,1)S(1)} %all_to_all.21.all_ref, bf16[96,128]{1,0:T(8,128)(2,1)S(1)} %get-tuple-element.11.weights_ref.own_ref, s32[1,512]{1,0:T(1,128)S(1)} %bitcast.12, s32[1,512]{1,0:T(1,128)S(1)} %bitcast.13), custom_call_target="tpu_custom_call" | custom-call | tf_op jit(solution)/shard_map/pallas_call | solution.py:35
  45.9 9.0 %all_to_all.22.parts_ref = bf16[4,80,128]{2,1,0:T(8,128)(2,1)S(1)} all-to-all(bf16[4,80,128]{2,1,0:T(8,128)(2,1)S(1)} %shard_map.134), channel_id=1, replica_groups=mesh['row'=4,'col'=8,'x'=4,'core'=2] {'row'}, dimensions={0} | all-to-all | bytes 163840 | tf_op jit(solution)/shard_map/all_to_all | solution.py:317
  55.0 0.2 shard_map.135
  55.1 11.8 %all_to_all.23.parts_ref = bf16[8,80,128]{2,1,0:T(8,128)(2,1)S(1)} all-to-all(bf16[8,80,128]{2,1,0:T(8,128)(2,1)S(1)} %shard_map.135), channel_id=1, replica_groups=mesh['row'=4,'col'=8,'x'=4,'core'=2] {'col'}, dimensions={0} | all-to-all | bytes 327680 | tf_op jit(solution)/shard_map/all_to_all | solution.py:319
  66.9 0.8 %shard_map.136 = (f32[32,128]{1,0:T(8,128)}, f32[32,172]{1,0:T(8,128)}, f32[1,32]{1,0:T(1,128)}, f32[1,1]{1,0:T(1,128)}) custom-call(bf16[8,80,128]{2,1,0:T(8,128)(2,1)S(1)} %all_to_all.23.parts_ref), custom_call_target="tpu_custom_call" | custom-call | tf_op jit(solution)/shard_map/pallas_call | solution.py:35
  (12 shorter events, 0.1 us)
Async XLA Ops:
  0.6 1.5 %collective-permute-start = (bf16[16,512]{1,0:T(8,128)(2,1)}, bf16[16,512]{1,0:T(8,128)(2,1)S(1)}, u32[]{:S(2)}, u32[]{:S(2)}) collective-permute-start(bf16[16,512]{1,0:T(8,128)(2,1)} %bitcast.9), channel_id=1, source_target_pairs={{0,1},{1,0},{2,3},{3,2},{4,5},{5,4},{6,7},{7,6},{8,9},{9,8},{10,11... | collective-permute-start | bytes 49160 | tf_op jit(solution)/shard_map/ppermute | solution.py:266
  2.1 0.7 %copy-start.1 = (bf16[512,16]{0,1:T(8,128)(2,1)S(1)}, bf16[512,16]{0,1:T(8,128)(2,1)}, u32[]{:S(2)}) copy-start(bf16[512,16]{0,1:T(8,128)(2,1)} %param.10) | copy-start | bytes 49156
  2.8 10.3 %collective-permute-start.3 = (bf16[32,512]{1,0:T(8,128)(2,1)S(1)}, bf16[32,512]{1,0:T(8,128)(2,1)S(1)}, u32[]{:S(2)}, u32[]{:S(2)}) collective-permute-start(bf16[32,512]{1,0:T(8,128)(2,1)S(1)} %shard_map.130.x0_ref), channel_id=1, source_target_pairs={{0,192},{64,0},{128,64},{192,128},{1,193},{65,1},{129,65},{193,129... | collective-permute-start | bytes 98312 | tf_op jit(solution)/shard_map/ppermute | solution.py:269
  5.9 7.3 %collective-permute-start.2 = (bf16[32,512]{1,0:T(8,128)(2,1)S(1)}, bf16[32,512]{1,0:T(8,128)(2,1)S(1)}, u32[]{:S(2)}, u32[]{:S(2)}) collective-permute-start(bf16[32,512]{1,0:T(8,128)(2,1)S(1)} %shard_map.130.x0_ref), channel_id=1, source_target_pairs={{0,128},{64,192},{128,0},{192,64},{1,129},{65,193},{129,1},{193,65... | collective-permute-start | bytes 98312 | tf_op jit(solution)/shard_map/ppermute | solution.py:269
  6.5 6.7 %collective-permute-start.1 = (bf16[32,512]{1,0:T(8,128)(2,1)S(1)}, bf16[32,512]{1,0:T(8,128)(2,1)S(1)}, u32[]{:S(2)}, u32[]{:S(2)}) collective-permute-start(bf16[32,512]{1,0:T(8,128)(2,1)S(1)} %shard_map.130.x0_ref), channel_id=1, source_target_pairs={{0,64},{64,128},{128,192},{192,0},{1,65},{65,129},{129,193},{193,1... | collective-permute-start | bytes 98312 | tf_op jit(solution)/shard_map/ppermute | solution.py:269
  8.1 4.8 %copy-start = (bf16[32,172]{1,0:T(8,128)(2,1)S(1)}, bf16[32,172]{1,0:T(8,128)(2,1)}, u32[]{:S(2)}) copy-start(bf16[32,172]{1,0:T(8,128)(2,1)} %w2_ref.1) | copy-start | bytes 33028
  8.1 4.8 %copy-start.2 = (bf16[128,32]{0,1:T(8,128)(2,1)S(1)}, bf16[128,32]{0,1:T(8,128)(2,1)}, u32[]{:S(2)}) copy-start(bf16[128,32]{0,1:T(8,128)(2,1)} %param.11) | copy-start | bytes 24580
  8.1 4.8 %copy-start.5 = (s32[1,1,384]{2,1,0:T(1,128)S(1)}, s32[1,1,384]{2,1,0:T(1,128)}, u32[]{:S(2)}) copy-start(s32[1,1,384]{2,1,0:T(1,128)} %rows_ref.1) | copy-start | bytes 4612
  8.1 4.8 %copy-start.6 = (s32[1,1,384]{2,1,0:T(1,128)S(1)}, s32[1,1,384]{2,1,0:T(1,128)}, u32[]{:S(2)}) copy-start(s32[1,1,384]{2,1,0:T(1,128)} %cols_ref.1) | copy-start | bytes 4612
  8.2 4.8 %copy-start.7 = (f32[32]{0:T(128)S(1)}, f32[32]{0:T(128)}, u32[]{:S(2)}) copy-start(f32[32]{0:T(128)} %param.12) | copy-start | bytes 388
  12.9 31.8 %copy-start.3 = (s32[512]{0:T(512)S(1)}, s32[512]{0:T(512)}, u32[]{:S(2)}) copy-start(s32[512]{0:T(512)} %param.18) | copy-start | bytes 6148
  12.9 31.8 %copy-start.4 = (s32[512]{0:T(512)S(1)}, s32[512]{0:T(512)}, u32[]{:S(2)}) copy-start(s32[512]{0:T(512)} %param.19) | copy-start | bytes 6148

commit v3 on v2

--- a/solution.py
+++ b/solution.py
@@ -13,7 +13,7 @@
 HALF = TILE // 2
 GELU_SCALE = 0.7978845608028654
 GELU_CUBE = 0.044715
-COST = 60000000
+LOAD_UNROLL = 16
 F32 = jnp.float32
 BF16 = jnp.bfloat16
 IN_VMEM = pl.BlockSpec(memory_space=pltpu.VMEM)
@@ -42,6 +42,30 @@
         cost_estimate=cost,
     )(*placed)
 
+def load_kernel(place_ref, tiles_ref, after_ref, out_ref, sem):
+    del after_ref
+    slots = tiles_ref.shape[0]
+
+    def start(trip, started):
+        for part in range(LOAD_UNROLL):
+            slot = trip * LOAD_UNROLL + part
+            place = place_ref[0, slot]
+
+            @pl.when(place >= 0)
+            def _():
+                pltpu.make_async_copy(tiles_ref.at[slot], out_ref.at[place], sem).start()
+
+            started = started + (place >= 0).astype(jnp.int32)
+        return started
+
+    def finish(k, carry):
+        pltpu.make_async_copy(tiles_ref.at[0], out_ref.at[0], sem).wait()
+        return carry
+
+    started = lax.fori_loop(0, slots // LOAD_UNROLL, start, 0)
+    lax.fori_loop(0, started, finish, 0)
+
+
 def pair_kernel(x_ref, other_ref, out_ref):
     first = lax.axis_index("core") == 0
     mine, other = x_ref[...], other_ref[...]
@@ -50,41 +74,40 @@
     out_ref[feats:, :] = jnp.where(first, other, mine)
 
 
-def load_kernel(tiles_ref, out_ref, sems):
-    chunk = tiles_ref.shape[0] // sems.shape[0]
-    copies = []
-    for k in range(sems.shape[0]):
-        part = pl.ds(k * chunk, chunk)
-        copies.append(pltpu.make_async_copy(tiles_ref.at[part], out_ref.at[part], sems.at[k]))
+def setup_kernel(
+    live_ref, rows_in, cols_in, w1_in, w2_in, bias_in, x_in,
+    place_ref, used_ref, weights_ref, x_ref, rows_ref, cols_ref, w1_ref, w2_ref, bias_ref, sems,
+):
+    sources = (rows_in, cols_in, w1_in, w2_in, bias_in, x_in)
+    targets = (rows_ref, cols_ref, w1_ref, w2_ref, bias_ref, x_ref)
+    copies = [
+        pltpu.make_async_copy(source, target, sems.at[k])
+        for k, (source, target) in enumerate(zip(sources, targets))
+    ]
     for copy in copies:
         copy.start()
     for copy in copies:
         copy.wait()
-
-
-def setup_kernel(live_ref, rows_ref, cols_ref, w1_ref, w2_ref, bias_ref, slots_ref, weights_ref):
-    inverse(live_ref, rows_ref, cols_ref, slots_ref)
+    place_tiles(live_ref, rows_ref, cols_ref, place_ref, used_ref)
     pack_weights(w1_ref, w2_ref, bias_ref, weights_ref)
 
 
-def inverse(live_ref, rows_ref, cols_ref, out_ref):
-    places = out_ref.shape[1]
+def place_tiles(live_ref, rows_ref, cols_ref, place_ref, used_ref):
+    places = used_ref.shape[1]
     slots = rows_ref.shape[2]
     slot = lax.broadcasted_iota(jnp.int32, (1, slots), 1)
     rows = rows_ref[0]
     place = ((rows >> 2) * 2 + (rows & 1)) * (places // 16) + cols_ref[0]
     mine = (slot < live_ref[0, 0]) & (((rows >> 1) & 1) == lax.axis_index("core"))
     place = jnp.where(mine, place, -1)
+    place_ref[...] = place
     here = lax.broadcasted_iota(jnp.int32, (places, slots), 0) == place
     onehot = jnp.where(here, 1.0, 0.0).astype(BF16)
-    number = lax.broadcasted_iota(jnp.int32, (8, slots), 1) + 1
-    digit = lax.broadcasted_iota(jnp.int32, (8, slots), 0)
-    digits = jnp.where(digit == 0, number & 127, jnp.where(digit == 1, number >> 7, 0))
-    found = dot(digits.astype(F32).astype(BF16), onehot, ((1,), (1,)))
-    out_ref[...] = (found[0:1] + 128.0 * found[1:2]).astype(jnp.int32) - 1
-
-
-def aggregate_kernel(slot_ref, x0_ref, x1_ref, x2_ref, x3_ref, tiles_ref, out_ref, all_ref):
+    used = dot(jnp.ones((8, slots), BF16), onehot, ((1,), (1,)))
+    used_ref[...] = used[0:1].astype(jnp.int32)
+
+
+def aggregate_kernel(used_ref, x0_ref, x1_ref, x2_ref, x3_ref, tiles_ref, out_ref, all_ref):
     feats, nodes = x0_ref.shape
     row, n_row = lax.axis_index("row"), lax.axis_size("row")
     for k, part in enumerate((x0_ref, x1_ref, x2_ref, x3_ref)):
@@ -92,15 +115,15 @@
         all_ref[:, pl.ds(pl.multiple_of(source * nodes, TILE), nodes)] = part[...]
     x_all = all_ref[...]
     groups = out_ref.shape[0]
-    col_blocks = slot_ref.shape[1] // (2 * groups)
+    col_blocks = used_ref.shape[1] // (2 * groups)
     for group in range(groups):
         strips = []
         for block in (2 * group, 2 * group + 1):
             tiles = []
             for j in range(col_blocks):
-                slot = slot_ref[0, block * col_blocks + j]
-                tile = tiles_ref[jnp.maximum(slot, 0)]
-                tiles.append(jnp.where(slot >= 0, tile, jnp.zeros_like(tile)))
+                place = block * col_blocks + j
+                tile = tiles_ref[place]
+                tiles.append(jnp.where(used_ref[0, place] > 0, tile, jnp.zeros_like(tile)))
             strips.append(jnp.concatenate(tiles, 1))
         wide = dot(x_all, jnp.concatenate(strips, 0), ((1,), (1,))).astype(BF16)
         out_ref[group, :feats, :] = wide[:, :TILE]
@@ -128,9 +151,14 @@
 def total_kernel(parts_ref, weights_ref, out_ref):
     total = jnp.sum(parts_ref[...].astype(F32), axis=0).astype(BF16)
     rows = total.shape[0]
-    for k in range(out_ref.shape[0]):
-        out_ref[k, :rows, :] = total
-        out_ref[k, rows:, :] = weights_ref[...]
+    out_ref[:rows, :] = total
+    out_ref[rows:, :] = weights_ref[...]
+
+
+def stack_kernel(*refs):
+    for k, part in enumerate(refs[:-1]):
+        refs[-1][k] = part[...]
+
 
 def lanes16():
     return lax.broadcasted_iota(jnp.int32, (16, TILE), 1)
@@ -146,16 +174,24 @@
 def join_tail(tail):
     return jnp.where(is_fine(lanes16()), tail + pltpu.roll(tail, TILE - 2, 1), tail)
 
-def node_kernel(all_ref, own_ref, labels_ref, mask_ref, out_ref, y_ref):
-    groups = all_ref.shape[0]
-    for f in range(groups):
-        for b in range(2):
-            feat, node = 32 * (f // 2), TILE * (2 * (f % 2) + b)
-            y_ref[feat : feat + 32, node : node + TILE] = all_ref[f, 32 * b : 32 * b + 32, :]
+def node_kernel(mine_ref, other_ref, labels_ref, mask_ref, out_ref, y_ref):
+    n_x = mine_ref.shape[0]
+    x, core = lax.axis_index("x"), lax.axis_index("core")
+    for ref, owner in ((mine_ref, core), (other_ref, 1 - core)):
+        for k in range(n_x):
+            feat = pl.multiple_of(lax.rem(x + n_x - k, n_x) * 32, 32)
+            for b in range(2):
+                node = pl.multiple_of((2 * owner + b) * TILE, TILE)
+                y_ref[pl.ds(feat, 32), pl.ds(node, TILE)] = ref[k, 32 * b : 32 * b + 32, :]
     y = y_ref[...]
-    w1 = all_ref[:, 64:96, :].reshape(32 * groups, TILE)
-    w2a = all_ref[:, 96:128, :].reshape(32 * groups, TILE)
-    w2b = all_ref[:, 128:, :].reshape(32 * groups, TILE)
+
+    def both(begin):
+        rows = 32 * n_x
+        return jnp.concatenate(
+            [ref[:, begin : begin + 32, :].reshape(rows, TILE) for ref in (mine_ref, other_ref)], 0
+        )
+
+    w1, w2a, w2b = both(64), both(96), both(128)
 
     def bias_of(block):
         wide = block.astype(F32)
@@ -190,9 +226,9 @@
     grad_a = ((exp_a * inverse - hit_a.astype(F32)) * mask).astype(BF16)
     grad_b = ((exp_b * inverse - hit_b.astype(F32)) * mask).astype(BF16)
 
-    own_w1 = own_ref[:32, :]
-    own_w2a = own_ref[32:64, :]
-    own_w2b = own_ref[64:, :]
+    own_w1 = mine_ref[0, 64:96, :]
+    own_w2a = mine_ref[0, 96:128, :]
+    own_w2b = mine_ref[0, 128:, :]
     own_pre = dot(own_w1, y) + bias_of(own_w2b)
     squared, own_t = gelu_parts(own_pre)
     own_hidden = (0.5 * own_pre * (1.0 + own_t)).astype(BF16)
@@ -214,13 +250,14 @@
     tail = jnp.where(lane == REST + 1, extra, tail)
     tail = jnp.where(lane == HALF + REST, grad_b1[16:], tail)
     tail = split_tail(tail)
-    for k in range(out_ref.shape[0]):
-        out_ref[k, :32, :] = grad_w1
-        out_ref[k, 32:64, :] = grad_w2a
-        out_ref[k, 64:, :] = tail
-
-def middle_kernel(parts_ref, out_ref):
-    total = jnp.sum(parts_ref[...].astype(F32), axis=0)
+    out_ref[:32, :] = grad_w1
+    out_ref[32:64, :] = grad_w2a
+    out_ref[64:, :] = tail
+
+
+def middle_kernel(*refs):
+    out_ref = refs[-1]
+    total = sum(part[...].astype(F32) for part in refs[:-1])
     tail = split_tail(join_tail(total[64:]))
     for k in range(out_ref.shape[0]):
         out_ref[k, :64, :] = total[:64].astype(BF16)
@@ -241,6 +278,14 @@
     eye = lax.broadcasted_iota(jnp.int32, square, 0) == lax.broadcasted_iota(jnp.int32, square, 1)
     b1_ref[...] = jnp.sum(jnp.where(eye, column, 0.0), axis=0, keepdims=True) * inverse
     loss_ref[...] = tail[0:1, REST + 1 : REST + 2] * inverse
+
+def shifted(value, axis):
+    size = lax.axis_size(axis)
+    return [
+        lax.ppermute(value, axis, [(k, (k + step) % size) for k in range(size)])
+        for step in range(1, size)
+    ]
+
 
 def on_device(
     features,
@@ -264,37 +309,42 @@
 
     x_mine = features.T
     x_other = lax.ppermute(x_mine, "core", [(0, 1), (1, 0)])
+    tiles = pltpu.with_memory_space_constraint(
+        adj_tiles.reshape(adj_tiles.shape[2:]), pltpu.HBM
+    )
+    places = row_blocks // 2 * col_blocks
+    small = (tile_rows, tile_cols, weight_in.T, weight_out, bias.reshape(1, -1), x_mine)
+    place, used, weights, x_mine = pl.pallas_call(
+        setup_kernel,
+        out_shape=(
+            pltpu.VMEM((1, tiles.shape[0]), jnp.int32),
+            pltpu.VMEM((1, places), jnp.int32),
+            pltpu.VMEM((96, TILE), BF16),
+            pltpu.VMEM(x_mine.shape, BF16),
+        ),
+        in_specs=[IN_SMEM] + [pl.BlockSpec(memory_space=pltpu.HBM)] * 6,
+        out_specs=(IN_VMEM,) * 4,
+        scratch_shapes=[pltpu.VMEM(v.shape, v.dtype) for v in small[:5]]
+        + [pltpu.SemaphoreType.DMA((6,))],
+        compiler_params=pltpu.CompilerParams(vmem_limit_bytes=8 * 2**20),
+    )(tile_live, *(pltpu.with_memory_space_constraint(v, pltpu.HBM) for v in small))
     x_pair = call(pair_kernel, pltpu.VMEM((2 * feats, nodes), BF16), x_mine, x_other)
-    x_rows = [
-        lax.ppermute(x_pair, "row", [(r, (r + k) % n_row) for r in range(n_row)])
-        for k in range(1, n_row)
-    ]
-    tiles = adj_tiles.reshape(adj_tiles.shape[2:])
+    x_rows = shifted(x_pair, "row")
     loaded = pl.pallas_call(
         load_kernel,
-        out_shape=pltpu.VMEM(tiles.shape, BF16),
-        in_specs=[pl.BlockSpec(memory_space=pltpu.HBM)],
+        out_shape=pltpu.VMEM((places, TILE, TILE), BF16),
+        in_specs=[IN_SMEM, pl.BlockSpec(memory_space=pltpu.HBM), IN_VMEM],
         out_specs=IN_VMEM,
-        scratch_shapes=[pltpu.SemaphoreType.DMA((8,))],
+        scratch_shapes=[pltpu.SemaphoreType.DMA],
         compiler_params=pltpu.CompilerParams(vmem_limit_bytes=2**20),
         cost_estimate=pl.CostEstimate(
-            flops=0, bytes_accessed=4 * tiles.size, transcendentals=0
+            flops=0, bytes_accessed=2 * tiles.size, transcendentals=0
         ),
-    )(pltpu.with_memory_space_constraint(tiles, pltpu.HBM))
-    slots, weights = pl.pallas_call(
-        setup_kernel,
-        out_shape=(
-            pltpu.VMEM((1, row_blocks // 2 * col_blocks), jnp.int32),
-            pltpu.VMEM((96, TILE), BF16),
-        ),
-        in_specs=[IN_SMEM] + [IN_VMEM] * 5,
-        out_specs=(IN_VMEM, IN_VMEM),
-        compiler_params=pltpu.CompilerParams(vmem_limit_bytes=8 * 2**20),
-    )(tile_live, tile_rows, tile_cols, weight_in.T, weight_out, bias.reshape(1, -1))
+    )(place, tiles, pltpu.with_memory_space_constraint(x_pair, pltpu.VMEM))
     partial = call(
         aggregate_kernel,
         pltpu.VMEM((n_col, 4 * feats, TILE), BF16),
-        slots,
+        used,
         x_pair,
         *x_rows,
         loaded,
@@ -303,19 +353,25 @@
     )
     parts = lax.all_to_all(partial, "col", 0, 0)
     rows = parts.shape[1] + weights.shape[0]
-    message = call(total_kernel, pltpu.VMEM((n_feat, rows, TILE), BF16), parts, weights)
-    gathered = lax.all_to_all(message, ("x", "core"), 0, 0)
+    message = call(total_kernel, pltpu.VMEM((rows, TILE), BF16), parts, weights)
+    messages = (message, *shifted(message, "x"))
+    mine = call(stack_kernel, pltpu.VMEM((len(messages), rows, TILE), BF16), *messages)
+    other = lax.ppermute(mine, "core", [(0, 1), (1, 0)])
     grads = call(
         node_kernel,
-        pltpu.VMEM((n_row, grad_rows, TILE), BF16),
-        gathered,
-        weights,
+        pltpu.VMEM((grad_rows, TILE), BF16),
+        mine,
+        other,
         labels.reshape(1, -1),
         label_mask.reshape(1, -1),
         scratch=[pltpu.VMEM((feats * n_feat, nodes), BF16)],
     )
-    grads = lax.all_to_all(grads, "row", 0, 0)
-    grads = call(middle_kernel, pltpu.VMEM((n_col, grad_rows, TILE), BF16), grads)
+    grads = call(
+        middle_kernel,
+        pltpu.VMEM((n_col, grad_rows, TILE), BF16),
+        grads,
+        *shifted(grads, "row"),
+    )
     grads = lax.all_to_all(grads, "col", 0, 0)
     w1, w2, b1, loss = call(
         final_kernel,

time: 68.5 us -> 62.4 us (0.911)
  blocking collectives: 49.2 us -> 27.8 us
  waiting for transfers between devices: 1.39 us -> 11.9 us
  starting transfers between devices: 4.71 us -> 12.5 us
  Pallas kernels: 10.2 us -> 8.5 us
  local copies, waits for them, and re-layouts: 0.76 us -> 0.01 us
    all_to_all x2 -> x0, blocking collectives: 21.4 us -> none  [the longest x1 12.3 us: on_device(): gathered = lax.all_to_all(message, ('x', 'core'), 0, 0)]
    ppermute x3 -> x10, waiting for transfers between devices: 0.01 us -> 11.9 us  [the longest x9 10.5 us: shifted(): lax.ppermute(value, axis, [(k, (k + step) % size) for k in range(size)])]
    ppermute x3 -> x10, starting transfers between devices: 4.61 us -> 12.4 us  [the longest x9 12.3 us: shifted(): lax.ppermute(value, axis, [(k, (k + step) % size) for k in range(size)])]
    pallas_call x2, Pallas kernels: 4.92 us -> 3.16 us  [the longest x1 2.1 us: on_device(): pl.pallas_call(load_kernel, out_shape=pltpu.VMEM((places, TILE, TILE), BF...]
    ppermute x1, waiting for transfers between devices: 1.38 us -> 0.01 us  [on_device(): x_other = lax.ppermute(x_mine, 'core', [(0, 1), (1, 0)])]
    unnamed x16 -> x4, local copies, waits for them, and re-layouts: 0.76 us -> 0.01 us
    pallas_call x6 -> x7, Pallas kernels: 5.33 us -> 5.35 us  [call(): pl.pallas_call(kernel, out_shape=out_shape, in_specs=[IN_SMEM] * scalars...]
  transfers between devices with their start and end apart: 4 -> 11, of which waited for: 1 -> 8; matrix products, arithmetic and copies ran while one was open for 0% -> 0% of each run, Pallas kernels for 7% -> 5%
where the time goes in v3:
time: 62.4 us; the launch traced here: 62.1 us
  blocking collectives  27.8 us (45%)
  starting transfers between devices  12.5 us (20%)
  waiting for transfers between devices  11.9 us (19%)
  Pallas kernels  8.5 us (14%)
  between operations  1.35 us (2%)
    all_to_all x1, blocking collectives, on_device(): parts = lax.all_to_all(partial, 'col', 0, 0)  16 us
    ppermute x9, starting transfers between devices, shifted(): lax.ppermute(value, axis, [(k, (k + step) % size) for k in range(size)])  12.3 us
    all_to_all x1, blocking collectives, on_device(): grads = lax.all_to_all(grads, 'col', 0, 0)  11.8 us
    ppermute x9, waiting for transfers between devices, shifted(): lax.ppermute(value, axis, [(k, (k + step) % size) for k in range(size)])  10.5 us
    pallas_call x7, Pallas kernels, call(): pl.pallas_call(kernel, out_shape=out_shape, in_specs=[IN_SMEM] * scalars...  5.35 us
    pallas_call x1, Pallas kernels, on_device(): pl.pallas_call(load_kernel, out_shape=pltpu.VMEM((places, TILE, TILE), BF...  2.1 us
    ppermute x1, waiting for transfers between devices, on_device(): other = lax.ppermute(mine, 'core', [(0, 1), (1, 0)])  1.38 us
  transfers between devices with their start and end apart: 11, of which 8 were waited for; matrix products, arithmetic and copies ran while one was open for 0% of the time, Pallas kernels for 5%

profile of v3, /device:TPU:32, one launch (start us, length us, event | category | flops | bytes accessed | tf_op | source)
XLA Modules:
  0.0 62.1 jit_solution(3283038029685844921)
XLA Ops:
  1.4 1.1 %shard_map.129 = (s32[1,384]{1,0:T(1,128)S(1)}, s32[1,256]{1,0:T(1,128)S(1)}, bf16[96,128]{1,0:T(8,128)(2,1)S(1)}, bf16[16,512]{1,0:T(8,128)(2,1)S(1)}) custom-call(s32[1,1]{1,0:T(1,128)S(6)} %copy.14.live_ref, s32[1,1,384]{2,1,0:T(1,128)} %rows_in.1, s32[1,1,384]{2,1,0:T(1,128)} %cols_in.1, bf16[32,128]{1,0:T(8,128)(2,1)} %bitcast.14, ...), custom_call_target="tpu_custom_call" | custom-call | tf_op jit(solution)/shard_map/pallas_call | solution.py:317
  2.5 3.1 %collective-permute-start.3 = (bf16[32,512]{1,0:T(8,128)(2,1)S(1)}, bf16[32,512]{1,0:T(8,128)(2,1)S(1)}, u32[]{:S(2)}, u32[]{:S(2)}) collective-permute-start(bf16[32,512]{1,0:T(8,128)(2,1)S(1)} %shard_map.130.after_ref.x0_ref), channel_id=1, source_target_pairs={{0,192},{64,0},{128,64},{192,128},{1,193},{65,1},{129,65},{193,129... | collective-permute-start | bytes 98312 | tf_op jit(solution)/shard_map/ppermute | solution.py:285
  5.6 0.6 %collective-permute-start.2 = (bf16[32,512]{1,0:T(8,128)(2,1)S(1)}, bf16[32,512]{1,0:T(8,128)(2,1)S(1)}, u32[]{:S(2)}, u32[]{:S(2)}) collective-permute-start(bf16[32,512]{1,0:T(8,128)(2,1)S(1)} %shard_map.130.after_ref.x0_ref), channel_id=1, source_target_pairs={{0,128},{64,192},{128,0},{192,64},{1,129},{65,193},{129,1},{193,65... | collective-permute-start | bytes 98312 | tf_op jit(solution)/shard_map/ppermute | solution.py:285
  6.2 1.0 %collective-permute-start.1 = (bf16[32,512]{1,0:T(8,128)(2,1)S(1)}, bf16[32,512]{1,0:T(8,128)(2,1)S(1)}, u32[]{:S(2)}, u32[]{:S(2)}) collective-permute-start(bf16[32,512]{1,0:T(8,128)(2,1)S(1)} %shard_map.130.after_ref.x0_ref), channel_id=1, source_target_pairs={{0,64},{64,128},{128,192},{192,0},{1,65},{65,129},{129,193},{193,1... | collective-permute-start | bytes 98312 | tf_op jit(solution)/shard_map/ppermute | solution.py:285
  7.2 2.1 %shard_map.131.tiles_ref = bf16[256,128,128]{2,1,0:T(8,128)(2,1)S(1)} custom-call(s32[1,384]{1,0:T(1,128)S(1)} %get-tuple-element.14.place_ref, bf16[384,128,128]{2,1,0:T(8,128)(2,1)} %bitcast.11, bf16[32,512]{1,0:T(8,128)(2,1)S(1)} %shard_map.130.after_ref.x0_ref), custom_call_target="tpu_custom_call" | custom-call | bytes 12582912 | tf_op jit(solution)/shard_map/pallas_call | solution.py:333
  9.3 1.7 %collective-permute-done.2.x2_ref = bf16[32,512]{1,0:T(8,128)(2,1)S(1)} collective-permute-done((bf16[32,512]{1,0:T(8,128)(2,1)S(1)}, bf16[32,512]{1,0:T(8,128)(2,1)S(1)}, u32[]{:S(2)}, u32[]{:S(2)}) %collective-permute-start.2) | collective-permute-done | bytes 32800 | tf_op jit(solution)/shard_map/ppermute | solution.py:285
  11.0 0.4 collective-permute-done.1.x1_ref
  11.3 3.1 %shard_map.132 = bf16[8,64,128]{2,1,0:T(8,128)(2,1)S(1)} custom-call(s32[1,256]{1,0:T(1,128)S(1)} %get-tuple-element.12.used_ref, bf16[32,512]{1,0:T(8,128)(2,1)S(1)} %shard_map.130.after_ref.x0_ref, bf16[32,512]{1,0:T(8,128)(2,1)S(1)} %collective-permute-done.1.x1_ref, bf16[32,512]{1,0:T(8,128)(2,1)S(1)} %collective-permute-done.2.x2_ref, ...), custom_call_target="tpu_custom_call" | custom-call | tf_op jit(solution)/shard_map/pallas_call | solution.py:35
  14.5 16.0 %all_to_all.10.parts_ref = bf16[8,64,128]{2,1,0:T(8,128)(2,1)S(1)} all-to-all(bf16[8,64,128]{2,1,0:T(8,128)(2,1)S(1)} %shard_map.132), channel_id=1, replica_groups=mesh['row'=4,'col'=8,'x'=4,'core'=2] {'col'}, dimensions={0} | all-to-all | bytes 262144 | tf_op jit(solution)/shard_map/all_to_all | solution.py:354
  30.5 2.8 %collective-permute-start.6 = (bf16[160,128]{1,0:T(8,128)(2,1)S(1)}, bf16[160,128]{1,0:T(8,128)(2,1)S(1)}, u32[]{:S(2)}, u32[]{:S(2)}) collective-permute-start(bf16[160,128]{1,0:T(8,128)(2,1)S(1)} %shard_map.133.refs_0_), channel_id=1, source_target_pairs={{0,6},{2,0},{4,2},{6,4},{1,7},{3,1},{5,3},{7,5},{8,14},{10,8},{12,... | collective-permute-start | bytes 122888 | tf_op jit(solution)/shard_map/ppermute | solution.py:285
  33.3 0.8 %collective-permute-start.5 = (bf16[160,128]{1,0:T(8,128)(2,1)S(1)}, bf16[160,128]{1,0:T(8,128)(2,1)S(1)}, u32[]{:S(2)}, u32[]{:S(2)}) collective-permute-start(bf16[160,128]{1,0:T(8,128)(2,1)S(1)} %shard_map.133.refs_0_), channel_id=1, source_target_pairs={{0,4},{2,6},{4,0},{6,2},{1,5},{3,7},{5,1},{7,3},{8,12},{10,14},{12... | collective-permute-start | bytes 122888 | tf_op jit(solution)/shard_map/ppermute | solution.py:285
  34.1 0.9 %collective-permute-start.4 = (bf16[160,128]{1,0:T(8,128)(2,1)S(1)}, bf16[160,128]{1,0:T(8,128)(2,1)S(1)}, u32[]{:S(2)}, u32[]{:S(2)}) collective-permute-start(bf16[160,128]{1,0:T(8,128)(2,1)S(1)} %shard_map.133.refs_0_), channel_id=1, source_target_pairs={{0,2},{2,4},{4,6},{6,0},{1,3},{3,5},{5,7},{7,1},{8,10},{10,12},{12... | collective-permute-start | bytes 122888 | tf_op jit(solution)/shard_map/ppermute | solution.py:285
  35.0 3.8 %collective-permute-done.5.refs_2_ = bf16[160,128]{1,0:T(8,128)(2,1)S(1)} collective-permute-done((bf16[160,128]{1,0:T(8,128)(2,1)S(1)}, bf16[160,128]{1,0:T(8,128)(2,1)S(1)}, u32[]{:S(2)}, u32[]{:S(2)}) %collective-permute-start.5) | collective-permute-done | bytes 40992 | tf_op jit(solution)/shard_map/ppermute | solution.py:285
  38.8 0.5 collective-permute-done.4.refs_1_
  39.5 1.4 %collective-permute-done.7.other_ref = bf16[4,160,128]{2,1,0:T(8,128)(2,1)S(1)} collective-permute-done((bf16[4,160,128]{2,1,0:T(8,128)(2,1)S(1)}, bf16[4,160,128]{2,1,0:T(8,128)(2,1)S(1)}, u32[]{:S(2)}, u32[]{:S(2)}) %collective-permute-start.7) | collective-permute-done | bytes 163872 | tf_op jit(solution)/shard_map/ppermute | solution.py:359
  40.9 1.2 %shard_map.135.refs_0_ = bf16[80,128]{1,0:T(8,128)(2,1)S(1)} custom-call(bf16[4,160,128]{2,1,0:T(8,128)(2,1)S(1)} %shard_map.134.mine_ref, bf16[4,160,128]{2,1,0:T(8,128)(2,1)S(1)} %collective-permute-done.7.other_ref, s32[1,512]{1,0:T(1,128)S(1)} %bitcast.9, s32[1,512]{1,0:T(1,128)S(1)} %bitcast.10), custom_call_target="tpu_custom_call" | custom-call | tf_op jit(solution)/shard_map/pallas_call | solution.py:35
  42.1 0.6 collective-permute-start.10
  42.6 1.7 %collective-permute-start.9 = (bf16[80,128]{1,0:T(8,128)(2,1)S(1)}, bf16[80,128]{1,0:T(8,128)(2,1)S(1)}, u32[]{:S(2)}, u32[]{:S(2)}) collective-permute-start(bf16[80,128]{1,0:T(8,128)(2,1)S(1)} %shard_map.135.refs_0_), channel_id=1, source_target_pairs={{0,128},{64,192},{128,0},{192,64},{1,129},{65,193},{129,1},{193,65... | collective-permute-start | bytes 61448 | tf_op jit(solution)/shard_map/ppermute | solution.py:285
  44.3 0.8 %collective-permute-start.8 = (bf16[80,128]{1,0:T(8,128)(2,1)S(1)}, bf16[80,128]{1,0:T(8,128)(2,1)S(1)}, u32[]{:S(2)}, u32[]{:S(2)}) collective-permute-start(bf16[80,128]{1,0:T(8,128)(2,1)S(1)} %shard_map.135.refs_0_), channel_id=1, source_target_pairs={{0,64},{64,128},{128,192},{192,0},{1,65},{65,129},{129,193},{193,1... | collective-permute-start | bytes 61448 | tf_op jit(solution)/shard_map/ppermute | solution.py:285
  45.2 0.9 %collective-permute-done.10.refs_3_ = bf16[80,128]{1,0:T(8,128)(2,1)S(1)} collective-permute-done((bf16[80,128]{1,0:T(8,128)(2,1)S(1)}, bf16[80,128]{1,0:T(8,128)(2,1)S(1)}, u32[]{:S(2)}, u32[]{:S(2)}) %collective-permute-start.10) | collective-permute-done | bytes 20512 | tf_op jit(solution)/shard_map/ppermute | solution.py:285
  46.0 1.9 %collective-permute-done.9.refs_2_ = bf16[80,128]{1,0:T(8,128)(2,1)S(1)} collective-permute-done((bf16[80,128]{1,0:T(8,128)(2,1)S(1)}, bf16[80,128]{1,0:T(8,128)(2,1)S(1)}, u32[]{:S(2)}, u32[]{:S(2)}) %collective-permute-start.9) | collective-permute-done | bytes 20512 | tf_op jit(solution)/shard_map/ppermute | solution.py:285
  47.9 1.4 %collective-permute-done.8.refs_1_ = bf16[80,128]{1,0:T(8,128)(2,1)S(1)} collective-permute-done((bf16[80,128]{1,0:T(8,128)(2,1)S(1)}, bf16[80,128]{1,0:T(8,128)(2,1)S(1)}, u32[]{:S(2)}, u32[]{:S(2)}) %collective-permute-start.8) | collective-permute-done | bytes 20512 | tf_op jit(solution)/shard_map/ppermute | solution.py:285
  49.5 11.8 %all_to_all.11.parts_ref = bf16[8,80,128]{2,1,0:T(8,128)(2,1)S(1)} all-to-all(bf16[8,80,128]{2,1,0:T(8,128)(2,1)S(1)} %shard_map.136), channel_id=1, replica_groups=mesh['row'=4,'col'=8,'x'=4,'core'=2] {'col'}, dimensions={0} | all-to-all | bytes 327680 | tf_op jit(solution)/shard_map/all_to_all | solution.py:375
  61.3 0.8 %shard_map.137 = (f32[32,128]{1,0:T(8,128)}, f32[32,172]{1,0:T(8,128)}, f32[1,32]{1,0:T(1,128)}, f32[1,1]{1,0:T(1,128)}) custom-call(bf16[8,80,128]{2,1,0:T(8,128)(2,1)S(1)} %all_to_all.11.parts_ref), custom_call_target="tpu_custom_call" | custom-call | tf_op jit(solution)/shard_map/pallas_call | solution.py:35
  (13 shorter events, 0.4 us)
Async XLA Ops:
  0.6 1.8 %collective-permute-start = (bf16[16,512]{1,0:T(8,128)(2,1)}, bf16[16,512]{1,0:T(8,128)(2,1)S(1)}, u32[]{:S(2)}, u32[]{:S(2)}) collective-permute-start(bf16[16,512]{1,0:T(8,128)(2,1)} %bitcast.12), channel_id=1, source_target_pairs={{0,1},{1,0},{2,3},{3,2},{4,5},{5,4},{6,7},{7,6},{8,9},{9,8},{10,11... | collective-permute-start | bytes 49160 | tf_op jit(solution)/shard_map/ppermute | solution.py:311
  2.5 6.8 %collective-permute-start.3 = (bf16[32,512]{1,0:T(8,128)(2,1)S(1)}, bf16[32,512]{1,0:T(8,128)(2,1)S(1)}, u32[]{:S(2)}, u32[]{:S(2)}) collective-permute-start(bf16[32,512]{1,0:T(8,128)(2,1)S(1)} %shard_map.130.after_ref.x0_ref), channel_id=1, source_target_pairs={{0,192},{64,0},{128,64},{192,128},{1,193},{65,1},{129,65},{193,129... | collective-permute-start | bytes 98312 | tf_op jit(solution)/shard_map/ppermute | solution.py:285
  5.6 5.4 %collective-permute-start.2 = (bf16[32,512]{1,0:T(8,128)(2,1)S(1)}, bf16[32,512]{1,0:T(8,128)(2,1)S(1)}, u32[]{:S(2)}, u32[]{:S(2)}) collective-permute-start(bf16[32,512]{1,0:T(8,128)(2,1)S(1)} %shard_map.130.after_ref.x0_ref), channel_id=1, source_target_pairs={{0,128},{64,192},{128,0},{192,64},{1,129},{65,193},{129,1},{193,65... | collective-permute-start | bytes 98312 | tf_op jit(solution)/shard_map/ppermute | solution.py:285
  6.2 5.1 %collective-permute-start.1 = (bf16[32,512]{1,0:T(8,128)(2,1)S(1)}, bf16[32,512]{1,0:T(8,128)(2,1)S(1)}, u32[]{:S(2)}, u32[]{:S(2)}) collective-permute-start(bf16[32,512]{1,0:T(8,128)(2,1)S(1)} %shard_map.130.after_ref.x0_ref), channel_id=1, source_target_pairs={{0,64},{64,128},{128,192},{192,0},{1,65},{65,129},{129,193},{193,1... | collective-permute-start | bytes 98312 | tf_op jit(solution)/shard_map/ppermute | solution.py:285
  7.2 33.7 %copy-start = (s32[512]{0:T(512)S(1)}, s32[512]{0:T(512)}, u32[]{:S(2)}) copy-start(s32[512]{0:T(512)} %param.18) | copy-start | bytes 6148
  7.2 33.7 %copy-start.1 = (s32[512]{0:T(512)S(1)}, s32[512]{0:T(512)}, u32[]{:S(2)}) copy-start(s32[512]{0:T(512)} %param.19) | copy-start | bytes 6148
  30.5 4.5 %collective-permute-start.6 = (bf16[160,128]{1,0:T(8,128)(2,1)S(1)}, bf16[160,128]{1,0:T(8,128)(2,1)S(1)}, u32[]{:S(2)}, u32[]{:S(2)}) collective-permute-start(bf16[160,128]{1,0:T(8,128)(2,1)S(1)} %shard_map.133.refs_0_), channel_id=1, source_target_pairs={{0,6},{2,0},{4,2},{6,4},{1,7},{3,1},{5,3},{7,5},{8,14},{10,8},{12,... | collective-permute-start | bytes 122888 | tf_op jit(solution)/shard_map/ppermute | solution.py:285
  33.3 5.5 %collective-permute-start.5 = (bf16[160,128]{1,0:T(8,128)(2,1)S(1)}, bf16[160,128]{1,0:T(8,128)(2,1)S(1)}, u32[]{:S(2)}, u32[]{:S(2)}) collective-permute-start(bf16[160,128]{1,0:T(8,128)(2,1)S(1)} %shard_map.133.refs_0_), channel_id=1, source_target_pairs={{0,4},{2,6},{4,0},{6,2},{1,5},{3,7},{5,1},{7,3},{8,12},{10,14},{12... | collective-permute-start | bytes 122888 | tf_op jit(solution)/shard_map/ppermute | solution.py:285
  34.1 5.2 %collective-permute-start.4 = (bf16[160,128]{1,0:T(8,128)(2,1)S(1)}, bf16[160,128]{1,0:T(8,128)(2,1)S(1)}, u32[]{:S(2)}, u32[]{:S(2)}) collective-permute-start(bf16[160,128]{1,0:T(8,128)(2,1)S(1)} %shard_map.133.refs_0_), channel_id=1, source_target_pairs={{0,2},{2,4},{4,6},{6,0},{1,3},{3,5},{5,7},{7,1},{8,10},{10,12},{12... | collective-permute-start | bytes 122888 | tf_op jit(solution)/shard_map/ppermute | solution.py:285
  39.4 1.5 %collective-permute-start.7 = (bf16[4,160,128]{2,1,0:T(8,128)(2,1)S(1)}, bf16[4,160,128]{2,1,0:T(8,128)(2,1)S(1)}, u32[]{:S(2)}, u32[]{:S(2)}) collective-permute-start(bf16[4,160,128]{2,1,0:T(8,128)(2,1)S(1)} %shard_map.134.mine_ref), channel_id=1, source_target_pairs={{0,1},{1,0},{2,3},{3,2},{4,5},{5,4},{6,7},{7,6},{8,9},{9,8},{10,11... | collective-permute-start | bytes 491528 | tf_op jit(solution)/shard_map/ppermute | solution.py:359
  42.1 4.0 %collective-permute-start.10 = (bf16[80,128]{1,0:T(8,128)(2,1)S(1)}, bf16[80,128]{1,0:T(8,128)(2,1)S(1)}, u32[]{:S(2)}, u32[]{:S(2)}) collective-permute-start(bf16[80,128]{1,0:T(8,128)(2,1)S(1)} %shard_map.135.refs_0_), channel_id=1, source_target_pairs={{0,192},{64,0},{128,64},{192,128},{1,193},{65,1},{129,65},{193,129... | collective-permute-start | bytes 61448 | tf_op jit(solution)/shard_map/ppermute | solution.py:285
  42.6 5.3 %collective-permute-start.9 = (bf16[80,128]{1,0:T(8,128)(2,1)S(1)}, bf16[80,128]{1,0:T(8,128)(2,1)S(1)}, u32[]{:S(2)}, u32[]{:S(2)}) collective-permute-start(bf16[80,128]{1,0:T(8,128)(2,1)S(1)} %shard_map.135.refs_0_), channel_id=1, source_target_pairs={{0,128},{64,192},{128,0},{192,64},{1,129},{65,193},{129,1},{193,65... | collective-permute-start | bytes 61448 | tf_op jit(solution)/shard_map/ppermute | solution.py:285
  44.3 5.0 %collective-permute-start.8 = (bf16[80,128]{1,0:T(8,128)(2,1)S(1)}, bf16[80,128]{1,0:T(8,128)(2,1)S(1)}, u32[]{:S(2)}, u32[]{:S(2)}) collective-permute-start(bf16[80,128]{1,0:T(8,128)(2,1)S(1)} %shard_map.135.refs_0_), channel_id=1, source_target_pairs={{0,64},{64,128},{128,192},{192,0},{1,65},{65,129},{129,193},{193,1... | collective-permute-start | bytes 61448 | tf_op jit(solution)/shard_map/ppermute | solution.py:285

commit v4 on v3

--- a/solution.py
+++ b/solution.py
@@ -14,6 +14,7 @@
 GELU_SCALE = 0.7978845608028654
 GELU_CUBE = 0.044715
 LOAD_UNROLL = 16
+ORDER = (1, 3, 2)
 F32 = jnp.float32
 BF16 = jnp.bfloat16
 IN_VMEM = pl.BlockSpec(memory_space=pltpu.VMEM)
@@ -110,8 +111,8 @@
 def aggregate_kernel(used_ref, x0_ref, x1_ref, x2_ref, x3_ref, tiles_ref, out_ref, all_ref):
     feats, nodes = x0_ref.shape
     row, n_row = lax.axis_index("row"), lax.axis_size("row")
-    for k, part in enumerate((x0_ref, x1_ref, x2_ref, x3_ref)):
-        source = lax.rem(row + n_row - k, n_row)
+    for k, part in zip((0, *ORDER), (x0_ref, x1_ref, x2_ref, x3_ref)):
+        source = row ^ k
         all_ref[:, pl.ds(pl.multiple_of(source * nodes, TILE), nodes)] = part[...]
     x_all = all_ref[...]
     groups = out_ref.shape[0]
@@ -125,7 +126,7 @@
                 tile = tiles_ref[place]
                 tiles.append(jnp.where(used_ref[0, place] > 0, tile, jnp.zeros_like(tile)))
             strips.append(jnp.concatenate(tiles, 1))
-        wide = dot(x_all, jnp.concatenate(strips, 0), ((1,), (1,))).astype(BF16)
+        wide = dot(jnp.concatenate(strips, 0), x_all, ((1,), (1,))).T.astype(BF16)
         out_ref[group, :feats, :] = wide[:, :TILE]
         out_ref[group, feats:, :] = wide[:, TILE:]
 
@@ -156,7 +157,7 @@
 
 
 def stack_kernel(*refs):
-    for k, part in enumerate(refs[:-1]):
+    for k, part in zip((0, *ORDER), refs[:-1]):
         refs[-1][k] = part[...]
 
 
@@ -179,7 +180,7 @@
     x, core = lax.axis_index("x"), lax.axis_index("core")
     for ref, owner in ((mine_ref, core), (other_ref, 1 - core)):
         for k in range(n_x):
-            feat = pl.multiple_of(lax.rem(x + n_x - k, n_x) * 32, 32)
+            feat = pl.multiple_of((x ^ k) * 32, 32)
             for b in range(2):
                 node = pl.multiple_of((2 * owner + b) * TILE, TILE)
                 y_ref[pl.ds(feat, 32), pl.ds(node, TILE)] = ref[k, 32 * b : 32 * b + 32, :]
@@ -279,11 +280,11 @@
     b1_ref[...] = jnp.sum(jnp.where(eye, column, 0.0), axis=0, keepdims=True) * inverse
     loss_ref[...] = tail[0:1, REST + 1 : REST + 2] * inverse
 
-def shifted(value, axis):
+def exchanged(value, axis):
     size = lax.axis_size(axis)
     return [
-        lax.ppermute(value, axis, [(k, (k + step) % size) for k in range(size)])
-        for step in range(1, size)
+        lax.ppermute(value, axis, [(k, k ^ step) for k in range(size)])
+        for step in ORDER
     ]
 
 
@@ -329,7 +330,7 @@
         compiler_params=pltpu.CompilerParams(vmem_limit_bytes=8 * 2**20),
     )(tile_live, *(pltpu.with_memory_space_constraint(v, pltpu.HBM) for v in small))
     x_pair = call(pair_kernel, pltpu.VMEM((2 * feats, nodes), BF16), x_mine, x_other)
-    x_rows = shifted(x_pair, "row")
+    x_rows = exchanged(x_pair, "row")
     loaded = pl.pallas_call(
         load_kernel,
         out_shape=pltpu.VMEM((places, TILE, TILE), BF16),
@@ -354,7 +355,7 @@
     parts = lax.all_to_all(partial, "col", 0, 0)
     rows = parts.shape[1] + weights.shape[0]
     message = call(total_kernel, pltpu.VMEM((rows, TILE), BF16), parts, weights)
-    messages = (message, *shifted(message, "x"))
+    messages = (message, *exchanged(message, "x"))
     mine = call(stack_kernel, pltpu.VMEM((len(messages), rows, TILE), BF16), *messages)
     other = lax.ppermute(mine, "core", [(0, 1), (1, 0)])
     grads = call(
@@ -370,7 +371,7 @@
         middle_kernel,
         pltpu.VMEM((n_col, grad_rows, TILE), BF16),
         grads,
-        *shifted(grads, "row"),
+        *exchanged(grads, "row"),
     )
     grads = lax.all_to_all(grads, "col", 0, 0)
     w1, w2, b1, loss = call(

time: 62.4 us -> 61.4 us (0.984); the launches traced: 62.1 us -> 60.4 us
  waiting for transfers between devices: 11.9 us -> 10.7 us
    ppermute x9, waiting for transfers between devices: 10.5 us -> 9.27 us  [exchanged(): lax.ppermute(value, axis, [(k, k ^ step) for k in range(size)])]
  transfers between devices with their start and end apart: 11 -> 11, of which waited for: 8 -> 6; matrix products, arithmetic and copies ran while one was open for 0% -> 0% of each run, Pallas kernels for 5% -> 5%
where the time goes in v4:
time: 61.4 us; the launch traced here: 60.4 us
  blocking collectives  27.8 us (45%)
  starting transfers between devices  12.3 us (20%)
  waiting for transfers between devices  10.7 us (17%)
  Pallas kernels  8.27 us (13%)
  between operations  1.35 us (2%)
    all_to_all x1, blocking collectives, on_device(): parts = lax.all_to_all(partial, 'col', 0, 0)  16 us
    ppermute x9, starting transfers between devices, exchanged(): lax.ppermute(value, axis, [(k, k ^ step) for k in range(size)])  12.1 us
    all_to_all x1, blocking collectives, on_device(): grads = lax.all_to_all(grads, 'col', 0, 0)  11.8 us
    ppermute x9, waiting for transfers between devices, exchanged(): lax.ppermute(value, axis, [(k, k ^ step) for k in range(size)])  9.27 us
    pallas_call x7, Pallas kernels, call(): pl.pallas_call(kernel, out_shape=out_shape, in_specs=[IN_SMEM] * scalars...  5.12 us
    pallas_call x1, Pallas kernels, on_device(): pl.pallas_call(load_kernel, out_shape=pltpu.VMEM((places, TILE, TILE), BF...  2.1 us
    ppermute x1, waiting for transfers between devices, on_device(): other = lax.ppermute(mine, 'core', [(0, 1), (1, 0)])  1.38 us
  transfers between devices with their start and end apart: 11, of which 6 were waited for; matrix products, arithmetic and copies ran while one was open for 0% of the time, Pallas kernels for 5%

profile of v4, /device:TPU:32, one launch (start us, length us, event | category | flops | bytes accessed | tf_op | source)
XLA Modules:
  0.0 60.4 jit_solution(360636892902570876)
XLA Ops:
  0.6 0.1 collective-permute-start
  1.4 1.1 %shard_map.129 = (s32[1,384]{1,0:T(1,128)S(1)}, s32[1,256]{1,0:T(1,128)S(1)}, bf16[96,128]{1,0:T(8,128)(2,1)S(1)}, bf16[16,512]{1,0:T(8,128)(2,1)S(1)}) custom-call(s32[1,1]{1,0:T(1,128)S(6)} %copy.14.live_ref, s32[1,1,384]{2,1,0:T(1,128)} %rows_in.1, s32[1,1,384]{2,1,0:T(1,128)} %cols_in.1, bf16[32,128]{1,0:T(8,128)(2,1)} %bitcast.14, ...), custom_call_target="tpu_custom_call" | custom-call | tf_op jit(solution)/shard_map/pallas_call | solution.py:318
  2.5 3.3 %collective-permute-start.3 = (bf16[32,512]{1,0:T(8,128)(2,1)S(1)}, bf16[32,512]{1,0:T(8,128)(2,1)S(1)}, u32[]{:S(2)}, u32[]{:S(2)}) collective-permute-start(bf16[32,512]{1,0:T(8,128)(2,1)S(1)} %shard_map.130.after_ref.x0_ref), channel_id=1, source_target_pairs={{0,128},{64,192},{128,0},{192,64},{1,129},{65,193},{129,1},{193,65... | collective-permute-start | bytes 98312 | tf_op jit(solution)/shard_map/ppermute | solution.py:286
  5.8 1.1 %collective-permute-start.2 = (bf16[32,512]{1,0:T(8,128)(2,1)S(1)}, bf16[32,512]{1,0:T(8,128)(2,1)S(1)}, u32[]{:S(2)}, u32[]{:S(2)}) collective-permute-start(bf16[32,512]{1,0:T(8,128)(2,1)S(1)} %shard_map.130.after_ref.x0_ref), channel_id=1, source_target_pairs={{0,192},{64,128},{128,64},{192,0},{1,193},{65,129},{129,65},{193,1... | collective-permute-start | bytes 98312 | tf_op jit(solution)/shard_map/ppermute | solution.py:286
  6.8 2.1 %shard_map.131.tiles_ref = bf16[256,128,128]{2,1,0:T(8,128)(2,1)S(1)} custom-call(s32[1,384]{1,0:T(1,128)S(1)} %get-tuple-element.14.place_ref, bf16[384,128,128]{2,1,0:T(8,128)(2,1)} %bitcast.11, bf16[32,512]{1,0:T(8,128)(2,1)S(1)} %shard_map.130.after_ref.x0_ref), custom_call_target="tpu_custom_call" | custom-call | bytes 12582912 | tf_op jit(solution)/shard_map/pallas_call | solution.py:334
  8.9 1.9 %collective-permute-done.2.x2_ref = bf16[32,512]{1,0:T(8,128)(2,1)S(1)} collective-permute-done((bf16[32,512]{1,0:T(8,128)(2,1)S(1)}, bf16[32,512]{1,0:T(8,128)(2,1)S(1)}, u32[]{:S(2)}, u32[]{:S(2)}) %collective-permute-start.2) | collective-permute-done | bytes 32800 | tf_op jit(solution)/shard_map/ppermute | solution.py:286
  10.9 2.9 %shard_map.132 = bf16[8,64,128]{2,1,0:T(8,128)(2,1)S(1)} custom-call(s32[1,256]{1,0:T(1,128)S(1)} %get-tuple-element.12.used_ref, bf16[32,512]{1,0:T(8,128)(2,1)S(1)} %shard_map.130.after_ref.x0_ref, bf16[32,512]{1,0:T(8,128)(2,1)S(1)} %collective-permute-done.1.x1_ref, bf16[32,512]{1,0:T(8,128)(2,1)S(1)} %collective-permute-done.2.x2_ref, ...), custom_call_target="tpu_custom_call" | custom-call | tf_op jit(solution)/shard_map/pallas_call | solution.py:36
  13.8 16.0 %all_to_all.10.parts_ref = bf16[8,64,128]{2,1,0:T(8,128)(2,1)S(1)} all-to-all(bf16[8,64,128]{2,1,0:T(8,128)(2,1)S(1)} %shard_map.132), channel_id=1, replica_groups=mesh['row'=4,'col'=8,'x'=4,'core'=2] {'col'}, dimensions={0} | all-to-all | bytes 262144 | tf_op jit(solution)/shard_map/all_to_all | solution.py:355
  29.8 3.1 %collective-permute-start.6 = (bf16[160,128]{1,0:T(8,128)(2,1)S(1)}, bf16[160,128]{1,0:T(8,128)(2,1)S(1)}, u32[]{:S(2)}, u32[]{:S(2)}) collective-permute-start(bf16[160,128]{1,0:T(8,128)(2,1)S(1)} %shard_map.133.refs_0_), channel_id=1, source_target_pairs={{0,4},{2,6},{4,0},{6,2},{1,5},{3,7},{5,1},{7,3},{8,12},{10,14},{12... | collective-permute-start | bytes 122888 | tf_op jit(solution)/shard_map/ppermute | solution.py:286
  32.9 1.1 %collective-permute-start.5 = (bf16[160,128]{1,0:T(8,128)(2,1)S(1)}, bf16[160,128]{1,0:T(8,128)(2,1)S(1)}, u32[]{:S(2)}, u32[]{:S(2)}) collective-permute-start(bf16[160,128]{1,0:T(8,128)(2,1)S(1)} %shard_map.133.refs_0_), channel_id=1, source_target_pairs={{0,6},{2,4},{4,2},{6,0},{1,7},{3,5},{5,3},{7,1},{8,14},{10,12},{12... | collective-permute-start | bytes 122888 | tf_op jit(solution)/shard_map/ppermute | solution.py:286
  34.1 1.5 %collective-permute-done.6.refs_3_ = bf16[160,128]{1,0:T(8,128)(2,1)S(1)} collective-permute-done((bf16[160,128]{1,0:T(8,128)(2,1)S(1)}, bf16[160,128]{1,0:T(8,128)(2,1)S(1)}, u32[]{:S(2)}, u32[]{:S(2)}) %collective-permute-start.6) | collective-permute-done | bytes 40992 | tf_op jit(solution)/shard_map/ppermute | solution.py:286
  35.5 2.6 %collective-permute-done.5.refs_2_ = bf16[160,128]{1,0:T(8,128)(2,1)S(1)} collective-permute-done((bf16[160,128]{1,0:T(8,128)(2,1)S(1)}, bf16[160,128]{1,0:T(8,128)(2,1)S(1)}, u32[]{:S(2)}, u32[]{:S(2)}) %collective-permute-start.5) | collective-permute-done | bytes 40992 | tf_op jit(solution)/shard_map/ppermute | solution.py:286
  38.2 0.1 collective-permute-start.7
  38.3 1.4 %collective-permute-done.7.other_ref = bf16[4,160,128]{2,1,0:T(8,128)(2,1)S(1)} collective-permute-done((bf16[4,160,128]{2,1,0:T(8,128)(2,1)S(1)}, bf16[4,160,128]{2,1,0:T(8,128)(2,1)S(1)}, u32[]{:S(2)}, u32[]{:S(2)}) %collective-permute-start.7) | collective-permute-done | bytes 163872 | tf_op jit(solution)/shard_map/ppermute | solution.py:360
  39.6 1.2 %shard_map.135.refs_0_ = bf16[80,128]{1,0:T(8,128)(2,1)S(1)} custom-call(bf16[4,160,128]{2,1,0:T(8,128)(2,1)S(1)} %shard_map.134.mine_ref, bf16[4,160,128]{2,1,0:T(8,128)(2,1)S(1)} %collective-permute-done.7.other_ref, s32[1,512]{1,0:T(1,128)S(1)} %bitcast.9, s32[1,512]{1,0:T(1,128)S(1)} %bitcast.10), custom_call_target="tpu_custom_call" | custom-call | tf_op jit(solution)/shard_map/pallas_call | solution.py:36
  40.8 1.7 %collective-permute-start.10 = (bf16[80,128]{1,0:T(8,128)(2,1)S(1)}, bf16[80,128]{1,0:T(8,128)(2,1)S(1)}, u32[]{:S(2)}, u32[]{:S(2)}) collective-permute-start(bf16[80,128]{1,0:T(8,128)(2,1)S(1)} %shard_map.135.refs_0_), channel_id=1, source_target_pairs={{0,128},{64,192},{128,0},{192,64},{1,129},{65,193},{129,1},{193,65... | collective-permute-start | bytes 61448 | tf_op jit(solution)/shard_map/ppermute | solution.py:286
  42.6 1.2 %collective-permute-start.9 = (bf16[80,128]{1,0:T(8,128)(2,1)S(1)}, bf16[80,128]{1,0:T(8,128)(2,1)S(1)}, u32[]{:S(2)}, u32[]{:S(2)}) collective-permute-start(bf16[80,128]{1,0:T(8,128)(2,1)S(1)} %shard_map.135.refs_0_), channel_id=1, source_target_pairs={{0,192},{64,128},{128,64},{192,0},{1,193},{65,129},{129,65},{193,1... | collective-permute-start | bytes 61448 | tf_op jit(solution)/shard_map/ppermute | solution.py:286
  43.8 0.5 collective-permute-start.8
  44.3 1.8 %collective-permute-done.10.refs_3_ = bf16[80,128]{1,0:T(8,128)(2,1)S(1)} collective-permute-done((bf16[80,128]{1,0:T(8,128)(2,1)S(1)}, bf16[80,128]{1,0:T(8,128)(2,1)S(1)}, u32[]{:S(2)}, u32[]{:S(2)}) %collective-permute-start.10) | collective-permute-done | bytes 20512 | tf_op jit(solution)/shard_map/ppermute | solution.py:286
  46.1 1.4 %collective-permute-done.9.refs_2_ = bf16[80,128]{1,0:T(8,128)(2,1)S(1)} collective-permute-done((bf16[80,128]{1,0:T(8,128)(2,1)S(1)}, bf16[80,128]{1,0:T(8,128)(2,1)S(1)}, u32[]{:S(2)}, u32[]{:S(2)}) %collective-permute-start.9) | collective-permute-done | bytes 20512 | tf_op jit(solution)/shard_map/ppermute | solution.py:286
  47.5 0.0 collective-permute-done.8.refs_1_
  47.6 0.2 shard_map.136
  47.7 11.8 %all_to_all.11.parts_ref = bf16[8,80,128]{2,1,0:T(8,128)(2,1)S(1)} all-to-all(bf16[8,80,128]{2,1,0:T(8,128)(2,1)S(1)} %shard_map.136), channel_id=1, replica_groups=mesh['row'=4,'col'=8,'x'=4,'core'=2] {'col'}, dimensions={0} | all-to-all | bytes 327680 | tf_op jit(solution)/shard_map/all_to_all | solution.py:376
  59.6 0.8 %shard_map.137 = (f32[32,128]{1,0:T(8,128)}, f32[32,172]{1,0:T(8,128)}, f32[1,32]{1,0:T(1,128)}, f32[1,1]{1,0:T(1,128)}) custom-call(bf16[8,80,128]{2,1,0:T(8,128)(2,1)S(1)} %all_to_all.11.parts_ref), custom_call_target="tpu_custom_call" | custom-call | tf_op jit(solution)/shard_map/pallas_call | solution.py:36
  (13 shorter events, 0.1 us)
Async XLA Ops:
  0.6 1.8 %collective-permute-start = (bf16[16,512]{1,0:T(8,128)(2,1)}, bf16[16,512]{1,0:T(8,128)(2,1)S(1)}, u32[]{:S(2)}, u32[]{:S(2)}) collective-permute-start(bf16[16,512]{1,0:T(8,128)(2,1)} %bitcast.12), channel_id=1, source_target_pairs={{0,1},{1,0},{2,3},{3,2},{4,5},{5,4},{6,7},{7,6},{8,9},{9,8},{10,11... | collective-permute-start | bytes 49160 | tf_op jit(solution)/shard_map/ppermute | solution.py:312
  2.5 6.5 %collective-permute-start.3 = (bf16[32,512]{1,0:T(8,128)(2,1)S(1)}, bf16[32,512]{1,0:T(8,128)(2,1)S(1)}, u32[]{:S(2)}, u32[]{:S(2)}) collective-permute-start(bf16[32,512]{1,0:T(8,128)(2,1)S(1)} %shard_map.130.after_ref.x0_ref), channel_id=1, source_target_pairs={{0,128},{64,192},{128,0},{192,64},{1,129},{65,193},{129,1},{193,65... | collective-permute-start | bytes 98312 | tf_op jit(solution)/shard_map/ppermute | solution.py:286
  5.8 5.1 %collective-permute-start.2 = (bf16[32,512]{1,0:T(8,128)(2,1)S(1)}, bf16[32,512]{1,0:T(8,128)(2,1)S(1)}, u32[]{:S(2)}, u32[]{:S(2)}) collective-permute-start(bf16[32,512]{1,0:T(8,128)(2,1)S(1)} %shard_map.130.after_ref.x0_ref), channel_id=1, source_target_pairs={{0,192},{64,128},{128,64},{192,0},{1,193},{65,129},{129,65},{193,1... | collective-permute-start | bytes 98312 | tf_op jit(solution)/shard_map/ppermute | solution.py:286
  6.8 4.1 %collective-permute-start.1 = (bf16[32,512]{1,0:T(8,128)(2,1)S(1)}, bf16[32,512]{1,0:T(8,128)(2,1)S(1)}, u32[]{:S(2)}, u32[]{:S(2)}) collective-permute-start(bf16[32,512]{1,0:T(8,128)(2,1)S(1)} %shard_map.130.after_ref.x0_ref), channel_id=1, source_target_pairs={{0,64},{64,0},{128,192},{192,128},{1,65},{65,1},{129,193},{193,129... | collective-permute-start | bytes 98312 | tf_op jit(solution)/shard_map/ppermute | solution.py:286
  6.8 32.8 %copy-start = (s32[512]{0:T(512)S(1)}, s32[512]{0:T(512)}, u32[]{:S(2)}) copy-start(s32[512]{0:T(512)} %param.18) | copy-start | bytes 6148
  6.8 32.8 %copy-start.1 = (s32[512]{0:T(512)S(1)}, s32[512]{0:T(512)}, u32[]{:S(2)}) copy-start(s32[512]{0:T(512)} %param.19) | copy-start | bytes 6148
  29.8 5.7 %collective-permute-start.6 = (bf16[160,128]{1,0:T(8,128)(2,1)S(1)}, bf16[160,128]{1,0:T(8,128)(2,1)S(1)}, u32[]{:S(2)}, u32[]{:S(2)}) collective-permute-start(bf16[160,128]{1,0:T(8,128)(2,1)S(1)} %shard_map.133.refs_0_), channel_id=1, source_target_pairs={{0,4},{2,6},{4,0},{6,2},{1,5},{3,7},{5,1},{7,3},{8,12},{10,14},{12... | collective-permute-start | bytes 122888 | tf_op jit(solution)/shard_map/ppermute | solution.py:286
  32.9 5.2 %collective-permute-start.5 = (bf16[160,128]{1,0:T(8,128)(2,1)S(1)}, bf16[160,128]{1,0:T(8,128)(2,1)S(1)}, u32[]{:S(2)}, u32[]{:S(2)}) collective-permute-start(bf16[160,128]{1,0:T(8,128)(2,1)S(1)} %shard_map.133.refs_0_), channel_id=1, source_target_pairs={{0,6},{2,4},{4,2},{6,0},{1,7},{3,5},{5,3},{7,1},{8,14},{10,12},{12... | collective-permute-start | bytes 122888 | tf_op jit(solution)/shard_map/ppermute | solution.py:286
  34.1 4.1 %collective-permute-start.4 = (bf16[160,128]{1,0:T(8,128)(2,1)S(1)}, bf16[160,128]{1,0:T(8,128)(2,1)S(1)}, u32[]{:S(2)}, u32[]{:S(2)}) collective-permute-start(bf16[160,128]{1,0:T(8,128)(2,1)S(1)} %shard_map.133.refs_0_), channel_id=1, source_target_pairs={{0,2},{2,0},{4,6},{6,4},{1,3},{3,1},{5,7},{7,5},{8,10},{10,8},{12,... | collective-permute-start | bytes 122888 | tf_op jit(solution)/shard_map/ppermute | solution.py:286
  38.2 1.5 %collective-permute-start.7 = (bf16[4,160,128]{2,1,0:T(8,128)(2,1)S(1)}, bf16[4,160,128]{2,1,0:T(8,128)(2,1)S(1)}, u32[]{:S(2)}, u32[]{:S(2)}) collective-permute-start(bf16[4,160,128]{2,1,0:T(8,128)(2,1)S(1)} %shard_map.134.mine_ref), channel_id=1, source_target_pairs={{0,1},{1,0},{2,3},{3,2},{4,5},{5,4},{6,7},{7,6},{8,9},{9,8},{10,11... | collective-permute-start | bytes 491528 | tf_op jit(solution)/shard_map/ppermute | solution.py:360
  40.8 5.3 %collective-permute-start.10 = (bf16[80,128]{1,0:T(8,128)(2,1)S(1)}, bf16[80,128]{1,0:T(8,128)(2,1)S(1)}, u32[]{:S(2)}, u32[]{:S(2)}) collective-permute-start(bf16[80,128]{1,0:T(8,128)(2,1)S(1)} %shard_map.135.refs_0_), channel_id=1, source_target_pairs={{0,128},{64,192},{128,0},{192,64},{1,129},{65,193},{129,1},{193,65... | collective-permute-start | bytes 61448 | tf_op jit(solution)/shard_map/ppermute | solution.py:286
  42.6 5.0 %collective-permute-start.9 = (bf16[80,128]{1,0:T(8,128)(2,1)S(1)}, bf16[80,128]{1,0:T(8,128)(2,1)S(1)}, u32[]{:S(2)}, u32[]{:S(2)}) collective-permute-start(bf16[80,128]{1,0:T(8,128)(2,1)S(1)} %shard_map.135.refs_0_), channel_id=1, source_target_pairs={{0,192},{64,128},{128,64},{192,0},{1,193},{65,129},{129,65},{193,1... | collective-permute-start | bytes 61448 | tf_op jit(solution)/shard_map/ppermute | solution.py:286
  43.8 3.8 %collective-permute-start.8 = (bf16[80,128]{1,0:T(8,128)(2,1)S(1)}, bf16[80,128]{1,0:T(8,128)(2,1)S(1)}, u32[]{:S(2)}, u32[]{:S(2)}) collective-permute-start(bf16[80,128]{1,0:T(8,128)(2,1)S(1)} %shard_map.135.refs_0_), channel_id=1, source_target_pairs={{0,64},{64,0},{128,192},{192,128},{1,65},{65,1},{129,193},{193,129... | collective-permute-start | bytes 61448 | tf_op jit(solution)/shard_map/ppermute | solution.py:286

commit v5 on v4

--- a/solution.py
+++ b/solution.py
@@ -14,6 +14,7 @@
 GELU_SCALE = 0.7978845608028654
 GELU_CUBE = 0.044715
 LOAD_UNROLL = 16
+COL_BITS = ("c0", "c1", "c2")
 ORDER = (1, 3, 2)
 F32 = jnp.float32
 BF16 = jnp.bfloat16
@@ -106,6 +107,10 @@
     onehot = jnp.where(here, 1.0, 0.0).astype(BF16)
     used = dot(jnp.ones((8, slots), BF16), onehot, ((1,), (1,)))
     used_ref[...] = used[0:1].astype(jnp.int32)
+
+
+def bit_reversed(k):
+    return (k & 1) << 2 | (k & 2) | k >> 2
 
 
 def aggregate_kernel(used_ref, x0_ref, x1_ref, x2_ref, x3_ref, tiles_ref, out_ref, all_ref):
@@ -127,8 +132,9 @@
                 tiles.append(jnp.where(used_ref[0, place] > 0, tile, jnp.zeros_like(tile)))
             strips.append(jnp.concatenate(tiles, 1))
         wide = dot(jnp.concatenate(strips, 0), x_all, ((1,), (1,))).T.astype(BF16)
-        out_ref[group, :feats, :] = wide[:, :TILE]
-        out_ref[group, feats:, :] = wide[:, TILE:]
+        place = bit_reversed(group)
+        out_ref[place, :feats, :] = wide[:, :TILE]
+        out_ref[place, feats:, :] = wide[:, TILE:]
 
 
 def pack_weights(w1_ref, w2_ref, bias_ref, out_ref):
@@ -300,7 +306,7 @@
     labels,
     label_mask,
 ):
-    n_row, n_col = lax.axis_size("row"), lax.axis_size("col")
+    n_row, n_col = lax.axis_size("row"), lax.axis_size(COL_BITS)
     n_core = lax.axis_size("core")
     n_feat = lax.axis_size("x") * n_core
     nodes, feats = features.shape
@@ -352,7 +358,7 @@
         scalars=1,
         scratch=[pltpu.VMEM((2 * feats, n_row * nodes), BF16)],
     )
-    parts = lax.all_to_all(partial, "col", 0, 0)
+    parts = lax.all_to_all(partial, COL_BITS, 0, 0)
     rows = parts.shape[1] + weights.shape[0]
     message = call(total_kernel, pltpu.VMEM((rows, TILE), BF16), parts, weights)
     messages = (message, *exchanged(message, "x"))
@@ -373,7 +379,7 @@
         grads,
         *exchanged(grads, "row"),
     )
-    grads = lax.all_to_all(grads, "col", 0, 0)
+    grads = lax.all_to_all(grads, COL_BITS, 0, 0)
     w1, w2, b1, loss = call(
         final_kernel,
         (
@@ -389,20 +395,21 @@
 def solution(mesh):
     shape = mesh.devices.shape
     split = jax.sharding.Mesh(
-        mesh.devices.reshape(*shape[:2], shape[2] // 2, 2), ("row", "col", "x", "core")
-    )
-    feat = ("x", "core")
+        mesh.devices.reshape(shape[0], 2, 2, 2, shape[2] // 2, 2),
+        ("row", "c2", "c1", "c0", "x", "core"),
+    )
+    col, feat = ("c2", "c1", "c0"), ("x", "core")
     in_specs = (
-        P(("col", "row"), feat),
+        P((*col, "row"), feat),
         P(None, feat),
         P(feat),
         P(feat, None),
-        P("row", "col", None, None, None),
-        P("row", "col", None),
-        P("row", "col", None),
-        P("row", "col"),
-        P(("row", "col")),
-        P(("row", "col")),
+        P("row", col, None, None, None),
+        P("row", col, None),
+        P("row", col, None),
+        P("row", col),
+        P(("row", *col)),
+        P(("row", *col)),
     )
     out_specs = (P(), P(None, feat), P(feat), P(feat, None))
     return jax.shard_map(

time: 61.4 us -> 59.3 us (0.966); the launches traced: 60.4 us -> 59.1 us
  blocking collectives: 27.8 us -> 26.1 us
    all_to_all x2, blocking collectives: 27.8 us -> 26.1 us  [the longest x1 15.2 us: on_device(): parts = lax.all_to_all(partial, COL_BITS, 0, 0)]
  transfers between devices with their start and end apart: 11 -> 11, of which waited for: 6 -> 6; matrix products, arithmetic and copies ran while one was open for 0% -> 0% of each run, Pallas kernels for 5% -> 6%
where the time goes in v5:
time: 59.3 us; the launch traced here: 59.1 us
  blocking collectives  26.1 us (44%)
  starting transfers between devices  12.3 us (21%)
  waiting for transfers between devices  10.8 us (18%)
  Pallas kernels  8.52 us (14%)
  between operations  1.35 us (2%)
    all_to_all x1, blocking collectives, on_device(): parts = lax.all_to_all(partial, COL_BITS, 0, 0)  15.2 us
    ppermute x9, starting transfers between devices, exchanged(): lax.ppermute(value, axis, [(k, k ^ step) for k in range(size)])  12.1 us
    all_to_all x1, blocking collectives, on_device(): grads = lax.all_to_all(grads, COL_BITS, 0, 0)  10.8 us
    ppermute x9, waiting for transfers between devices, exchanged(): lax.ppermute(value, axis, [(k, k ^ step) for k in range(size)])  9.47 us
    pallas_call x7, Pallas kernels, call(): pl.pallas_call(kernel, out_shape=out_shape, in_specs=[IN_SMEM] * scalars...  5.12 us
    pallas_call x1, Pallas kernels, on_device(): pl.pallas_call(load_kernel, out_shape=pltpu.VMEM((places, TILE, TILE), BF...  2.35 us
    ppermute x1, waiting for transfers between devices, on_device(): other = lax.ppermute(mine, 'core', [(0, 1), (1, 0)])  1.38 us
  transfers between devices with their start and end apart: 11, of which 6 were waited for; matrix products, arithmetic and copies ran while one was open for 0% of the time, Pallas kernels for 6%

profile of v5, /device:TPU:32, one launch (start us, length us, event | category | flops | bytes accessed | tf_op | source)
XLA Modules:
  0.0 59.1 jit_solution(16586378963851112066)
XLA Ops:
  0.6 0.1 collective-permute-start
  1.4 1.1 %shard_map.129 = (s32[1,384]{1,0:T(1,128)S(1)}, s32[1,256]{1,0:T(1,128)S(1)}, bf16[96,128]{1,0:T(8,128)(2,1)S(1)}, bf16[16,512]{1,0:T(8,128)(2,1)S(1)}) custom-call(s32[1,1]{1,0:T(1,128)S(6)} %copy.14.live_ref, s32[1,1,384]{2,1,0:T(1,128)} %rows_in.1, s32[1,1,384]{2,1,0:T(1,128)} %cols_in.1, bf16[32,128]{1,0:T(8,128)(2,1)} %bitcast.14, ...), custom_call_target="tpu_custom_call" | custom-call | tf_op jit(solution)/shard_map/pallas_call | solution.py:324
  2.5 3.3 %collective-permute-start.3 = (bf16[32,512]{1,0:T(8,128)(2,1)S(1)}, bf16[32,512]{1,0:T(8,128)(2,1)S(1)}, u32[]{:S(2)}, u32[]{:S(2)}) collective-permute-start(bf16[32,512]{1,0:T(8,128)(2,1)S(1)} %shard_map.130.after_ref.x0_ref), channel_id=1, source_target_pairs={{0,128},{64,192},{128,0},{192,64},{1,129},{65,193},{129,1},{193,65... | collective-permute-start | bytes 98312 | tf_op jit(solution)/shard_map/ppermute | solution.py:292
  5.8 1.1 %collective-permute-start.2 = (bf16[32,512]{1,0:T(8,128)(2,1)S(1)}, bf16[32,512]{1,0:T(8,128)(2,1)S(1)}, u32[]{:S(2)}, u32[]{:S(2)}) collective-permute-start(bf16[32,512]{1,0:T(8,128)(2,1)S(1)} %shard_map.130.after_ref.x0_ref), channel_id=1, source_target_pairs={{0,192},{64,128},{128,64},{192,0},{1,193},{65,129},{129,65},{193,1... | collective-permute-start | bytes 98312 | tf_op jit(solution)/shard_map/ppermute | solution.py:292
  6.8 2.3 %shard_map.131.tiles_ref = bf16[256,128,128]{2,1,0:T(8,128)(2,1)S(1)} custom-call(s32[1,384]{1,0:T(1,128)S(1)} %get-tuple-element.14.place_ref, bf16[384,128,128]{2,1,0:T(8,128)(2,1)} %bitcast.11, bf16[32,512]{1,0:T(8,128)(2,1)S(1)} %shard_map.130.after_ref.x0_ref), custom_call_target="tpu_custom_call" | custom-call | bytes 12582912 | tf_op jit(solution)/shard_map/pallas_call | solution.py:340
  9.2 1.7 %collective-permute-done.2.x2_ref = bf16[32,512]{1,0:T(8,128)(2,1)S(1)} collective-permute-done((bf16[32,512]{1,0:T(8,128)(2,1)S(1)}, bf16[32,512]{1,0:T(8,128)(2,1)S(1)}, u32[]{:S(2)}, u32[]{:S(2)}) %collective-permute-start.2) | collective-permute-done | bytes 32800 | tf_op jit(solution)/shard_map/ppermute | solution.py:292
  10.9 0.0 collective-permute-done.1.x1_ref
  10.9 2.9 %shard_map.132 = bf16[8,64,128]{2,1,0:T(8,128)(2,1)S(1)} custom-call(s32[1,256]{1,0:T(1,128)S(1)} %get-tuple-element.12.used_ref, bf16[32,512]{1,0:T(8,128)(2,1)S(1)} %shard_map.130.after_ref.x0_ref, bf16[32,512]{1,0:T(8,128)(2,1)S(1)} %collective-permute-done.1.x1_ref, bf16[32,512]{1,0:T(8,128)(2,1)S(1)} %collective-permute-done.2.x2_ref, ...), custom_call_target="tpu_custom_call" | custom-call | tf_op jit(solution)/shard_map/pallas_call | solution.py:37
  13.8 15.2 %all_to_all.10.parts_ref = bf16[8,64,128]{2,1,0:T(8,128)(2,1)S(1)} all-to-all(bf16[8,64,128]{2,1,0:T(8,128)(2,1)S(1)} %shard_map.132), channel_id=1, replica_groups=mesh['row'=4,'c2'=2,'c1'=2,'c0'=2,'x'=4,'core'=2] {'c0','c1','c2'}, dimensions={0} | all-to-all | bytes 262144 | tf_op jit(solution)/shard_map/all_to_all | solution.py:361
  29.0 3.1 %collective-permute-start.6 = (bf16[160,128]{1,0:T(8,128)(2,1)S(1)}, bf16[160,128]{1,0:T(8,128)(2,1)S(1)}, u32[]{:S(2)}, u32[]{:S(2)}) collective-permute-start(bf16[160,128]{1,0:T(8,128)(2,1)S(1)} %shard_map.133.refs_0_), channel_id=1, source_target_pairs={{0,4},{2,6},{4,0},{6,2},{1,5},{3,7},{5,1},{7,3},{8,12},{10,14},{12... | collective-permute-start | bytes 122888 | tf_op jit(solution)/shard_map/ppermute | solution.py:292
  32.1 1.1 %collective-permute-start.5 = (bf16[160,128]{1,0:T(8,128)(2,1)S(1)}, bf16[160,128]{1,0:T(8,128)(2,1)S(1)}, u32[]{:S(2)}, u32[]{:S(2)}) collective-permute-start(bf16[160,128]{1,0:T(8,128)(2,1)S(1)} %shard_map.133.refs_0_), channel_id=1, source_target_pairs={{0,6},{2,4},{4,2},{6,0},{1,7},{3,5},{5,3},{7,1},{8,14},{10,12},{12... | collective-permute-start | bytes 122888 | tf_op jit(solution)/shard_map/ppermute | solution.py:292
  33.3 1.3 %collective-permute-done.6.refs_3_ = bf16[160,128]{1,0:T(8,128)(2,1)S(1)} collective-permute-done((bf16[160,128]{1,0:T(8,128)(2,1)S(1)}, bf16[160,128]{1,0:T(8,128)(2,1)S(1)}, u32[]{:S(2)}, u32[]{:S(2)}) %collective-permute-start.6) | collective-permute-done | bytes 40992 | tf_op jit(solution)/shard_map/ppermute | solution.py:292
  34.6 2.7 %collective-permute-done.5.refs_2_ = bf16[160,128]{1,0:T(8,128)(2,1)S(1)} collective-permute-done((bf16[160,128]{1,0:T(8,128)(2,1)S(1)}, bf16[160,128]{1,0:T(8,128)(2,1)S(1)}, u32[]{:S(2)}, u32[]{:S(2)}) %collective-permute-start.5) | collective-permute-done | bytes 40992 | tf_op jit(solution)/shard_map/ppermute | solution.py:292
  37.4 0.1 collective-permute-start.7
  37.5 1.4 %collective-permute-done.7.other_ref = bf16[4,160,128]{2,1,0:T(8,128)(2,1)S(1)} collective-permute-done((bf16[4,160,128]{2,1,0:T(8,128)(2,1)S(1)}, bf16[4,160,128]{2,1,0:T(8,128)(2,1)S(1)}, u32[]{:S(2)}, u32[]{:S(2)}) %collective-permute-start.7) | collective-permute-done | bytes 163872 | tf_op jit(solution)/shard_map/ppermute | solution.py:366
  38.9 1.2 %shard_map.135.refs_0_ = bf16[80,128]{1,0:T(8,128)(2,1)S(1)} custom-call(bf16[4,160,128]{2,1,0:T(8,128)(2,1)S(1)} %shard_map.134.mine_ref, bf16[4,160,128]{2,1,0:T(8,128)(2,1)S(1)} %collective-permute-done.7.other_ref, s32[1,512]{1,0:T(1,128)S(1)} %bitcast.9, s32[1,512]{1,0:T(1,128)S(1)} %bitcast.10), custom_call_target="tpu_custom_call" | custom-call | tf_op jit(solution)/shard_map/pallas_call | solution.py:37
  40.1 2.2 %collective-permute-start.10 = (bf16[80,128]{1,0:T(8,128)(2,1)S(1)}, bf16[80,128]{1,0:T(8,128)(2,1)S(1)}, u32[]{:S(2)}, u32[]{:S(2)}) collective-permute-start(bf16[80,128]{1,0:T(8,128)(2,1)S(1)} %shard_map.135.refs_0_), channel_id=1, source_target_pairs={{0,128},{64,192},{128,0},{192,64},{1,129},{65,193},{129,1},{193,65... | collective-permute-start | bytes 61448 | tf_op jit(solution)/shard_map/ppermute | solution.py:292
  42.3 0.9 %collective-permute-start.9 = (bf16[80,128]{1,0:T(8,128)(2,1)S(1)}, bf16[80,128]{1,0:T(8,128)(2,1)S(1)}, u32[]{:S(2)}, u32[]{:S(2)}) collective-permute-start(bf16[80,128]{1,0:T(8,128)(2,1)S(1)} %shard_map.135.refs_0_), channel_id=1, source_target_pairs={{0,192},{64,128},{128,64},{192,0},{1,193},{65,129},{129,65},{193,1... | collective-permute-start | bytes 61448 | tf_op jit(solution)/shard_map/ppermute | solution.py:292
  43.2 0.4 collective-permute-start.8
  43.6 1.8 %collective-permute-done.10.refs_3_ = bf16[80,128]{1,0:T(8,128)(2,1)S(1)} collective-permute-done((bf16[80,128]{1,0:T(8,128)(2,1)S(1)}, bf16[80,128]{1,0:T(8,128)(2,1)S(1)}, u32[]{:S(2)}, u32[]{:S(2)}) %collective-permute-start.10) | collective-permute-done | bytes 20512 | tf_op jit(solution)/shard_map/ppermute | solution.py:292
  45.4 1.9 %collective-permute-done.9.refs_2_ = bf16[80,128]{1,0:T(8,128)(2,1)S(1)} collective-permute-done((bf16[80,128]{1,0:T(8,128)(2,1)S(1)}, bf16[80,128]{1,0:T(8,128)(2,1)S(1)}, u32[]{:S(2)}, u32[]{:S(2)}) %collective-permute-start.9) | collective-permute-done | bytes 20512 | tf_op jit(solution)/shard_map/ppermute | solution.py:292
  47.2 0.2 shard_map.136
  47.4 10.8 %all_to_all.11.parts_ref = bf16[8,80,128]{2,1,0:T(8,128)(2,1)S(1)} all-to-all(bf16[8,80,128]{2,1,0:T(8,128)(2,1)S(1)} %shard_map.136), channel_id=1, replica_groups=mesh['row'=4,'c2'=2,'c1'=2,'c0'=2,'x'=4,'core'=2] {'c0','c1','c2'}, dimensions={0} | all-to-all | bytes 327680 | tf_op jit(solution)/shard_map/all_to_all | solution.py:382
  58.3 0.8 %shard_map.137 = (f32[32,128]{1,0:T(8,128)}, f32[32,172]{1,0:T(8,128)}, f32[1,32]{1,0:T(1,128)}, f32[1,1]{1,0:T(1,128)}) custom-call(bf16[8,80,128]{2,1,0:T(8,128)(2,1)S(1)} %all_to_all.11.parts_ref), custom_call_target="tpu_custom_call" | custom-call | tf_op jit(solution)/shard_map/pallas_call | solution.py:37
  (13 shorter events, 0.1 us)
Async XLA Ops:
  0.6 1.8 %collective-permute-start = (bf16[16,512]{1,0:T(8,128)(2,1)}, bf16[16,512]{1,0:T(8,128)(2,1)S(1)}, u32[]{:S(2)}, u32[]{:S(2)}) collective-permute-start(bf16[16,512]{1,0:T(8,128)(2,1)} %bitcast.12), channel_id=1, source_target_pairs={{0,1},{1,0},{2,3},{3,2},{4,5},{5,4},{6,7},{7,6},{8,9},{9,8},{10,11... | collective-permute-start | bytes 49160 | tf_op jit(solution)/shard_map/ppermute | solution.py:318
  2.5 6.7 %collective-permute-start.3 = (bf16[32,512]{1,0:T(8,128)(2,1)S(1)}, bf16[32,512]{1,0:T(8,128)(2,1)S(1)}, u32[]{:S(2)}, u32[]{:S(2)}) collective-permute-start(bf16[32,512]{1,0:T(8,128)(2,1)S(1)} %shard_map.130.after_ref.x0_ref), channel_id=1, source_target_pairs={{0,128},{64,192},{128,0},{192,64},{1,129},{65,193},{129,1},{193,65... | collective-permute-start | bytes 98312 | tf_op jit(solution)/shard_map/ppermute | solution.py:292
  5.8 5.1 %collective-permute-start.2 = (bf16[32,512]{1,0:T(8,128)(2,1)S(1)}, bf16[32,512]{1,0:T(8,128)(2,1)S(1)}, u32[]{:S(2)}, u32[]{:S(2)}) collective-permute-start(bf16[32,512]{1,0:T(8,128)(2,1)S(1)} %shard_map.130.after_ref.x0_ref), channel_id=1, source_target_pairs={{0,192},{64,128},{128,64},{192,0},{1,193},{65,129},{129,65},{193,1... | collective-permute-start | bytes 98312 | tf_op jit(solution)/shard_map/ppermute | solution.py:292
  6.8 4.1 %collective-permute-start.1 = (bf16[32,512]{1,0:T(8,128)(2,1)S(1)}, bf16[32,512]{1,0:T(8,128)(2,1)S(1)}, u32[]{:S(2)}, u32[]{:S(2)}) collective-permute-start(bf16[32,512]{1,0:T(8,128)(2,1)S(1)} %shard_map.130.after_ref.x0_ref), channel_id=1, source_target_pairs={{0,64},{64,0},{128,192},{192,128},{1,65},{65,1},{129,193},{193,129... | collective-permute-start | bytes 98312 | tf_op jit(solution)/shard_map/ppermute | solution.py:292
  6.8 32.1 %copy-start = (s32[512]{0:T(512)S(1)}, s32[512]{0:T(512)}, u32[]{:S(2)}) copy-start(s32[512]{0:T(512)} %param.18) | copy-start | bytes 6148
  6.8 32.1 %copy-start.1 = (s32[512]{0:T(512)S(1)}, s32[512]{0:T(512)}, u32[]{:S(2)}) copy-start(s32[512]{0:T(512)} %param.19) | copy-start | bytes 6148
  29.0 5.6 %collective-permute-start.6 = (bf16[160,128]{1,0:T(8,128)(2,1)S(1)}, bf16[160,128]{1,0:T(8,128)(2,1)S(1)}, u32[]{:S(2)}, u32[]{:S(2)}) collective-permute-start(bf16[160,128]{1,0:T(8,128)(2,1)S(1)} %shard_map.133.refs_0_), channel_id=1, source_target_pairs={{0,4},{2,6},{4,0},{6,2},{1,5},{3,7},{5,1},{7,3},{8,12},{10,14},{12... | collective-permute-start | bytes 122888 | tf_op jit(solution)/shard_map/ppermute | solution.py:292
  32.1 5.2 %collective-permute-start.5 = (bf16[160,128]{1,0:T(8,128)(2,1)S(1)}, bf16[160,128]{1,0:T(8,128)(2,1)S(1)}, u32[]{:S(2)}, u32[]{:S(2)}) collective-permute-start(bf16[160,128]{1,0:T(8,128)(2,1)S(1)} %shard_map.133.refs_0_), channel_id=1, source_target_pairs={{0,6},{2,4},{4,2},{6,0},{1,7},{3,5},{5,3},{7,1},{8,14},{10,12},{12... | collective-permute-start | bytes 122888 | tf_op jit(solution)/shard_map/ppermute | solution.py:292
  33.3 4.1 %collective-permute-start.4 = (bf16[160,128]{1,0:T(8,128)(2,1)S(1)}, bf16[160,128]{1,0:T(8,128)(2,1)S(1)}, u32[]{:S(2)}, u32[]{:S(2)}) collective-permute-start(bf16[160,128]{1,0:T(8,128)(2,1)S(1)} %shard_map.133.refs_0_), channel_id=1, source_target_pairs={{0,2},{2,0},{4,6},{6,4},{1,3},{3,1},{5,7},{7,5},{8,10},{10,8},{12,... | collective-permute-start | bytes 122888 | tf_op jit(solution)/shard_map/ppermute | solution.py:292
  37.4 1.5 %collective-permute-start.7 = (bf16[4,160,128]{2,1,0:T(8,128)(2,1)S(1)}, bf16[4,160,128]{2,1,0:T(8,128)(2,1)S(1)}, u32[]{:S(2)}, u32[]{:S(2)}) collective-permute-start(bf16[4,160,128]{2,1,0:T(8,128)(2,1)S(1)} %shard_map.134.mine_ref), channel_id=1, source_target_pairs={{0,1},{1,0},{2,3},{3,2},{4,5},{5,4},{6,7},{7,6},{8,9},{9,8},{10,11... | collective-permute-start | bytes 491528 | tf_op jit(solution)/shard_map/ppermute | solution.py:366
  40.1 5.3 %collective-permute-start.10 = (bf16[80,128]{1,0:T(8,128)(2,1)S(1)}, bf16[80,128]{1,0:T(8,128)(2,1)S(1)}, u32[]{:S(2)}, u32[]{:S(2)}) collective-permute-start(bf16[80,128]{1,0:T(8,128)(2,1)S(1)} %shard_map.135.refs_0_), channel_id=1, source_target_pairs={{0,128},{64,192},{128,0},{192,64},{1,129},{65,193},{129,1},{193,65... | collective-permute-start | bytes 61448 | tf_op jit(solution)/shard_map/ppermute | solution.py:292
  42.3 5.0 %collective-permute-start.9 = (bf16[80,128]{1,0:T(8,128)(2,1)S(1)}, bf16[80,128]{1,0:T(8,128)(2,1)S(1)}, u32[]{:S(2)}, u32[]{:S(2)}) collective-permute-start(bf16[80,128]{1,0:T(8,128)(2,1)S(1)} %shard_map.135.refs_0_), channel_id=1, source_target_pairs={{0,192},{64,128},{128,64},{192,0},{1,193},{65,129},{129,65},{193,1... | collective-permute-start | bytes 61448 | tf_op jit(solution)/shard_map/ppermute | solution.py:292
  43.2 4.1 %collective-permute-start.8 = (bf16[80,128]{1,0:T(8,128)(2,1)S(1)}, bf16[80,128]{1,0:T(8,128)(2,1)S(1)}, u32[]{:S(2)}, u32[]{:S(2)}) collective-permute-start(bf16[80,128]{1,0:T(8,128)(2,1)S(1)} %shard_map.135.refs_0_), channel_id=1, source_target_pairs={{0,64},{64,0},{128,192},{192,128},{1,65},{65,1},{129,193},{193,129... | collective-permute-start | bytes 61448 | tf_op jit(solution)/shard_map/ppermute | solution.py:292

commit v6 on v5

--- a/solution.py
+++ b/solution.py
@@ -44,27 +44,28 @@
         cost_estimate=cost,
     )(*placed)
 
-def load_kernel(place_ref, tiles_ref, after_ref, out_ref, sem):
+def load_kernel(live_ref, place_ref, tiles_ref, after_ref, out_ref, sem):
     del after_ref
-    slots = tiles_ref.shape[0]
+    live = jnp.minimum(live_ref[0, 0], tiles_ref.shape[0])
 
     def start(trip, started):
         for part in range(LOAD_UNROLL):
             slot = trip * LOAD_UNROLL + part
             place = place_ref[0, slot]
-
-            @pl.when(place >= 0)
+            mine = (place >= 0) & (slot < live)
+
+            @pl.when(mine)
             def _():
                 pltpu.make_async_copy(tiles_ref.at[slot], out_ref.at[place], sem).start()
 
-            started = started + (place >= 0).astype(jnp.int32)
+            started = started + mine.astype(jnp.int32)
         return started
 
     def finish(k, carry):
         pltpu.make_async_copy(tiles_ref.at[0], out_ref.at[0], sem).wait()
         return carry
 
-    started = lax.fori_loop(0, slots // LOAD_UNROLL, start, 0)
+    started = lax.fori_loop(0, (live + LOAD_UNROLL - 1) // LOAD_UNROLL, start, 0)
     lax.fori_loop(0, started, finish, 0)
 
 
@@ -77,8 +78,8 @@
 
 
 def setup_kernel(
-    live_ref, rows_in, cols_in, w1_in, w2_in, bias_in, x_in,
-    place_ref, used_ref, weights_ref, x_ref, rows_ref, cols_ref, w1_ref, w2_ref, bias_ref, sems,
+    rows_in, cols_in, w1_in, w2_in, bias_in, x_in,
+    place_ref, slot_ref, weights_ref, x_ref, rows_ref, cols_ref, w1_ref, w2_ref, bias_ref, place_vmem, slot_vmem, sems,
 ):
     sources = (rows_in, cols_in, w1_in, w2_in, bias_in, x_in)
     targets = (rows_ref, cols_ref, w1_ref, w2_ref, bias_ref, x_ref)
@@ -90,38 +91,48 @@
         copy.start()
     for copy in copies:
         copy.wait()
-    place_tiles(live_ref, rows_ref, cols_ref, place_ref, used_ref)
+    place_tiles(rows_ref, cols_ref, place_vmem, slot_vmem)
+    maps = (
+        pltpu.make_async_copy(place_vmem, place_ref, sems.at[0]),
+        pltpu.make_async_copy(slot_vmem, slot_ref, sems.at[1]),
+    )
+    for copy in maps:
+        copy.start()
     pack_weights(w1_ref, w2_ref, bias_ref, weights_ref)
-
-
-def place_tiles(live_ref, rows_ref, cols_ref, place_ref, used_ref):
-    places = used_ref.shape[1]
+    for copy in maps:
+        copy.wait()
+
+
+def place_tiles(rows_ref, cols_ref, place_ref, slot_ref):
+    places = slot_ref.shape[1]
     slots = rows_ref.shape[2]
-    slot = lax.broadcasted_iota(jnp.int32, (1, slots), 1)
     rows = rows_ref[0]
     place = ((rows >> 2) * 2 + (rows & 1)) * (places // 16) + cols_ref[0]
-    mine = (slot < live_ref[0, 0]) & (((rows >> 1) & 1) == lax.axis_index("core"))
-    place = jnp.where(mine, place, -1)
+    place = jnp.where(((rows >> 1) & 1) == lax.axis_index("core"), place, -1)
     place_ref[...] = place
     here = lax.broadcasted_iota(jnp.int32, (places, slots), 0) == place
     onehot = jnp.where(here, 1.0, 0.0).astype(BF16)
-    used = dot(jnp.ones((8, slots), BF16), onehot, ((1,), (1,)))
-    used_ref[...] = used[0:1].astype(jnp.int32)
+    number = lax.broadcasted_iota(jnp.int32, (8, slots), 1) + 1
+    digit = lax.broadcasted_iota(jnp.int32, (8, slots), 0)
+    digits = jnp.where(digit == 0, number & 127, jnp.where(digit == 1, number >> 7, 0))
+    found = dot(digits.astype(F32).astype(BF16), onehot, ((1,), (1,)))
+    slot_ref[...] = (found[0:1] + 128.0 * found[1:2]).astype(jnp.int32) - 1
 
 
 def bit_reversed(k):
     return (k & 1) << 2 | (k & 2) | k >> 2
 
 
-def aggregate_kernel(used_ref, x0_ref, x1_ref, x2_ref, x3_ref, tiles_ref, out_ref, all_ref):
+def aggregate_kernel(live_ref, slot_ref, x0_ref, x1_ref, x2_ref, x3_ref, tiles_ref, out_ref, all_ref):
     feats, nodes = x0_ref.shape
     row, n_row = lax.axis_index("row"), lax.axis_size("row")
     for k, part in zip((0, *ORDER), (x0_ref, x1_ref, x2_ref, x3_ref)):
         source = row ^ k
         all_ref[:, pl.ds(pl.multiple_of(source * nodes, TILE), nodes)] = part[...]
     x_all = all_ref[...]
+    live = live_ref[0, 0]
     groups = out_ref.shape[0]
-    col_blocks = used_ref.shape[1] // (2 * groups)
+    col_blocks = slot_ref.shape[1] // (2 * groups)
     for group in range(groups):
         strips = []
         for block in (2 * group, 2 * group + 1):
@@ -129,7 +140,9 @@
             for j in range(col_blocks):
                 place = block * col_blocks + j
                 tile = tiles_ref[place]
-                tiles.append(jnp.where(used_ref[0, place] > 0, tile, jnp.zeros_like(tile)))
+                slot = slot_ref[0, place]
+                here = (slot >= 0) & (slot < live)
+                tiles.append(jnp.where(here, tile, jnp.zeros_like(tile)))
             strips.append(jnp.concatenate(tiles, 1))
         wide = dot(jnp.concatenate(strips, 0), x_all, ((1,), (1,))).T.astype(BF16)
         place = bit_reversed(group)
@@ -321,41 +334,43 @@
     )
     places = row_blocks // 2 * col_blocks
     small = (tile_rows, tile_cols, weight_in.T, weight_out, bias.reshape(1, -1), x_mine)
-    place, used, weights, x_mine = pl.pallas_call(
+    place, slots, weights, x_mine = pl.pallas_call(
         setup_kernel,
         out_shape=(
-            pltpu.VMEM((1, tiles.shape[0]), jnp.int32),
-            pltpu.VMEM((1, places), jnp.int32),
+            pltpu.SMEM((1, tiles.shape[0]), jnp.int32),
+            pltpu.SMEM((1, places), jnp.int32),
             pltpu.VMEM((96, TILE), BF16),
             pltpu.VMEM(x_mine.shape, BF16),
         ),
-        in_specs=[IN_SMEM] + [pl.BlockSpec(memory_space=pltpu.HBM)] * 6,
-        out_specs=(IN_VMEM,) * 4,
+        in_specs=[pl.BlockSpec(memory_space=pltpu.HBM)] * 6,
+        out_specs=(IN_SMEM, IN_SMEM, IN_VMEM, IN_VMEM),
         scratch_shapes=[pltpu.VMEM(v.shape, v.dtype) for v in small[:5]]
+        + [pltpu.VMEM((1, tiles.shape[0]), jnp.int32), pltpu.VMEM((1, places), jnp.int32)]
         + [pltpu.SemaphoreType.DMA((6,))],
         compiler_params=pltpu.CompilerParams(vmem_limit_bytes=8 * 2**20),
-    )(tile_live, *(pltpu.with_memory_space_constraint(v, pltpu.HBM) for v in small))
+    )(*(pltpu.with_memory_space_constraint(v, pltpu.HBM) for v in small))
     x_pair = call(pair_kernel, pltpu.VMEM((2 * feats, nodes), BF16), x_mine, x_other)
     x_rows = exchanged(x_pair, "row")
     loaded = pl.pallas_call(
         load_kernel,
         out_shape=pltpu.VMEM((places, TILE, TILE), BF16),
-        in_specs=[IN_SMEM, pl.BlockSpec(memory_space=pltpu.HBM), IN_VMEM],
+        in_specs=[IN_SMEM, IN_SMEM, pl.BlockSpec(memory_space=pltpu.HBM), IN_VMEM],
         out_specs=IN_VMEM,
         scratch_shapes=[pltpu.SemaphoreType.DMA],
         compiler_params=pltpu.CompilerParams(vmem_limit_bytes=2**20),
         cost_estimate=pl.CostEstimate(
             flops=0, bytes_accessed=2 * tiles.size, transcendentals=0
         ),
-    )(place, tiles, pltpu.with_memory_space_constraint(x_pair, pltpu.VMEM))
+    )(tile_live, place, tiles, pltpu.with_memory_space_constraint(x_pair, pltpu.VMEM))
     partial = call(
         aggregate_kernel,
         pltpu.VMEM((n_col, 4 * feats, TILE), BF16),
-        used,
+        tile_live,
+        slots,
         x_pair,
         *x_rows,
         loaded,
-        scalars=1,
+        scalars=2,
         scratch=[pltpu.VMEM((2 * feats, n_row * nodes), BF16)],
     )
     parts = lax.all_to_all(partial, COL_BITS, 0, 0)

time: 59.3 us -> 58.8 us (level)
  transfers between devices with their start and end apart: 11 -> 11, of which waited for: 6 -> 7; matrix products, arithmetic and copies ran while one was open for 0% -> 0% of each run, Pallas kernels for 6% -> 6%
where the time goes in v6:
time: 58.8 us; the launch traced here: 58.3 us
  blocking collectives  26.2 us (45%)
  starting transfers between devices  12.3 us (21%)
  waiting for transfers between devices  10.4 us (18%)
  Pallas kernels  8.05 us (14%)
  between operations  1.38 us (2%)
    all_to_all x1, blocking collectives, on_device(): parts = lax.all_to_all(partial, COL_BITS, 0, 0)  15.2 us
    ppermute x9, starting transfers between devices, exchanged(): lax.ppermute(value, axis, [(k, k ^ step) for k in range(size)])  12.1 us
    all_to_all x1, blocking collectives, on_device(): grads = lax.all_to_all(grads, COL_BITS, 0, 0)  11 us
    ppermute x9, waiting for transfers between devices, exchanged(): lax.ppermute(value, axis, [(k, k ^ step) for k in range(size)])  8.99 us
    pallas_call x7, Pallas kernels, call(): pl.pallas_call(kernel, out_shape=out_shape, in_specs=[IN_SMEM] * scalars...  4.56 us
    pallas_call x1, Pallas kernels, on_device(): pl.pallas_call(load_kernel, out_shape=pltpu.VMEM((places, TILE, TILE), BF...  1.89 us
    pallas_call x1, Pallas kernels, on_device(): pl.pallas_call(setup_kernel, out_shape=(pltpu.SMEM((1, tiles.shape[0]), j...  1.6 us
    ppermute x1, waiting for transfers between devices, on_device(): other = lax.ppermute(mine, 'core', [(0, 1), (1, 0)])  1.38 us
  transfers between devices with their start and end apart: 11, of which 7 were waited for; matrix products, arithmetic and copies ran while one was open for 0% of the time, Pallas kernels for 6%

profile of v6, /device:TPU:32, one launch (start us, length us, event | category | flops | bytes accessed | tf_op | source)
XLA Modules:
  0.0 58.3 jit_solution(8228310086021329740)
XLA Ops:
  0.6 0.1 collective-permute-start
  0.7 1.6 %shard_map.129 = (s32[1,384]{1,0:T(1,128)S(4)}, s32[1,256]{1,0:T(1,128)S(4)}, bf16[96,128]{1,0:T(8,128)(2,1)S(1)}, bf16[16,512]{1,0:T(8,128)(2,1)S(1)}) custom-call(s32[1,1,384]{2,1,0:T(1,128)} %rows_in.1, s32[1,1,384]{2,1,0:T(1,128)} %cols_in.1, bf16[32,128]{1,0:T(8,128)(2,1)} %bitcast.14, bf16[32,172]{1,0:T(8,128)(2,1)} %w2_in.1, f32[1,32]{1,0:T(1,128)} %bitcast.15, ...), custom_call_target="tpu_custom_call" | custom-call | tf_op jit(solution)/shard_map/pallas_call | solution.py:337
  2.4 3.3 %collective-permute-start.3 = (bf16[32,512]{1,0:T(8,128)(2,1)S(1)}, bf16[32,512]{1,0:T(8,128)(2,1)S(1)}, u32[]{:S(2)}, u32[]{:S(2)}) collective-permute-start(bf16[32,512]{1,0:T(8,128)(2,1)S(1)} %shard_map.130.after_ref.x0_ref), channel_id=1, source_target_pairs={{0,128},{64,192},{128,0},{192,64},{1,129},{65,193},{129,1},{193,65... | collective-permute-start | bytes 98312 | tf_op jit(solution)/shard_map/ppermute | solution.py:305
  5.7 1.1 %collective-permute-start.2 = (bf16[32,512]{1,0:T(8,128)(2,1)S(1)}, bf16[32,512]{1,0:T(8,128)(2,1)S(1)}, u32[]{:S(2)}, u32[]{:S(2)}) collective-permute-start(bf16[32,512]{1,0:T(8,128)(2,1)S(1)} %shard_map.130.after_ref.x0_ref), channel_id=1, source_target_pairs={{0,192},{64,128},{128,64},{192,0},{1,193},{65,129},{129,65},{193,1... | collective-permute-start | bytes 98312 | tf_op jit(solution)/shard_map/ppermute | solution.py:305
  7.4 1.9 %shard_map.131.tiles_ref = bf16[256,128,128]{2,1,0:T(8,128)(2,1)S(1)} custom-call(s32[1,1]{1,0:T(1,128)S(6)} %copy.14.live_ref, s32[1,384]{1,0:T(1,128)S(4)} %get-tuple-element.14.place_ref, bf16[384,128,128]{2,1,0:T(8,128)(2,1)} %bitcast.11, bf16[32,512]{1,0:T(8,128)(2,1)S(1)} %shard_map.130.after_ref.x0_ref), custom_call_target="tpu_custom_call" | custom-call | bytes 12582912 | tf_op jit(solution)/shard_map/pallas_call | solution.py:354
  9.3 1.5 %collective-permute-done.2.x2_ref = bf16[32,512]{1,0:T(8,128)(2,1)S(1)} collective-permute-done((bf16[32,512]{1,0:T(8,128)(2,1)S(1)}, bf16[32,512]{1,0:T(8,128)(2,1)S(1)}, u32[]{:S(2)}, u32[]{:S(2)}) %collective-permute-start.2) | collective-permute-done | bytes 32800 | tf_op jit(solution)/shard_map/ppermute | solution.py:305
  10.8 2.4 %shard_map.132 = bf16[8,64,128]{2,1,0:T(8,128)(2,1)S(1)} custom-call(s32[1,1]{1,0:T(1,128)S(6)} %copy.14.live_ref, s32[1,256]{1,0:T(1,128)S(4)} %get-tuple-element.12.slot_ref, bf16[32,512]{1,0:T(8,128)(2,1)S(1)} %shard_map.130.after_ref.x0_ref, bf16[32,512]{1,0:T(8,128)(2,1)S(1)} %collective-permute-done.1.x1_ref, ...), custom_call_target="tpu_custom_call" | custom-call | tf_op jit(solution)/shard_map/pallas_call | solution.py:37
  13.1 15.2 %all_to_all.10.parts_ref = bf16[8,64,128]{2,1,0:T(8,128)(2,1)S(1)} all-to-all(bf16[8,64,128]{2,1,0:T(8,128)(2,1)S(1)} %shard_map.132), channel_id=1, replica_groups=mesh['row'=4,'c2'=2,'c1'=2,'c0'=2,'x'=4,'core'=2] {'c0','c1','c2'}, dimensions={0} | all-to-all | bytes 262144 | tf_op jit(solution)/shard_map/all_to_all | solution.py:376
  28.4 3.1 %collective-permute-start.6 = (bf16[160,128]{1,0:T(8,128)(2,1)S(1)}, bf16[160,128]{1,0:T(8,128)(2,1)S(1)}, u32[]{:S(2)}, u32[]{:S(2)}) collective-permute-start(bf16[160,128]{1,0:T(8,128)(2,1)S(1)} %shard_map.133.refs_0_), channel_id=1, source_target_pairs={{0,4},{2,6},{4,0},{6,2},{1,5},{3,7},{5,1},{7,3},{8,12},{10,14},{12... | collective-permute-start | bytes 122888 | tf_op jit(solution)/shard_map/ppermute | solution.py:305
  31.5 1.1 %collective-permute-start.5 = (bf16[160,128]{1,0:T(8,128)(2,1)S(1)}, bf16[160,128]{1,0:T(8,128)(2,1)S(1)}, u32[]{:S(2)}, u32[]{:S(2)}) collective-permute-start(bf16[160,128]{1,0:T(8,128)(2,1)S(1)} %shard_map.133.refs_0_), channel_id=1, source_target_pairs={{0,6},{2,4},{4,2},{6,0},{1,7},{3,5},{5,3},{7,1},{8,14},{10,12},{12... | collective-permute-start | bytes 122888 | tf_op jit(solution)/shard_map/ppermute | solution.py:305
  32.6 1.3 %collective-permute-done.6.refs_3_ = bf16[160,128]{1,0:T(8,128)(2,1)S(1)} collective-permute-done((bf16[160,128]{1,0:T(8,128)(2,1)S(1)}, bf16[160,128]{1,0:T(8,128)(2,1)S(1)}, u32[]{:S(2)}, u32[]{:S(2)}) %collective-permute-start.6) | collective-permute-done | bytes 40992 | tf_op jit(solution)/shard_map/ppermute | solution.py:305
  34.0 2.7 %collective-permute-done.5.refs_2_ = bf16[160,128]{1,0:T(8,128)(2,1)S(1)} collective-permute-done((bf16[160,128]{1,0:T(8,128)(2,1)S(1)}, bf16[160,128]{1,0:T(8,128)(2,1)S(1)}, u32[]{:S(2)}, u32[]{:S(2)}) %collective-permute-start.5) | collective-permute-done | bytes 40992 | tf_op jit(solution)/shard_map/ppermute | solution.py:305
  36.7 0.1 collective-permute-start.7
  36.8 1.4 %collective-permute-done.7.other_ref = bf16[4,160,128]{2,1,0:T(8,128)(2,1)S(1)} collective-permute-done((bf16[4,160,128]{2,1,0:T(8,128)(2,1)S(1)}, bf16[4,160,128]{2,1,0:T(8,128)(2,1)S(1)}, u32[]{:S(2)}, u32[]{:S(2)}) %collective-permute-start.7) | collective-permute-done | bytes 163872 | tf_op jit(solution)/shard_map/ppermute | solution.py:381
  38.2 1.2 %shard_map.135.refs_0_ = bf16[80,128]{1,0:T(8,128)(2,1)S(1)} custom-call(bf16[4,160,128]{2,1,0:T(8,128)(2,1)S(1)} %shard_map.134.mine_ref, bf16[4,160,128]{2,1,0:T(8,128)(2,1)S(1)} %collective-permute-done.7.other_ref, s32[1,512]{1,0:T(1,128)S(1)} %bitcast.9, s32[1,512]{1,0:T(1,128)S(1)} %bitcast.10), custom_call_target="tpu_custom_call" | custom-call | tf_op jit(solution)/shard_map/pallas_call | solution.py:37
  39.4 1.7 %collective-permute-start.10 = (bf16[80,128]{1,0:T(8,128)(2,1)S(1)}, bf16[80,128]{1,0:T(8,128)(2,1)S(1)}, u32[]{:S(2)}, u32[]{:S(2)}) collective-permute-start(bf16[80,128]{1,0:T(8,128)(2,1)S(1)} %shard_map.135.refs_0_), channel_id=1, source_target_pairs={{0,128},{64,192},{128,0},{192,64},{1,129},{65,193},{129,1},{193,65... | collective-permute-start | bytes 61448 | tf_op jit(solution)/shard_map/ppermute | solution.py:305
  41.1 1.4 %collective-permute-start.9 = (bf16[80,128]{1,0:T(8,128)(2,1)S(1)}, bf16[80,128]{1,0:T(8,128)(2,1)S(1)}, u32[]{:S(2)}, u32[]{:S(2)}) collective-permute-start(bf16[80,128]{1,0:T(8,128)(2,1)S(1)} %shard_map.135.refs_0_), channel_id=1, source_target_pairs={{0,192},{64,128},{128,64},{192,0},{1,193},{65,129},{129,65},{193,1... | collective-permute-start | bytes 61448 | tf_op jit(solution)/shard_map/ppermute | solution.py:305
  42.6 0.4 collective-permute-start.8
  42.9 1.8 %collective-permute-done.10.refs_3_ = bf16[80,128]{1,0:T(8,128)(2,1)S(1)} collective-permute-done((bf16[80,128]{1,0:T(8,128)(2,1)S(1)}, bf16[80,128]{1,0:T(8,128)(2,1)S(1)}, u32[]{:S(2)}, u32[]{:S(2)}) %collective-permute-start.10) | collective-permute-done | bytes 20512 | tf_op jit(solution)/shard_map/ppermute | solution.py:305
  44.7 1.4 %collective-permute-done.9.refs_2_ = bf16[80,128]{1,0:T(8,128)(2,1)S(1)} collective-permute-done((bf16[80,128]{1,0:T(8,128)(2,1)S(1)}, bf16[80,128]{1,0:T(8,128)(2,1)S(1)}, u32[]{:S(2)}, u32[]{:S(2)}) %collective-permute-start.9) | collective-permute-done | bytes 20512 | tf_op jit(solution)/shard_map/ppermute | solution.py:305
  46.1 0.2 collective-permute-done.8.refs_1_
  46.3 0.2 shard_map.136
  46.5 11.0 %all_to_all.11.parts_ref = bf16[8,80,128]{2,1,0:T(8,128)(2,1)S(1)} all-to-all(bf16[8,80,128]{2,1,0:T(8,128)(2,1)S(1)} %shard_map.136), channel_id=1, replica_groups=mesh['row'=4,'c2'=2,'c1'=2,'c0'=2,'x'=4,'core'=2] {'c0','c1','c2'}, dimensions={0} | all-to-all | bytes 327680 | tf_op jit(solution)/shard_map/all_to_all | solution.py:397
  57.5 0.8 %shard_map.137 = (f32[32,128]{1,0:T(8,128)}, f32[32,172]{1,0:T(8,128)}, f32[1,32]{1,0:T(1,128)}, f32[1,1]{1,0:T(1,128)}) custom-call(bf16[8,80,128]{2,1,0:T(8,128)(2,1)S(1)} %all_to_all.11.parts_ref), custom_call_target="tpu_custom_call" | custom-call | tf_op jit(solution)/shard_map/pallas_call | solution.py:37
  (13 shorter events, 0.1 us)
Async XLA Ops:
  0.6 1.7 %collective-permute-start = (bf16[16,512]{1,0:T(8,128)(2,1)}, bf16[16,512]{1,0:T(8,128)(2,1)S(1)}, u32[]{:S(2)}, u32[]{:S(2)}) collective-permute-start(bf16[16,512]{1,0:T(8,128)(2,1)} %bitcast.12), channel_id=1, source_target_pairs={{0,1},{1,0},{2,3},{3,2},{4,5},{5,4},{6,7},{7,6},{8,9},{9,8},{10,11... | collective-permute-start | bytes 49160 | tf_op jit(solution)/shard_map/ppermute | solution.py:331
  2.4 6.9 %collective-permute-start.3 = (bf16[32,512]{1,0:T(8,128)(2,1)S(1)}, bf16[32,512]{1,0:T(8,128)(2,1)S(1)}, u32[]{:S(2)}, u32[]{:S(2)}) collective-permute-start(bf16[32,512]{1,0:T(8,128)(2,1)S(1)} %shard_map.130.after_ref.x0_ref), channel_id=1, source_target_pairs={{0,128},{64,192},{128,0},{192,64},{1,129},{65,193},{129,1},{193,65... | collective-permute-start | bytes 98312 | tf_op jit(solution)/shard_map/ppermute | solution.py:305
  5.7 5.1 %collective-permute-start.2 = (bf16[32,512]{1,0:T(8,128)(2,1)S(1)}, bf16[32,512]{1,0:T(8,128)(2,1)S(1)}, u32[]{:S(2)}, u32[]{:S(2)}) collective-permute-start(bf16[32,512]{1,0:T(8,128)(2,1)S(1)} %shard_map.130.after_ref.x0_ref), channel_id=1, source_target_pairs={{0,192},{64,128},{128,64},{192,0},{1,193},{65,129},{129,65},{193,1... | collective-permute-start | bytes 98312 | tf_op jit(solution)/shard_map/ppermute | solution.py:305
  6.7 4.1 %collective-permute-start.1 = (bf16[32,512]{1,0:T(8,128)(2,1)S(1)}, bf16[32,512]{1,0:T(8,128)(2,1)S(1)}, u32[]{:S(2)}, u32[]{:S(2)}) collective-permute-start(bf16[32,512]{1,0:T(8,128)(2,1)S(1)} %shard_map.130.after_ref.x0_ref), channel_id=1, source_target_pairs={{0,64},{64,0},{128,192},{192,128},{1,65},{65,1},{129,193},{193,129... | collective-permute-start | bytes 98312 | tf_op jit(solution)/shard_map/ppermute | solution.py:305
  7.4 30.9 %copy-start = (s32[512]{0:T(512)S(1)}, s32[512]{0:T(512)}, u32[]{:S(2)}) copy-start(s32[512]{0:T(512)} %param.18) | copy-start | bytes 6148
  7.4 30.8 %copy-start.1 = (s32[512]{0:T(512)S(1)}, s32[512]{0:T(512)}, u32[]{:S(2)}) copy-start(s32[512]{0:T(512)} %param.19) | copy-start | bytes 6148
  28.4 5.6 %collective-permute-start.6 = (bf16[160,128]{1,0:T(8,128)(2,1)S(1)}, bf16[160,128]{1,0:T(8,128)(2,1)S(1)}, u32[]{:S(2)}, u32[]{:S(2)}) collective-permute-start(bf16[160,128]{1,0:T(8,128)(2,1)S(1)} %shard_map.133.refs_0_), channel_id=1, source_target_pairs={{0,4},{2,6},{4,0},{6,2},{1,5},{3,7},{5,1},{7,3},{8,12},{10,14},{12... | collective-permute-start | bytes 122888 | tf_op jit(solution)/shard_map/ppermute | solution.py:305
  31.5 5.2 %collective-permute-start.5 = (bf16[160,128]{1,0:T(8,128)(2,1)S(1)}, bf16[160,128]{1,0:T(8,128)(2,1)S(1)}, u32[]{:S(2)}, u32[]{:S(2)}) collective-permute-start(bf16[160,128]{1,0:T(8,128)(2,1)S(1)} %shard_map.133.refs_0_), channel_id=1, source_target_pairs={{0,6},{2,4},{4,2},{6,0},{1,7},{3,5},{5,3},{7,1},{8,14},{10,12},{12... | collective-permute-start | bytes 122888 | tf_op jit(solution)/shard_map/ppermute | solution.py:305
  32.6 4.1 %collective-permute-start.4 = (bf16[160,128]{1,0:T(8,128)(2,1)S(1)}, bf16[160,128]{1,0:T(8,128)(2,1)S(1)}, u32[]{:S(2)}, u32[]{:S(2)}) collective-permute-start(bf16[160,128]{1,0:T(8,128)(2,1)S(1)} %shard_map.133.refs_0_), channel_id=1, source_target_pairs={{0,2},{2,0},{4,6},{6,4},{1,3},{3,1},{5,7},{7,5},{8,10},{10,8},{12,... | collective-permute-start | bytes 122888 | tf_op jit(solution)/shard_map/ppermute | solution.py:305
  36.7 1.5 %collective-permute-start.7 = (bf16[4,160,128]{2,1,0:T(8,128)(2,1)S(1)}, bf16[4,160,128]{2,1,0:T(8,128)(2,1)S(1)}, u32[]{:S(2)}, u32[]{:S(2)}) collective-permute-start(bf16[4,160,128]{2,1,0:T(8,128)(2,1)S(1)} %shard_map.134.mine_ref), channel_id=1, source_target_pairs={{0,1},{1,0},{2,3},{3,2},{4,5},{5,4},{6,7},{7,6},{8,9},{9,8},{10,11... | collective-permute-start | bytes 491528 | tf_op jit(solution)/shard_map/ppermute | solution.py:381
  39.4 5.3 %collective-permute-start.10 = (bf16[80,128]{1,0:T(8,128)(2,1)S(1)}, bf16[80,128]{1,0:T(8,128)(2,1)S(1)}, u32[]{:S(2)}, u32[]{:S(2)}) collective-permute-start(bf16[80,128]{1,0:T(8,128)(2,1)S(1)} %shard_map.135.refs_0_), channel_id=1, source_target_pairs={{0,128},{64,192},{128,0},{192,64},{1,129},{65,193},{129,1},{193,65... | collective-permute-start | bytes 61448 | tf_op jit(solution)/shard_map/ppermute | solution.py:305
  41.1 5.0 %collective-permute-start.9 = (bf16[80,128]{1,0:T(8,128)(2,1)S(1)}, bf16[80,128]{1,0:T(8,128)(2,1)S(1)}, u32[]{:S(2)}, u32[]{:S(2)}) collective-permute-start(bf16[80,128]{1,0:T(8,128)(2,1)S(1)} %shard_map.135.refs_0_), channel_id=1, source_target_pairs={{0,192},{64,128},{128,64},{192,0},{1,193},{65,129},{129,65},{193,1... | collective-permute-start | bytes 61448 | tf_op jit(solution)/shard_map/ppermute | solution.py:305
  42.6 3.8 %collective-permute-start.8 = (bf16[80,128]{1,0:T(8,128)(2,1)S(1)}, bf16[80,128]{1,0:T(8,128)(2,1)S(1)}, u32[]{:S(2)}, u32[]{:S(2)}) collective-permute-start(bf16[80,128]{1,0:T(8,128)(2,1)S(1)} %shard_map.135.refs_0_), channel_id=1, source_target_pairs={{0,64},{64,0},{128,192},{192,128},{1,65},{65,1},{129,193},{193,129... | collective-permute-start | bytes 61448 | tf_op jit(solution)/shard_map/ppermute | solution.py:305

commit v7 on v6

--- a/solution.py
+++ b/solution.py
@@ -89,34 +89,39 @@
     ]
     for copy in copies:
         copy.start()
-    for copy in copies:
+    for copy in copies[:2]:
         copy.wait()
-    place_tiles(rows_ref, cols_ref, place_vmem, slot_vmem)
     maps = (
-        pltpu.make_async_copy(place_vmem, place_ref, sems.at[0]),
-        pltpu.make_async_copy(slot_vmem, slot_ref, sems.at[1]),
-    )
-    for copy in maps:
-        copy.start()
+        pltpu.make_async_copy(place_vmem, place_ref, sems.at[6]),
+        pltpu.make_async_copy(slot_vmem, slot_ref, sems.at[7]),
+    )
+    place = places_of(rows_ref, cols_ref, slot_ref.shape[1])
+    place_vmem[...] = place
+    maps[0].start()
+    slot_vmem[...] = slots_of(place, slot_ref.shape[1])
+    maps[1].start()
+    for copy in copies[2:]:
+        copy.wait()
     pack_weights(w1_ref, w2_ref, bias_ref, weights_ref)
     for copy in maps:
         copy.wait()
 
 
-def place_tiles(rows_ref, cols_ref, place_ref, slot_ref):
-    places = slot_ref.shape[1]
-    slots = rows_ref.shape[2]
+def places_of(rows_ref, cols_ref, places):
     rows = rows_ref[0]
     place = ((rows >> 2) * 2 + (rows & 1)) * (places // 16) + cols_ref[0]
-    place = jnp.where(((rows >> 1) & 1) == lax.axis_index("core"), place, -1)
-    place_ref[...] = place
+    return jnp.where(((rows >> 1) & 1) == lax.axis_index("core"), place, -1)
+
+
+def slots_of(place, places):
+    slots = place.shape[1]
     here = lax.broadcasted_iota(jnp.int32, (places, slots), 0) == place
     onehot = jnp.where(here, 1.0, 0.0).astype(BF16)
     number = lax.broadcasted_iota(jnp.int32, (8, slots), 1) + 1
     digit = lax.broadcasted_iota(jnp.int32, (8, slots), 0)
     digits = jnp.where(digit == 0, number & 127, jnp.where(digit == 1, number >> 7, 0))
     found = dot(digits.astype(F32).astype(BF16), onehot, ((1,), (1,)))
-    slot_ref[...] = (found[0:1] + 128.0 * found[1:2]).astype(jnp.int32) - 1
+    return (found[0:1] + 128.0 * found[1:2]).astype(jnp.int32) - 1
 
 
 def bit_reversed(k):
@@ -346,7 +351,7 @@
         out_specs=(IN_SMEM, IN_SMEM, IN_VMEM, IN_VMEM),
         scratch_shapes=[pltpu.VMEM(v.shape, v.dtype) for v in small[:5]]
         + [pltpu.VMEM((1, tiles.shape[0]), jnp.int32), pltpu.VMEM((1, places), jnp.int32)]
-        + [pltpu.SemaphoreType.DMA((6,))],
+        + [pltpu.SemaphoreType.DMA((8,))],
         compiler_params=pltpu.CompilerParams(vmem_limit_bytes=8 * 2**20),
     )(*(pltpu.with_memory_space_constraint(v, pltpu.HBM) for v in small))
     x_pair = call(pair_kernel, pltpu.VMEM((2 * feats, nodes), BF16), x_mine, x_other)

time: 58.8 us -> 58.4 us (level)
  Pallas kernels: 8.05 us -> 7.42 us
  waiting for transfers between devices: 10.4 us -> 11 us
    ppermute x9, waiting for transfers between devices: 8.99 us -> 9.64 us  [exchanged(): lax.ppermute(value, axis, [(k, k ^ step) for k in range(size)])]
  transfers between devices with their start and end apart: 11 -> 11, of which waited for: 7 -> 6; matrix products, arithmetic and copies ran while one was open for 0% -> 0% of each run, Pallas kernels for 6% -> 5%
where the time goes in v7:
time: 58.4 us; the launch traced here: 58.2 us
  blocking collectives  26.1 us (45%)
  starting transfers between devices  12.3 us (21%)
  waiting for transfers between devices  11 us (19%)
  Pallas kernels  7.42 us (13%)
  between operations  1.38 us (2%)
    all_to_all x1, blocking collectives, on_device(): parts = lax.all_to_all(partial, COL_BITS, 0, 0)  15.2 us
    ppermute x9, starting transfers between devices, exchanged(): lax.ppermute(value, axis, [(k, k ^ step) for k in range(size)])  12.1 us
    all_to_all x1, blocking collectives, on_device(): grads = lax.all_to_all(grads, COL_BITS, 0, 0)  10.9 us
    ppermute x9, waiting for transfers between devices, exchanged(): lax.ppermute(value, axis, [(k, k ^ step) for k in range(size)])  9.64 us
    pallas_call x7, Pallas kernels, call(): pl.pallas_call(kernel, out_shape=out_shape, in_specs=[IN_SMEM] * scalars...  4.57 us
    pallas_call x1, Pallas kernels, on_device(): pl.pallas_call(setup_kernel, out_shape=(pltpu.SMEM((1, tiles.shape[0]), j...  1.52 us
    ppermute x1, waiting for transfers between devices, on_device(): other = lax.ppermute(mine, 'core', [(0, 1), (1, 0)])  1.38 us
    pallas_call x1, Pallas kernels, on_device(): pl.pallas_call(load_kernel, out_shape=pltpu.VMEM((places, TILE, TILE), BF...  1.34 us
  transfers between devices with their start and end apart: 11, of which 6 were waited for; matrix products, arithmetic and copies ran while one was open for 0% of the time, Pallas kernels for 5%

profile of v7, /device:TPU:32, one launch (start us, length us, event | category | flops | bytes accessed | tf_op | source)
XLA Modules:
  0.0 58.2 jit_solution(17331588841185398553)
XLA Ops:
  0.6 0.1 collective-permute-start
  0.7 1.5 %shard_map.129 = (s32[1,384]{1,0:T(1,128)S(4)}, s32[1,256]{1,0:T(1,128)S(4)}, bf16[96,128]{1,0:T(8,128)(2,1)S(1)}, bf16[16,512]{1,0:T(8,128)(2,1)S(1)}) custom-call(s32[1,1,384]{2,1,0:T(1,128)} %rows_in.1, s32[1,1,384]{2,1,0:T(1,128)} %cols_in.1, bf16[32,128]{1,0:T(8,128)(2,1)} %bitcast.14, bf16[32,172]{1,0:T(8,128)(2,1)} %w2_in.1, f32[1,32]{1,0:T(1,128)} %bitcast.15, ...), custom_call_target="tpu_custom_call" | custom-call | tf_op jit(solution)/shard_map/pallas_call | solution.py:342
  2.3 3.3 %collective-permute-start.3 = (bf16[32,512]{1,0:T(8,128)(2,1)S(1)}, bf16[32,512]{1,0:T(8,128)(2,1)S(1)}, u32[]{:S(2)}, u32[]{:S(2)}) collective-permute-start(bf16[32,512]{1,0:T(8,128)(2,1)S(1)} %shard_map.130.after_ref.x0_ref), channel_id=1, source_target_pairs={{0,128},{64,192},{128,0},{192,64},{1,129},{65,193},{129,1},{193,65... | collective-permute-start | bytes 98312 | tf_op jit(solution)/shard_map/ppermute | solution.py:310
  5.6 1.1 %collective-permute-start.2 = (bf16[32,512]{1,0:T(8,128)(2,1)S(1)}, bf16[32,512]{1,0:T(8,128)(2,1)S(1)}, u32[]{:S(2)}, u32[]{:S(2)}) collective-permute-start(bf16[32,512]{1,0:T(8,128)(2,1)S(1)} %shard_map.130.after_ref.x0_ref), channel_id=1, source_target_pairs={{0,192},{64,128},{128,64},{192,0},{1,193},{65,129},{129,65},{193,1... | collective-permute-start | bytes 98312 | tf_op jit(solution)/shard_map/ppermute | solution.py:310
  7.3 0.0 copy-start.1
  7.3 1.3 %shard_map.131.tiles_ref = bf16[256,128,128]{2,1,0:T(8,128)(2,1)S(1)} custom-call(s32[1,1]{1,0:T(1,128)S(6)} %copy.14.live_ref, s32[1,384]{1,0:T(1,128)S(4)} %get-tuple-element.14.place_ref, bf16[384,128,128]{2,1,0:T(8,128)(2,1)} %bitcast.11, bf16[32,512]{1,0:T(8,128)(2,1)S(1)} %shard_map.130.after_ref.x0_ref), custom_call_target="tpu_custom_call" | custom-call | bytes 12582912 | tf_op jit(solution)/shard_map/pallas_call | solution.py:359
  8.7 2.0 %collective-permute-done.2.x2_ref = bf16[32,512]{1,0:T(8,128)(2,1)S(1)} collective-permute-done((bf16[32,512]{1,0:T(8,128)(2,1)S(1)}, bf16[32,512]{1,0:T(8,128)(2,1)S(1)}, u32[]{:S(2)}, u32[]{:S(2)}) %collective-permute-start.2) | collective-permute-done | bytes 32800 | tf_op jit(solution)/shard_map/ppermute | solution.py:310
  10.7 2.4 %shard_map.132 = bf16[8,64,128]{2,1,0:T(8,128)(2,1)S(1)} custom-call(s32[1,1]{1,0:T(1,128)S(6)} %copy.14.live_ref, s32[1,256]{1,0:T(1,128)S(4)} %get-tuple-element.12.slot_ref, bf16[32,512]{1,0:T(8,128)(2,1)S(1)} %shard_map.130.after_ref.x0_ref, bf16[32,512]{1,0:T(8,128)(2,1)S(1)} %collective-permute-done.1.x1_ref, ...), custom_call_target="tpu_custom_call" | custom-call | tf_op jit(solution)/shard_map/pallas_call | solution.py:37
  13.1 15.2 %all_to_all.10.parts_ref = bf16[8,64,128]{2,1,0:T(8,128)(2,1)S(1)} all-to-all(bf16[8,64,128]{2,1,0:T(8,128)(2,1)S(1)} %shard_map.132), channel_id=1, replica_groups=mesh['row'=4,'c2'=2,'c1'=2,'c0'=2,'x'=4,'core'=2] {'c0','c1','c2'}, dimensions={0} | all-to-all | bytes 262144 | tf_op jit(solution)/shard_map/all_to_all | solution.py:381
  28.3 3.1 %collective-permute-start.6 = (bf16[160,128]{1,0:T(8,128)(2,1)S(1)}, bf16[160,128]{1,0:T(8,128)(2,1)S(1)}, u32[]{:S(2)}, u32[]{:S(2)}) collective-permute-start(bf16[160,128]{1,0:T(8,128)(2,1)S(1)} %shard_map.133.refs_0_), channel_id=1, source_target_pairs={{0,4},{2,6},{4,0},{6,2},{1,5},{3,7},{5,1},{7,3},{8,12},{10,14},{12... | collective-permute-start | bytes 122888 | tf_op jit(solution)/shard_map/ppermute | solution.py:310
  31.4 1.1 %collective-permute-start.5 = (bf16[160,128]{1,0:T(8,128)(2,1)S(1)}, bf16[160,128]{1,0:T(8,128)(2,1)S(1)}, u32[]{:S(2)}, u32[]{:S(2)}) collective-permute-start(bf16[160,128]{1,0:T(8,128)(2,1)S(1)} %shard_map.133.refs_0_), channel_id=1, source_target_pairs={{0,6},{2,4},{4,2},{6,0},{1,7},{3,5},{5,3},{7,1},{8,14},{10,12},{12... | collective-permute-start | bytes 122888 | tf_op jit(solution)/shard_map/ppermute | solution.py:310
  32.6 1.3 %collective-permute-done.6.refs_3_ = bf16[160,128]{1,0:T(8,128)(2,1)S(1)} collective-permute-done((bf16[160,128]{1,0:T(8,128)(2,1)S(1)}, bf16[160,128]{1,0:T(8,128)(2,1)S(1)}, u32[]{:S(2)}, u32[]{:S(2)}) %collective-permute-start.6) | collective-permute-done | bytes 40992 | tf_op jit(solution)/shard_map/ppermute | solution.py:310
  33.9 2.7 %collective-permute-done.5.refs_2_ = bf16[160,128]{1,0:T(8,128)(2,1)S(1)} collective-permute-done((bf16[160,128]{1,0:T(8,128)(2,1)S(1)}, bf16[160,128]{1,0:T(8,128)(2,1)S(1)}, u32[]{:S(2)}, u32[]{:S(2)}) %collective-permute-start.5) | collective-permute-done | bytes 40992 | tf_op jit(solution)/shard_map/ppermute | solution.py:310
  36.7 0.1 collective-permute-start.7
  36.8 1.4 %collective-permute-done.7.other_ref = bf16[4,160,128]{2,1,0:T(8,128)(2,1)S(1)} collective-permute-done((bf16[4,160,128]{2,1,0:T(8,128)(2,1)S(1)}, bf16[4,160,128]{2,1,0:T(8,128)(2,1)S(1)}, u32[]{:S(2)}, u32[]{:S(2)}) %collective-permute-start.7) | collective-permute-done | bytes 163872 | tf_op jit(solution)/shard_map/ppermute | solution.py:386
  38.1 1.2 %shard_map.135.refs_0_ = bf16[80,128]{1,0:T(8,128)(2,1)S(1)} custom-call(bf16[4,160,128]{2,1,0:T(8,128)(2,1)S(1)} %shard_map.134.mine_ref, bf16[4,160,128]{2,1,0:T(8,128)(2,1)S(1)} %collective-permute-done.7.other_ref, s32[1,512]{1,0:T(1,128)S(1)} %bitcast.9, s32[1,512]{1,0:T(1,128)S(1)} %bitcast.10), custom_call_target="tpu_custom_call" | custom-call | tf_op jit(solution)/shard_map/pallas_call | solution.py:37
  39.3 2.0 %collective-permute-start.10 = (bf16[80,128]{1,0:T(8,128)(2,1)S(1)}, bf16[80,128]{1,0:T(8,128)(2,1)S(1)}, u32[]{:S(2)}, u32[]{:S(2)}) collective-permute-start(bf16[80,128]{1,0:T(8,128)(2,1)S(1)} %shard_map.135.refs_0_), channel_id=1, source_target_pairs={{0,128},{64,192},{128,0},{192,64},{1,129},{65,193},{129,1},{193,65... | collective-permute-start | bytes 61448 | tf_op jit(solution)/shard_map/ppermute | solution.py:310
  41.4 0.9 %collective-permute-start.9 = (bf16[80,128]{1,0:T(8,128)(2,1)S(1)}, bf16[80,128]{1,0:T(8,128)(2,1)S(1)}, u32[]{:S(2)}, u32[]{:S(2)}) collective-permute-start(bf16[80,128]{1,0:T(8,128)(2,1)S(1)} %shard_map.135.refs_0_), channel_id=1, source_target_pairs={{0,192},{64,128},{128,64},{192,0},{1,193},{65,129},{129,65},{193,1... | collective-permute-start | bytes 61448 | tf_op jit(solution)/shard_map/ppermute | solution.py:310
  42.3 0.5 collective-permute-start.8
  42.8 1.8 %collective-permute-done.10.refs_3_ = bf16[80,128]{1,0:T(8,128)(2,1)S(1)} collective-permute-done((bf16[80,128]{1,0:T(8,128)(2,1)S(1)}, bf16[80,128]{1,0:T(8,128)(2,1)S(1)}, u32[]{:S(2)}, u32[]{:S(2)}) %collective-permute-start.10) | collective-permute-done | bytes 20512 | tf_op jit(solution)/shard_map/ppermute | solution.py:310
  44.6 1.7 %collective-permute-done.9.refs_2_ = bf16[80,128]{1,0:T(8,128)(2,1)S(1)} collective-permute-done((bf16[80,128]{1,0:T(8,128)(2,1)S(1)}, bf16[80,128]{1,0:T(8,128)(2,1)S(1)}, u32[]{:S(2)}, u32[]{:S(2)}) %collective-permute-start.9) | collective-permute-done | bytes 20512 | tf_op jit(solution)/shard_map/ppermute | solution.py:310
  46.4 0.2 shard_map.136
  46.5 10.9 %all_to_all.11.parts_ref = bf16[8,80,128]{2,1,0:T(8,128)(2,1)S(1)} all-to-all(bf16[8,80,128]{2,1,0:T(8,128)(2,1)S(1)} %shard_map.136), channel_id=1, replica_groups=mesh['row'=4,'c2'=2,'c1'=2,'c0'=2,'x'=4,'core'=2] {'c0','c1','c2'}, dimensions={0} | all-to-all | bytes 327680 | tf_op jit(solution)/shard_map/all_to_all | solution.py:402
  57.4 0.8 %shard_map.137 = (f32[32,128]{1,0:T(8,128)}, f32[32,172]{1,0:T(8,128)}, f32[1,32]{1,0:T(1,128)}, f32[1,1]{1,0:T(1,128)}) custom-call(bf16[8,80,128]{2,1,0:T(8,128)(2,1)S(1)} %all_to_all.11.parts_ref), custom_call_target="tpu_custom_call" | custom-call | tf_op jit(solution)/shard_map/pallas_call | solution.py:37
  (13 shorter events, 0.1 us)
Async XLA Ops:
  0.6 1.6 %collective-permute-start = (bf16[16,512]{1,0:T(8,128)(2,1)}, bf16[16,512]{1,0:T(8,128)(2,1)S(1)}, u32[]{:S(2)}, u32[]{:S(2)}) collective-permute-start(bf16[16,512]{1,0:T(8,128)(2,1)} %bitcast.12), channel_id=1, source_target_pairs={{0,1},{1,0},{2,3},{3,2},{4,5},{5,4},{6,7},{7,6},{8,9},{9,8},{10,11... | collective-permute-start | bytes 49160 | tf_op jit(solution)/shard_map/ppermute | solution.py:336
  2.3 6.4 %collective-permute-start.3 = (bf16[32,512]{1,0:T(8,128)(2,1)S(1)}, bf16[32,512]{1,0:T(8,128)(2,1)S(1)}, u32[]{:S(2)}, u32[]{:S(2)}) collective-permute-start(bf16[32,512]{1,0:T(8,128)(2,1)S(1)} %shard_map.130.after_ref.x0_ref), channel_id=1, source_target_pairs={{0,128},{64,192},{128,0},{192,64},{1,129},{65,193},{129,1},{193,65... | collective-permute-start | bytes 98312 | tf_op jit(solution)/shard_map/ppermute | solution.py:310
  5.6 5.1 %collective-permute-start.2 = (bf16[32,512]{1,0:T(8,128)(2,1)S(1)}, bf16[32,512]{1,0:T(8,128)(2,1)S(1)}, u32[]{:S(2)}, u32[]{:S(2)}) collective-permute-start(bf16[32,512]{1,0:T(8,128)(2,1)S(1)} %shard_map.130.after_ref.x0_ref), channel_id=1, source_target_pairs={{0,192},{64,128},{128,64},{192,0},{1,193},{65,129},{129,65},{193,1... | collective-permute-start | bytes 98312 | tf_op jit(solution)/shard_map/ppermute | solution.py:310
  6.6 4.1 %collective-permute-start.1 = (bf16[32,512]{1,0:T(8,128)(2,1)S(1)}, bf16[32,512]{1,0:T(8,128)(2,1)S(1)}, u32[]{:S(2)}, u32[]{:S(2)}) collective-permute-start(bf16[32,512]{1,0:T(8,128)(2,1)S(1)} %shard_map.130.after_ref.x0_ref), channel_id=1, source_target_pairs={{0,64},{64,0},{128,192},{192,128},{1,65},{65,1},{129,193},{193,129... | collective-permute-start | bytes 98312 | tf_op jit(solution)/shard_map/ppermute | solution.py:310
  7.3 30.9 %copy-start = (s32[512]{0:T(512)S(1)}, s32[512]{0:T(512)}, u32[]{:S(2)}) copy-start(s32[512]{0:T(512)} %param.18) | copy-start | bytes 6148
  7.3 30.8 %copy-start.1 = (s32[512]{0:T(512)S(1)}, s32[512]{0:T(512)}, u32[]{:S(2)}) copy-start(s32[512]{0:T(512)} %param.19) | copy-start | bytes 6148
  28.3 5.6 %collective-permute-start.6 = (bf16[160,128]{1,0:T(8,128)(2,1)S(1)}, bf16[160,128]{1,0:T(8,128)(2,1)S(1)}, u32[]{:S(2)}, u32[]{:S(2)}) collective-permute-start(bf16[160,128]{1,0:T(8,128)(2,1)S(1)} %shard_map.133.refs_0_), channel_id=1, source_target_pairs={{0,4},{2,6},{4,0},{6,2},{1,5},{3,7},{5,1},{7,3},{8,12},{10,14},{12... | collective-permute-start | bytes 122888 | tf_op jit(solution)/shard_map/ppermute | solution.py:310
  31.4 5.2 %collective-permute-start.5 = (bf16[160,128]{1,0:T(8,128)(2,1)S(1)}, bf16[160,128]{1,0:T(8,128)(2,1)S(1)}, u32[]{:S(2)}, u32[]{:S(2)}) collective-permute-start(bf16[160,128]{1,0:T(8,128)(2,1)S(1)} %shard_map.133.refs_0_), channel_id=1, source_target_pairs={{0,6},{2,4},{4,2},{6,0},{1,7},{3,5},{5,3},{7,1},{8,14},{10,12},{12... | collective-permute-start | bytes 122888 | tf_op jit(solution)/shard_map/ppermute | solution.py:310
  32.6 4.1 %collective-permute-start.4 = (bf16[160,128]{1,0:T(8,128)(2,1)S(1)}, bf16[160,128]{1,0:T(8,128)(2,1)S(1)}, u32[]{:S(2)}, u32[]{:S(2)}) collective-permute-start(bf16[160,128]{1,0:T(8,128)(2,1)S(1)} %shard_map.133.refs_0_), channel_id=1, source_target_pairs={{0,2},{2,0},{4,6},{6,4},{1,3},{3,1},{5,7},{7,5},{8,10},{10,8},{12,... | collective-permute-start | bytes 122888 | tf_op jit(solution)/shard_map/ppermute | solution.py:310
  36.7 1.5 %collective-permute-start.7 = (bf16[4,160,128]{2,1,0:T(8,128)(2,1)S(1)}, bf16[4,160,128]{2,1,0:T(8,128)(2,1)S(1)}, u32[]{:S(2)}, u32[]{:S(2)}) collective-permute-start(bf16[4,160,128]{2,1,0:T(8,128)(2,1)S(1)} %shard_map.134.mine_ref), channel_id=1, source_target_pairs={{0,1},{1,0},{2,3},{3,2},{4,5},{5,4},{6,7},{7,6},{8,9},{9,8},{10,11... | collective-permute-start | bytes 491528 | tf_op jit(solution)/shard_map/ppermute | solution.py:386
  39.3 5.3 %collective-permute-start.10 = (bf16[80,128]{1,0:T(8,128)(2,1)S(1)}, bf16[80,128]{1,0:T(8,128)(2,1)S(1)}, u32[]{:S(2)}, u32[]{:S(2)}) collective-permute-start(bf16[80,128]{1,0:T(8,128)(2,1)S(1)} %shard_map.135.refs_0_), channel_id=1, source_target_pairs={{0,128},{64,192},{128,0},{192,64},{1,129},{65,193},{129,1},{193,65... | collective-permute-start | bytes 61448 | tf_op jit(solution)/shard_map/ppermute | solution.py:310
  41.4 5.0 %collective-permute-start.9 = (bf16[80,128]{1,0:T(8,128)(2,1)S(1)}, bf16[80,128]{1,0:T(8,128)(2,1)S(1)}, u32[]{:S(2)}, u32[]{:S(2)}) collective-permute-start(bf16[80,128]{1,0:T(8,128)(2,1)S(1)} %shard_map.135.refs_0_), channel_id=1, source_target_pairs={{0,192},{64,128},{128,64},{192,0},{1,193},{65,129},{129,65},{193,1... | collective-permute-start | bytes 61448 | tf_op jit(solution)/shard_map/ppermute | solution.py:310
  42.3 4.1 %collective-permute-start.8 = (bf16[80,128]{1,0:T(8,128)(2,1)S(1)}, bf16[80,128]{1,0:T(8,128)(2,1)S(1)}, u32[]{:S(2)}, u32[]{:S(2)}) collective-permute-start(bf16[80,128]{1,0:T(8,128)(2,1)S(1)} %shard_map.135.refs_0_), channel_id=1, source_target_pairs={{0,64},{64,0},{128,192},{192,128},{1,65},{65,1},{129,193},{193,129... | collective-permute-start | bytes 61448 | tf_op jit(solution)/shard_map/ppermute | solution.py:310
